TPU v7x, 512 devices: a whole 4x4x16 slice. The times are simulated.
512 devices in a mesh: group: 4 (over z_lo), dp: 32 (over y, x, core), mp: 4 (over z_hi).
Axes of the slice: x: 4, y: 4, z: 16 (z_hi: 4, z_lo: 4; z = z_hi * 4 + z_lo), core: 2. Of those that a mesh axis runs over, the one named last changes fastest.
Arguments:
- dino_context: bfloat16 [256, 128, 1536], P('group', 'dp', 'mp'), may hold values from -6 to 6
- dino_stream: bfloat16 [256, 128, 1536], P('group', 'dp', 'mp'), may hold values from -6 to 6
- dino_out_proj: bfloat16 [1536, 1536], P('dp', 'mp'), may hold values from -0.15625 to 0.15625
- sam_context: bfloat16 [256, 128, 1280], P('group', 'dp', 'mp'), may hold values from -6 to 6
- sam_stream: bfloat16 [256, 128, 1280], P('group', 'dp', 'mp'), may hold values from -6 to 6
- sam_out_proj: bfloat16 [1280, 1280], P('dp', 'mp'), may hold values from -0.15625 to 0.15625
- owners: int32 [4, 64], P('group'), may hold values from 0 to 63, each once within a row
- valid_rows: int32 [256], P(('group', 'dp')), may hold values from 32 to 128, as said below
- student_stream: bfloat16 [256, 128, 1280], P(('group', 'dp'), None, 'mp'), may hold values from -6 to 6
- norm_gain: float32 [1280], P('mp'), may hold values from 0.1 to 1.9
- adapt_dino: bfloat16 [1280, 1536], P(None, 'mp'), may hold values from -0.15625 to 0.15625
- adapt_dino_bias: float32 [1536], P('mp'), may hold values from -4 to 4
- adapt_sam: bfloat16 [1280, 1280], P(None, 'mp'), may hold values from -0.15625 to 0.15625
- adapt_sam_bias: float32 [1280], P('mp'), may hold values from -4 to 4
Outputs:
- stream_grad: bfloat16 [256, 128, 1280], P(('group', 'dp'), None, 'mp')
- dino_head_grad: bfloat16 [1280, 1536], P(('group', 'dp'), 'mp')
- dino_bias_grad: float32 [1536], P('mp')
- sam_head_grad: bfloat16 [1280, 1280], P(('group', 'dp'), 'mp')
- sam_bias_grad: float32 [1280], P('mp')
- gain_grad: float32 [1280], P('mp')
Inputs may be any that keep to these rules, and one draw needn't show every extreme that they name: `valid_rows`: rows of a slot at or past its count are padding; some slot has all 128 rows and some has 32. `owners`: each row is a permutation of the slots of its slab.
All inputs are finite; a program needn't handle non-finite values.
Results may differ from a plain program's by a relative error of at most 0.017.
Values may be sent and summed in bfloat16 or wider, within the bound.
No kernel may reach another device: no remote copies, remote signals or barrier semaphores. Data moves between devices by JAX's collectives and lax.ppermute only.
A program may use at most 64 MiB of HBM per device.

v0:
```python
import jax
import jax.numpy as jnp
from jax import lax
from jax.sharding import PartitionSpec as P

eps = 1e-06
loss_weight = 1024.0


def head_grad(out, target, inner, square, tsquare, live):
    inverse = lax.rsqrt(square + eps) * lax.rsqrt(tsquare + eps)
    cosine = inner * inverse
    return -loss_weight * live * (target * inverse - cosine * out / (square + eps))


def learner(
    stream,
    dino_target,
    sam_target,
    live,
    norm_gain,
    adapt_dino,
    adapt_dino_bias,
    adapt_sam,
    adapt_sam_bias,
):
    width_local = stream.shape[1]
    feats = width_local * lax.axis_size("mp")
    values = stream.astype(jnp.float32)
    total, squares = lax.psum((jnp.sum(values, axis=1), jnp.sum(values * values, axis=1)), "mp")
    center = (total / feats)[:, None]
    spread = (squares / feats)[:, None] - center * center
    scale = lax.rsqrt(spread + eps)
    standard = (values - center) * scale
    local_normed = (standard * norm_gain[None, :]).astype(jnp.bfloat16)
    normed = lax.all_gather(local_normed, "mp", axis=1, tiled=True)
    dino_out = (
        jnp.dot(normed, adapt_dino, preferred_element_type=jnp.float32) + adapt_dino_bias[None, :]
    )
    sam_out = (
        jnp.dot(normed, adapt_sam, preferred_element_type=jnp.float32) + adapt_sam_bias[None, :]
    )
    stats = lax.psum(
        (
            jnp.sum(dino_out * dino_target, axis=1),
            jnp.sum(dino_out * dino_out, axis=1),
            jnp.sum(dino_target * dino_target, axis=1),
            jnp.sum(sam_out * sam_target, axis=1),
            jnp.sum(sam_out * sam_out, axis=1),
            jnp.sum(sam_target * sam_target, axis=1),
        ),
        "mp",
    )
    stats = [entry[:, None] for entry in stats]
    dino_grad = head_grad(dino_out, dino_target, stats[0], stats[1], stats[2], live)
    sam_grad = head_grad(sam_out, sam_target, stats[3], stats[4], stats[5], live)
    dino_back = dino_grad.astype(jnp.bfloat16)
    sam_back = sam_grad.astype(jnp.bfloat16)
    contract_last = (((1,), (1,)), ((), ()))
    first = lax.dot_general(
        adapt_dino, dino_back, contract_last, preferred_element_type=jnp.float32
    )
    normed_grad = (
        lax.psum_scatter(
            (
                first
                + lax.dot_general(
                    adapt_sam, sam_back, contract_last, preferred_element_type=jnp.float32
                )
            ).astype(jnp.bfloat16),
            "mp",
            scatter_dimension=0,
            tiled=True,
        )
        .astype(jnp.float32)
        .T
    )
    scaled = normed_grad * norm_gain[None, :]
    first_sum, second_sum = lax.psum(
        (jnp.sum(scaled, axis=1), jnp.sum(scaled * standard, axis=1)), "mp"
    )
    stream_grad = (
        (scaled - (first_sum / feats)[:, None] - standard * (second_sum / feats)[:, None]) * scale
    ).astype(jnp.bfloat16)
    contract_rows = (((0,), (0,)), ((), ()))
    dino_weight = lax.dot_general(
        normed, dino_back, contract_rows, preferred_element_type=jnp.float32
    )
    sam_weight = lax.dot_general(
        normed, sam_back, contract_rows, preferred_element_type=jnp.float32
    )
    sums = (
        dino_weight,
        sam_weight,
        jnp.sum(dino_grad, axis=0),
        jnp.sum(sam_grad, axis=0),
        jnp.sum(normed_grad * standard, axis=0),
        jnp.sum(live),
    )
    return (stream_grad, sums)


def local(
    dino_context,
    dino_stream,
    dino_out_proj,
    sam_context,
    sam_stream,
    sam_out_proj,
    owners,
    valid_rows,
    student_stream,
    norm_gain,
    adapt_dino,
    adapt_dino_bias,
    adapt_sam,
    adapt_sam_bias,
):
    slots, per_peer, dino_local = dino_context.shape
    sam_local = sam_context.shape[2]
    rows = slots * per_peer
    dino_flat = dino_context.reshape(rows, dino_local)
    sam_flat = sam_context.reshape(rows, sam_local)
    dino_full, sam_full = (
        lax.all_gather(dino_flat, "mp", axis=1, tiled=True),
        lax.all_gather(sam_flat, "mp", axis=1, tiled=True),
    )
    columns = dino_full
    dino_mixed = jnp.dot(
        columns,
        lax.all_gather(dino_out_proj, "dp", axis=0, tiled=True),
        preferred_element_type=jnp.float32,
    )
    columns = sam_full
    sam_mixed = jnp.dot(
        columns,
        lax.all_gather(sam_out_proj, "dp", axis=0, tiled=True),
        preferred_element_type=jnp.float32,
    )
    dino_feat = (dino_stream.reshape(rows, dino_local).astype(jnp.float32) + dino_mixed).astype(
        jnp.bfloat16
    )
    sam_feat = (sam_stream.reshape(rows, sam_local).astype(jnp.float32) + sam_mixed).astype(
        jnp.bfloat16
    )
    picker = (owners[0][None, :] == jnp.arange(slots, dtype=jnp.int32)[:, None]).astype(
        jnp.bfloat16
    )
    dino_sent = jnp.einsum(
        "oi,ird->ord",
        picker,
        dino_feat.reshape(slots, per_peer, dino_local),
        preferred_element_type=jnp.float32,
    ).astype(jnp.bfloat16)
    sam_sent = jnp.einsum(
        "oi,ird->ord",
        picker,
        sam_feat.reshape(slots, per_peer, sam_local),
        preferred_element_type=jnp.float32,
    ).astype(jnp.bfloat16)
    own_slots, window, width_local = student_stream.shape
    dino_here, sam_here = (
        lax.all_to_all(dino_sent, "dp", split_axis=0, concat_axis=1, tiled=True),
        lax.all_to_all(sam_sent, "dp", split_axis=0, concat_axis=1, tiled=True),
    )
    student_rows = own_slots * window
    live = (
        (jnp.arange(window, dtype=jnp.int32)[None, :] < valid_rows[:, None])
        .astype(jnp.float32)
        .reshape(student_rows, 1)
    )
    stream_grad, sums = learner(
        student_stream.reshape(student_rows, width_local),
        dino_here.reshape(student_rows, dino_local).astype(jnp.float32),
        sam_here.reshape(student_rows, sam_local).astype(jnp.float32),
        live,
        norm_gain,
        adapt_dino,
        adapt_dino_bias,
        adapt_sam,
        adapt_sam_bias,
    )
    stream_out = stream_grad.reshape(own_slots, window, width_local)
    dino_weight, sam_weight, dino_bias, sam_bias, gain_sum, count = sums
    dino_share, sam_share = (
        lax.psum_scatter(dino_weight, ("group", "dp"), scatter_dimension=0, tiled=True),
        lax.psum_scatter(sam_weight, ("group", "dp"), scatter_dimension=0, tiled=True),
    )
    dino_bias, sam_bias, gain_sum, count = lax.psum(
        (dino_bias, sam_bias, gain_sum, count), ("group", "dp")
    )
    factor = lax.rsqrt(count)
    return (
        stream_out,
        (factor * dino_share).astype(jnp.bfloat16),
        factor * dino_bias,
        (factor * sam_share).astype(jnp.bfloat16),
        factor * sam_bias,
        factor * gain_sum,
    )


def solution(mesh):
    placed = (
        P("group", "dp", "mp"),
        P("group", "dp", "mp"),
        P("dp", "mp"),
        P("group", "dp", "mp"),
        P("group", "dp", "mp"),
        P("dp", "mp"),
        P("group", None),
        P(("group", "dp")),
        P(("group", "dp"), None, "mp"),
        P("mp"),
        P(None, "mp"),
        P("mp"),
        P(None, "mp"),
        P("mp"),
    )
    return jax.shard_map(
        local,
        mesh=mesh,
        in_specs=placed,
        out_specs=(
            P(("group", "dp"), None, "mp"),
            P(("group", "dp"), "mp"),
            P("mp"),
            P(("group", "dp"), "mp"),
            P("mp"),
            P("mp"),
        ),
        check_vma=False,
    )
```

profile of v0, /device:TPU:1, one launch (start us, length us, event | category | flops | bytes accessed | tf_op | source)
XLA Modules:
  0.0 1571.1 jit_solution(4566420139637799475)
XLA Ops:
  7.2 0.0 copy-start
  7.2 0.0 all-gather.2.cloned.1.call-start
  7.2 0.7 all-gather.2.cloned.1.call-update
  7.9 1.0 reshape.124
  8.9 0.1 copy.77
  9.1 0.1 reshape.118
  9.2 0.1 copy.76
  9.3 35.1 %all_gather.18 = bf16[256,1280]{0,1:T(8,128)(2,1)S(1)} all-gather(bf16[256,320]{0,1:T(8,128)(2,1)S(1)} %copy.76), channel_id=1, replica_groups=mesh['group'=4,'dp'=32,'mp'=4] {'mp'}, dimensions={1}, use_global_device_ids=true | all-gather | bytes 819200 | tf_op jit(solution)/shard_map/all_gather | solution.py:126
  44.5 29.9 %all_gather.19 = bf16[1280,320]{1,0:T(8,128)(2,1)S(1)} all-gather(bf16[40,320]{1,0:T(8,128)(2,1)S(1)} %copy-done.7), channel_id=1, replica_groups=mesh['group'=4,'dp'=32,'mp'=4] {'dp'}, dimensions={0}, use_global_device_ids=true | all-gather | bytes 844800 | tf_op jit(solution)/shard_map/all_gather | solution.py:137
  74.3 0.5 fusion.3
  74.9 0.2 copy.78
  75.1 0.1 reshape.119
  75.1 0.2 convolution_convert_fusion
  75.3 0.8 copy.80
  76.2 5.1 all-to-all-start.1
  81.3 0.1 reshape.116
  81.3 0.1 convert_reduce_fusion
  81.4 10.9 all-reduce.6
  92.3 0.1 multiply_convert_fusion
  92.4 32.3 %all_gather.15 = bf16[256,1536]{1,0:T(8,128)(2,1)S(1)} all-gather(bf16[256,384]{1,0:T(8,128)(2,1)S(1)} %reshape.116), channel_id=1, replica_groups=mesh['group'=4,'dp'=32,'mp'=4] {'mp'}, dimensions={1}, use_global_device_ids=true | all-gather | bytes 983040 | tf_op jit(solution)/shard_map/all_gather | solution.py:125
  124.7 25.4 %all_gather.17 = bf16[256,1280]{0,1:T(8,128)(2,1)S(1)} all-gather(bf16[256,320]{0,1:T(8,128)(2,1)S(1)} %multiply_convert_fusion), channel_id=1, replica_groups=mesh['group'=4,'dp'=32,'mp'=4] {'mp'}, dimensions={1}, use_global_device_ids=true | all-gather | bytes 819200 | tf_op jit(solution)/shard_map/all_gather | solution.py:36
  150.1 1.0 reshape.121
  151.1 0.7 convert_reduce_fusion.1
  151.7 0.8 copy_bitcast_fusion
  152.5 1.9 reshape.125
  154.4 1.1 copy.85
  155.6 0.2 multiply_reduce_fusion
  155.8 0.7 reduce_sum.156
  156.4 1.8 fusion.2
  158.3 0.1 reshape.117
  158.4 0.9 convolution_convert_fusion.1
  159.3 0.8 copy.70
  160.1 16.3 %all-to-all-start = ((bf16[64,4,384]{2,1,0:T(4,128)(2,1)}), bf16[64,4,384]{2,1,0:T(4,128)(2,1)S(1)}, u32[]{:S(2)}, u32[]{:S(2)}) async-start(bf16[64,4,384]{2,1,0:T(4,128)(2,1)} %copy.70), calls=%async_computation | async-start | bytes 393216 | tf_op jit(solution)/shard_map/all_to_all | solution.py:163
  176.4 0.0 reduce-scatter.4.cloned.1.call-start
  176.5 1.7 multiply_reduce_fusion.4
  178.1 6.5 all-to-all-done
  184.7 0.9 reshape.122
  185.6 0.2 multiply_reduce_fusion.2
  185.8 0.1 reduce_sum.150
  185.9 2.3 multiply_reduce_fusion.1
  188.2 10.0 all-reduce.5
  198.2 1.8 fusion.32
  200.0 0.5 fusion.19
  200.6 0.4 copy-done.4
  201.0 0.2 fusion.31
  201.2 1.4 fusion.1
  202.5 2.2 copy.89
  204.8 0.0 reduce-scatter.4.cloned.1.call-update
  204.8 0.0 all-reduce.9.cloned.1.call-start
  204.8 1.8 fusion.21
  206.6 1.8 fusion.17
  208.4 0.0 all-reduce.9.cloned.1.call-update
  208.5 1.3 dynamic-slice
  210.4 40.4 %reduce-scatter.4.cloned.1.call-done = bf16[320,256]{1,0:T(8,128)(2,1)} async-done(((bf16[1280,256]{1,0:T(8,128)(2,1)}), bf16[320,256]{1,0:T(8,128)(2,1)}) %reduce-scatter.4.cloned.1.call-update) | async-done | bytes 163856 | tf_op jit(solution)/shard_map/reduce_scatter | solution.py:64
  250.8 1.1 fusion.13
  251.9 337.6 %all-reduce.2 = (f32[]{:T(128)}, f32[384]{0:T(512)S(1)}, f32[320]{0:T(512)S(1)}, f32[320]{0:T(512)S(1)}) all-reduce(f32[]{:T(128)} %get-tuple-element.73, f32[384]{0:T(512)S(1)} %copy-done.9, f32[320]{0:T(512)S(1)} %get-tuple-element.61, f32[320]{0:T(512)S(1)} %get-tuple-element.36), channel_id=1, replica_groups=mesh['group'=4,'dp'=32,'mp'=4] {'group','dp'}, use_global_device_ids=true, to_apply=%region_22.0 | all-reduce | flops 1025 | bytes 8200 | tf_op jit(solution)/shard_map/psum | solution.py:189
  590.2 12.0 all-reduce.4
  602.2 0.6 broadcast_multiply_fusion.2
  602.7 0.6 broadcast_multiply_fusion.1
  603.3 0.6 broadcast_multiply_fusion
  603.9 1.7 copy_bitcast_fusion.2
  605.6 956.2 %all-reduce.9.cloned.1.call-done = (f32[1280,384]{1,0:T(8,128)}, f32[1280,320]{1,0:T(8,128)}) async-done(((f32[1280,384]{1,0:T(8,128)}, f32[1280,320]{1,0:T(8,128)}), (f32[1280,384]{1,0:T(8,128)}, f32[1280,320]{1,0:T(8,128)})) %all-reduce.9.cloned.1.call-update) | async-done | bytes 3604496
  1561.8 1.4 fusion.28
  1563.2 1.4 fusion.27
  (39 shorter events, 0.2 us)
Async XLA Ops:
  7.2 178.8 %copy-start = (bf16[1280,384]{1,0:T(8,128)(2,1)S(1)}, bf16[1280,384]{1,0:T(8,128)(2,1)}, u32[]{:S(2)}) copy-start(bf16[1280,384]{1,0:T(8,128)(2,1)} %param.24) | copy-start | bytes 2949124
  7.2 1.9 copy-start.5
  7.2 149.2 %all-gather.2.cloned.1.call-start = ((), (), s32[]{:S(2)}) async-start(), calls=%async_computation.3 | async-start | bytes 1216512 | tf_op jit(solution)/shard_map/all_gather | solution.py:131
  7.9 36.5 %copy-start.7 = (bf16[40,320]{1,0:T(8,128)(2,1)S(1)}, bf16[40,320]{1,0:T(8,128)(2,1)}, u32[]{:S(2)}) copy-start(bf16[40,320]{1,0:T(8,128)(2,1)} %param.19) | copy-start | bytes 76804
  74.3 0.8 copy-start.13
  74.9 6.4 copy-start.6
  74.9 6.4 copy-start.2
  74.9 17.4 %copy-start.8 = (f32[320]{0:T(512)S(1)}, f32[320]{0:T(512)}, u32[]{:S(2)}) copy-start(f32[320]{0:T(512)} %param.23) | copy-start | bytes 3844
  76.2 75.6 %all-to-all-start.1 = ((bf16[64,4,320]{2,1,0:T(4,128)(2,1)}), bf16[64,4,320]{2,1,0:T(4,128)(2,1)S(1)}, u32[]{:S(2)}, u32[]{:S(2)}) async-start(bf16[64,4,320]{2,1,0:T(4,128)(2,1)} %copy.80), calls=%async_computation.1 | async-start | bytes 393216 | tf_op jit(solution)/shard_map/all_to_all | solution.py:164
  92.3 58.8 %copy-start.15 = (s32[2]{0:T(128)S(1)}, s32[2]{0:T(128)}, u32[]{:S(2)}) copy-start(s32[2]{0:T(128)} %param.21) | copy-start | bytes 28
  158.3 18.2 %copy-start.1 = (bf16[1280,320]{0,1:T(8,128)(2,1)S(1)}, bf16[1280,320]{0,1:T(8,128)(2,1)}, u32[]{:S(2)}) copy-start(bf16[1280,320]{0,1:T(8,128)(2,1)} %param.26) | copy-start | bytes 2457604
  158.3 18.2 %copy-start.14 = (f32[320]{0:T(512)S(1)}, f32[320]{0:T(512)}, u32[]{:S(2)}) copy-start(f32[320]{0:T(512)} %param.27) | copy-start | bytes 3844
  160.1 24.6 %all-to-all-start = ((bf16[64,4,384]{2,1,0:T(4,128)(2,1)}), bf16[64,4,384]{2,1,0:T(4,128)(2,1)S(1)}, u32[]{:S(2)}, u32[]{:S(2)}) async-start(bf16[64,4,384]{2,1,0:T(4,128)(2,1)} %copy.70), calls=%async_computation | async-start | bytes 393216 | tf_op jit(solution)/shard_map/all_to_all | solution.py:163
  176.4 74.4 %reduce-scatter.4.cloned.1.call-start = ((), (), s32[]{:S(2)}) async-start(), calls=%async_computation.4 | async-start | bytes 819200 | tf_op jit(solution)/shard_map/reduce_scatter | solution.py:64
  185.8 2.5 copy-start.10
  185.8 2.5 copy-start.11
  185.8 2.5 copy-start.12
  185.8 12.4 copy-start.3
  200.0 1.0 copy-start.4
  204.8 1357.0 %all-reduce.9.cloned.1.call-start = ((), (), s32[]{:S(2)}) async-start(), calls=%async_computation.5 | async-start | bytes 7864320
  208.4 43.5 %copy-start.9 = (f32[384]{0:T(512)S(1)}, f32[384]{0:T(512)}, u32[]{:S(2)}) copy-start(f32[384]{0:T(512)} %get-tuple-element.63) | copy-start | bytes 4612
Sparse Core Ops, SparseCore 0:
  11.2 64.5 all-gather.1
  204.9 45.8 reduce-scatter.3
  253.8 1307.9 all-reduce.8
where the time goes:
time: 1570 us
  waiting for transfers between devices  1000 us (64%)
  blocking collectives  493 us (31%)
  starting transfers between devices  21.5 us (1%)
    unnamed x4, waiting for transfers between devices  957 us
    psum x1, blocking collectives, local(): lax.psum((dino_bias, sam_bias, gain_sum, count), ('group', 'dp'))  338 us
    reduce_scatter x1, waiting for transfers between devices, learner(): lax.psum_scatter((first + lax.dot_general(adapt_sam, sam_back, contract_l...  40.4 us
    all_gather x1, blocking collectives, local(): lax.all_gather(sam_flat, 'mp', axis=1, tiled=True)  35.1 us
    all_gather x1, blocking collectives, local(): lax.all_gather(dino_flat, 'mp', axis=1, tiled=True)  32.3 us
  transfers between devices with their start and end apart: 5, of which 3 were waited for; matrix products, arithmetic and copies ran while one was open for 1% of the time, Pallas kernels for 0%

commit v1 on v0

v1 whole, which is shorter than its diff:
```python
import jax
import jax.numpy as jnp
from jax import lax
from jax.sharding import Mesh
from jax.sharding import PartitionSpec as P

eps = 1e-06
loss_weight = 1024.0
f32 = jnp.float32
bf16 = jnp.bfloat16

EXTENT = {"g": 4, "y": 4, "x": 4, "c": 2, "m": 4}
DP = ("y", "x", "c")


def shift(array, axis, by):
    extent = EXTENT[axis]
    return lax.ppermute(array, axis, [(i, (i + by) % extent) for i in range(extent)])


def dot(a, b):
    return jnp.dot(a, b, preferred_element_type=f32)


def dot_last(a, b):
    return lax.dot_general(a, b, (((1,), (1,)), ((), ())), preferred_element_type=f32)


def dot_rows(a, b):
    return lax.dot_general(a, b, (((0,), (0,)), ((), ())), preferred_element_type=f32)


def ring_m(block):
    before = shift(block, "m", 1)
    after = shift(block, "m", -1)
    half = block.shape[0] // 2
    far = jnp.concatenate([shift(before[:half], "m", 1), shift(after[half:], "m", -1)], axis=0)
    return [block, after, far, before]


def gather_axis(block, axis):
    extent = EXTENT[axis]
    here = lax.axis_index(axis)
    whole = jnp.zeros((extent,) + block.shape, block.dtype)
    whole = lax.dynamic_update_index_in_dim(whole, block, here, 0)
    for by in range(1, extent):
        whole = lax.dynamic_update_index_in_dim(
            whole, shift(block, axis, by), (here - by) % extent, 0
        )
    return whole


def sum_axis(array, axis):
    total = array
    for by in range(1, EXTENT[axis]):
        total = total + shift(array, axis, by)
    return total


def one_hot(picked, width):
    return (lax.broadcasted_iota(jnp.int32, (picked.shape[0], width), 1) == picked[:, None]).astype(
        bf16
    )


def head_grad(out, target, inner, square, tsquare, live):
    inverse = lax.rsqrt(square + eps) * lax.rsqrt(tsquare + eps)
    cosine = inner * inverse
    return -loss_weight * live * (target * inverse - cosine * out / (square + eps))


def local(
    dino_context,
    dino_stream,
    dino_out_proj,
    sam_context,
    sam_stream,
    sam_out_proj,
    owners,
    valid_rows,
    student_stream,
    norm_gain,
    adapt_dino,
    adapt_dino_bias,
    adapt_sam,
    adapt_sam_bias,
):
    m = lax.axis_index("m")
    c = lax.axis_index("c")
    slots, per_peer, wd = dino_context.shape
    ws = sam_context.shape[2]
    rows = slots * per_peer
    own_slots, window, wf = student_stream.shape
    feats = wf * EXTENT["m"]
    peers = slots // own_slots

    student = ring_m(student_stream.reshape(rows, wf))
    dino_blocks = ring_m(dino_context.reshape(rows, wd))
    sam_blocks = ring_m(sam_context.reshape(rows, ws))
    gains = [norm_gain] + [shift(norm_gain, "m", -by) for by in range(1, EXTENT["m"])]

    kd, ks = dino_out_proj.shape[0], sam_out_proj.shape[0]
    packed = jnp.concatenate(
        [dino_out_proj, jnp.pad(sam_out_proj, ((0, 0), (0, wd - ws)))], axis=0
    )
    plane = gather_axis(gather_axis(packed, "x"), "y")
    other = shift(plane, "c", 1)
    proj = jnp.stack(
        [jnp.where(c == 0, plane, other), jnp.where(c == 0, other, plane)], axis=2
    )
    dino_proj = proj[:, :, :, :kd, :].reshape(EXTENT["m"], -1, wd)
    sam_proj = proj[:, :, :, kd:, :ws].reshape(EXTENT["m"], -1, ws)

    dino_mixed = sum(
        dot(dino_blocks[by], lax.dynamic_index_in_dim(dino_proj, (m + by) % 4, 0, False))
        for by in range(4)
    )
    sam_mixed = sum(
        dot(sam_blocks[by], lax.dynamic_index_in_dim(sam_proj, (m + by) % 4, 0, False))
        for by in range(4)
    )
    dino_feat = (dino_stream.reshape(rows, wd).astype(f32) + dino_mixed).astype(bf16)
    sam_feat = (sam_stream.reshape(rows, ws).astype(f32) + sam_mixed).astype(bf16)
    feat = jnp.concatenate([dino_feat, sam_feat], axis=1)
    order = jnp.argsort(owners[0]).astype(jnp.int32)
    wanted = (order[:, None] * per_peer + jnp.arange(per_peer, dtype=jnp.int32)[None, :]).reshape(-1)
    sent = dot(one_hot(wanted, rows), feat).astype(bf16)
    arrived = lax.all_to_all(sent, DP, split_axis=0, concat_axis=0, tiled=True)
    place = jnp.arange(rows, dtype=jnp.int32)
    slot, row = place // window, place % window
    source = (row // per_peer) * (own_slots * per_peer) + slot * per_peer + row % per_peer
    target = dot(one_hot(source, rows), arrived)
    dino_target, sam_target = target[:, :wd], target[:, wd:]

    live = (
        (jnp.arange(window, dtype=jnp.int32)[None, :] < valid_rows[:, None])
        .astype(f32)
        .reshape(rows, 1)
    )
    values = [block.astype(f32) for block in student]
    total = sum(jnp.sum(block, axis=1, keepdims=True) for block in values)
    squares = sum(jnp.sum(block * block, axis=1, keepdims=True) for block in values)
    center = total / feats
    spread = squares / feats - center * center
    scale = lax.rsqrt(spread + eps)
    values = jnp.concatenate(values, axis=1)
    gain = jnp.concatenate(gains)[None, :]
    standard = (values - center) * scale
    normed = (standard * gain).astype(bf16)
    adapt = jnp.roll(
        jnp.concatenate([adapt_dino, adapt_sam], axis=1).reshape(EXTENT["m"], wf, wd + ws), -m, axis=0
    ).reshape(feats, wd + ws)
    out = dot(normed, adapt) + jnp.concatenate([adapt_dino_bias, adapt_sam_bias])[None, :]
    dino_out, sam_out = out[:, :wd], out[:, wd:]
    spot = jnp.arange(feats, dtype=jnp.int32)
    each = feats // (EXTENT["g"] * peers)
    i, rest = spot % each, spot // each
    g_of, rest = rest % 4, rest // 4
    x_of, rest = rest % 4, rest // 4
    y_of, c_of = rest % 4, rest // 4
    feature = (((g_of * 4 + y_of) * 4 + x_of) * 2 + c_of) * each + i
    where_now = ((feature // wf - m) % 4) * wf + feature % wf
    dealt = dot_last(normed, one_hot(where_now, feats)).astype(bf16)

    stats = lax.psum(
        jnp.stack(
            [
                jnp.sum(dino_out * dino_target, axis=1),
                jnp.sum(dino_out * dino_out, axis=1),
                jnp.sum(dino_target * dino_target, axis=1),
                jnp.sum(sam_out * sam_target, axis=1),
                jnp.sum(sam_out * sam_out, axis=1),
                jnp.sum(sam_target * sam_target, axis=1),
            ]
        ),
        "m",
    )[:, :, None]
    dino_grad = head_grad(dino_out, dino_target, stats[0], stats[1], stats[2], live)
    sam_grad = head_grad(sam_out, sam_target, stats[3], stats[4], stats[5], live)
    grad = jnp.concatenate([dino_grad, sam_grad], axis=1)
    back = grad.astype(bf16)

    weight = dot_rows(dealt, back)
    half = feats // 2
    mine = lax.dynamic_slice_in_dim(weight, c * half, half, 0)
    theirs = lax.dynamic_slice_in_dim(weight, (1 - c) * half, half, 0).astype(bf16)
    chip = (mine + shift(theirs, "c", 1).astype(f32)).astype(bf16)
    dealt_xy = lax.all_to_all(chip, ("y", "x"), split_axis=0, concat_axis=0, tiled=True)
    slab = jnp.sum(dealt_xy.reshape(16, -1, wd + ws).astype(f32), axis=0).astype(bf16)
    share = sum(
        piece.astype(f32)
        for piece in [lax.dynamic_slice_in_dim(slab, lax.axis_index("g") * each, each, 0)]
        + [
            shift(
                lax.dynamic_slice_in_dim(slab, ((lax.axis_index("g") + by) % 4) * each, each, 0),
                "g",
                by,
            )
            for by in range(1, 4)
        ]
    )

    partial = dot_last(back, adapt)
    scaled_part = partial * gain
    first_part = jnp.sum(scaled_part, axis=1)
    second_part = jnp.sum(scaled_part * standard, axis=1)
    gain_part = jnp.sum(partial * standard, axis=0)
    partial_low = partial.astype(bf16)
    normed_grad = partial[:, :wf]
    small = jnp.concatenate([first_part, second_part, gain_part[:wf]])
    for by in range(1, EXTENT["m"]):
        block = slice(by * wf, (by + 1) * wf)
        normed_grad = normed_grad + shift(partial_low[:, block], "m", by).astype(f32)
        small = small + shift(
            jnp.concatenate([first_part, second_part, gain_part[block]]), "m", by
        )
    first_sum = small[:rows, None] / feats
    second_sum = small[rows : 2 * rows, None] / feats
    own_standard = standard[:, :wf]
    scaled = normed_grad * norm_gain[None, :]
    stream_grad = ((scaled - first_sum - own_standard * second_sum) * scale).astype(bf16)

    vector = jnp.concatenate([jnp.sum(grad, axis=0), small[2 * rows :], jnp.sum(live).reshape(1)])
    for axis in ("c", "x", "y", "g"):
        vector = sum_axis(vector, axis)
    factor = lax.rsqrt(vector[-1])
    vector = factor * vector[:-1]
    share = (factor * share).astype(bf16)
    return (
        stream_grad.reshape(own_slots, window, wf),
        share[:, :wd],
        vector[:wd],
        share[:, wd:],
        vector[wd : wd + ws],
        vector[wd + ws :],
    )


def solution(mesh):
    parts = Mesh(
        mesh.devices.reshape(tuple(EXTENT[axis] for axis in ("g", "y", "x", "c", "m"))),
        ("g", "y", "x", "c", "m"),
    )
    every = ("g",) + DP
    placed = (
        P("g", DP, "m"),
        P("g", DP, "m"),
        P(DP, "m"),
        P("g", DP, "m"),
        P("g", DP, "m"),
        P(DP, "m"),
        P("g", None),
        P(every),
        P(every, None, "m"),
        P("m"),
        P(None, "m"),
        P("m"),
        P(None, "m"),
        P("m"),
    )
    return jax.shard_map(
        local,
        mesh=parts,
        in_specs=placed,
        out_specs=(
            P(every, None, "m"),
            P(every, "m"),
            P("m"),
            P(every, "m"),
            P("m"),
            P("m"),
        ),
        check_vma=False,
    )
```

time: 1570 us -> 334 us (0.21)
  waiting for transfers between devices: 1000 us -> 41.1 us
  blocking collectives: 493 us -> 10.8 us
  starting transfers between devices: 21.5 us -> 207 us
    unnamed x4 -> x0, waiting for transfers between devices: 957 us -> none
    psum x4 -> x1, blocking collectives: 370 us -> 10.8 us  [local(): lax.psum(jnp.stack([jnp.sum(dino_out * dino_target, axis=1), jnp.sum(dino...]
    ppermute x0 -> x42, starting transfers between devices: none -> 184 us  [shift(): lax.ppermute(array, axis, [(i, (i + by) % extent) for i in range(extent)])]
    all_gather x4 -> x0, blocking collectives: 123 us -> none  [the longest x1 35.1 us: local(): lax.all_gather(sam_flat, 'mp', axis=1, tiled=True)]
    reduce_scatter x1 -> x0, waiting for transfers between devices: 40.4 us -> none  [learner(): lax.psum_scatter((first + lax.dot_general(adapt_sam, sam_back, contract_l...]
    ppermute x0 -> x42, waiting for transfers between devices: none -> 26.2 us  [shift(): lax.ppermute(array, axis, [(i, (i + by) % extent) for i in range(extent)])]
  transfers between devices with their start and end apart: 5 -> 44, of which waited for: 3 -> 12; matrix products, arithmetic and copies ran while one was open for 1% -> 17% of each run, Pallas kernels for 0% -> 0%
where the time goes in v1:
time: 334 us; the launch traced here: 327 us
  starting transfers between devices  207 us (62%)
  waiting for transfers between devices  41.1 us (12%)
  local copies, waits for them, and re-layouts  25 us (7%)
  other arithmetic  22.5 us (7%)
  matrix products  17.7 us (5%)
  blocking collectives  10.8 us (3%)
    ppermute x42, starting transfers between devices, shift(): lax.ppermute(array, axis, [(i, (i + by) % extent) for i in range(extent)])  184 us
    ppermute x42, waiting for transfers between devices, shift(): lax.ppermute(array, axis, [(i, (i + by) % extent) for i in range(extent)])  26.2 us
    all_to_all x1, starting transfers between devices, local(): arrived = lax.all_to_all(sent, DP, split_axis=0, concat_axis=0, tiled=True)  17.9 us
    dot_general x11, matrix products, dot(): return jnp.dot(a, b, preferred_element_type=f32)  10.9 us
    psum x1, blocking collectives, local(): lax.psum(jnp.stack([jnp.sum(dino_out * dino_target, axis=1), jnp.sum(dino...  10.8 us
    all_to_all x1, waiting for transfers between devices, local(): lax.all_to_all(chip, ('y', 'x'), split_axis=0, concat_axis=0, tiled=True)  7.96 us
    all_to_all x1, waiting for transfers between devices, local(): arrived = lax.all_to_all(sent, DP, split_axis=0, concat_axis=0, tiled=True)  6.95 us
  transfers between devices with their start and end apart: 44, of which 12 were waited for; matrix products, arithmetic and copies ran while one was open for 17% of the time, Pallas kernels for 0%

profile of v1, /device:TPU:1, one launch (start us, length us, event | category | flops | bytes accessed | tf_op | source)
XLA Modules:
  0.0 327.2 jit_solution(671209400524459063)
XLA Ops:
  0.7 13.4 %collective-permute-start.19 = (f32[320]{0:T(512)}, f32[320]{0:T(512)S(1)}, u32[]{:S(2)}, u32[]{:S(2)}) collective-permute-start(f32[320]{0:T(512)} %param.23), channel_id=1, source_target_pairs={{0,3},{1,0},{2,1},{3,2},{4,7},{5,4},{6,5},{7,6},{8,11},{9,8},{10,9... | collective-permute-start | bytes 3848 | tf_op jit(solution)/shard_map/ppermute | solution.py:18
  14.1 4.9 %collective-permute-start.20 = (f32[320]{0:T(512)}, f32[320]{0:T(512)S(1)}, u32[]{:S(2)}, u32[]{:S(2)}) collective-permute-start(f32[320]{0:T(512)} %param.23), channel_id=1, source_target_pairs={{0,2},{1,3},{2,0},{3,1},{4,6},{5,7},{6,4},{7,5},{8,10},{9,11},{10,... | collective-permute-start | bytes 3848 | tf_op jit(solution)/shard_map/ppermute | solution.py:18
  19.0 7.3 %collective-permute-start.21 = (f32[320]{0:T(512)}, f32[320]{0:T(512)S(1)}, u32[]{:S(2)}, u32[]{:S(2)}) collective-permute-start(f32[320]{0:T(512)} %param.23), channel_id=1, source_target_pairs={{0,1},{1,2},{2,3},{3,0},{4,5},{5,6},{6,7},{7,4},{8,9},{9,10},{10,1... | collective-permute-start | bytes 3848 | tf_op jit(solution)/shard_map/ppermute | solution.py:18
  27.1 3.1 collective-permute-start
  30.3 4.4 %collective-permute-start.1 = (bf16[88,384]{1,0:T(8,128)(2,1)S(1)}, bf16[88,384]{1,0:T(8,128)(2,1)S(1)}, u32[]{:S(2)}, u32[]{:S(2)}) collective-permute-start(bf16[88,384]{1,0:T(8,128)(2,1)S(1)} %fusion.56), channel_id=1, source_target_pairs={{0,16},{8,24},{16,0},{24,8},{1,17},{9,25},{17,1},{25,9},{2,18},{10... | collective-permute-start | bytes 202760 | tf_op jit(solution)/shard_map/ppermute | solution.py:18
  34.6 1.7 copy.43
  37.4 1.7 bitcast_convert_fusion
  39.1 2.0 sort.17
  42.1 3.1 collective-permute-start.2
  45.2 1.9 collective-permute-done.2
  47.2 3.2 collective-permute-start.3
  51.2 4.5 %collective-permute-start.4 = (bf16[4,88,384]{2,1,0:T(8,128)(2,1)S(1)}, bf16[4,88,384]{2,1,0:T(8,128)(2,1)S(1)}, u32[]{:S(2)}, u32[]{:S(2)}) collective-permute-start(bf16[4,88,384]{2,1,0:T(8,128)(2,1)S(1)} %bitcast_dynamic-update-slice_fusion.4), channel_id=1, source_target_pairs={{0,64},{32,96},{64,0},{96,32},{1,65},{33,97},{65,1},{97,33},{2,66}... | collective-permute-start | bytes 811016 | tf_op jit(solution)/shard_map/ppermute | solution.py:18
  55.9 3.2 collective-permute-start.5
  59.2 3.0 collective-permute-done.4
  62.2 2.1 collective-permute-start.15
  64.4 1.6 collective-permute-done.5
  66.0 7.2 %collective-permute-start.6 = (bf16[4,4,88,384]{3,2,1,0:T(8,128)(2,1)S(1)}, bf16[4,4,88,384]{3,2,1,0:T(8,128)(2,1)}, u32[]{:S(2)}, u32[]{:S(2)}) collective-permute-start(bf16[4,4,88,384]{3,2,1,0:T(8,128)(2,1)S(1)} %bitcast_dynamic-update-slice_fusion), channel_id=1, source_target_pairs={{0,4},{4,0},{1,5},{5,1},{2,6},{6,2},{3,7},{7,3},{8,12},{12,8},{9,1... | collective-permute-start | bytes 3244040 | tf_op jit(solution)/shard_map/ppermute | solution.py:18
  75.6 4.8 %collective-permute-start.16 = (bf16[256,320]{1,0:T(8,128)(2,1)}, bf16[256,320]{1,0:T(8,128)(2,1)}, u32[]{:S(2)}, u32[]{:S(2)}) collective-permute-start(bf16[256,320]{1,0:T(8,128)(2,1)} %bitcast.29), channel_id=1, source_target_pairs={{0,1},{1,2},{2,3},{3,0},{4,5},{5,6},{6,7},{7,4},{8,9},{9,10},{10,1... | collective-permute-start | bytes 491528 | tf_op jit(solution)/shard_map/ppermute | solution.py:18
  80.3 4.4 %collective-permute-start.11 = (bf16[256,320]{1,0:T(8,128)(2,1)}, bf16[256,320]{1,0:T(8,128)(2,1)}, u32[]{:S(2)}, u32[]{:S(2)}) collective-permute-start(bf16[256,320]{1,0:T(8,128)(2,1)} %reshape.438), channel_id=1, source_target_pairs={{0,3},{1,0},{2,1},{3,2},{4,7},{5,4},{6,5},{7,6},{8,11},{9,8},{10,9... | collective-permute-start | bytes 491528 | tf_op jit(solution)/shard_map/ppermute | solution.py:18
  84.8 4.8 %collective-permute-start.12 = (bf16[256,320]{1,0:T(8,128)(2,1)}, bf16[256,320]{1,0:T(8,128)(2,1)}, u32[]{:S(2)}, u32[]{:S(2)}) collective-permute-start(bf16[256,320]{1,0:T(8,128)(2,1)} %reshape.438), channel_id=1, source_target_pairs={{0,1},{1,2},{2,3},{3,0},{4,5},{5,6},{6,7},{7,4},{8,9},{9,10},{10,1... | collective-permute-start | bytes 491528 | tf_op jit(solution)/shard_map/ppermute | solution.py:18
  91.7 2.3 fusion.3
  94.1 3.9 %collective-permute-start.8 = (bf16[256,384]{1,0:T(8,128)(2,1)S(1)}, bf16[256,384]{1,0:T(8,128)(2,1)S(1)}, u32[]{:S(2)}, u32[]{:S(2)}) collective-permute-start(bf16[256,384]{1,0:T(8,128)(2,1)S(1)} %reshape.436), channel_id=1, source_target_pairs={{0,1},{1,2},{2,3},{3,0},{4,5},{5,6},{6,7},{7,4},{8,9},{9,10},{10,1... | collective-permute-start | bytes 589832 | tf_op jit(solution)/shard_map/ppermute | solution.py:18
  98.1 5.3 %collective-permute-start.7 = (bf16[256,384]{1,0:T(8,128)(2,1)S(1)}, bf16[256,384]{1,0:T(8,128)(2,1)S(1)}, u32[]{:S(2)}, u32[]{:S(2)}) collective-permute-start(bf16[256,384]{1,0:T(8,128)(2,1)S(1)} %reshape.436), channel_id=1, source_target_pairs={{0,3},{1,0},{2,1},{3,2},{4,7},{5,4},{6,5},{7,6},{8,11},{9,8},{10,9... | collective-permute-start | bytes 589832 | tf_op jit(solution)/shard_map/ppermute | solution.py:18
  104.3 4.4 %collective-permute-start.18 = (bf16[128,320]{1,0:T(8,128)(2,1)S(1)}, bf16[128,320]{1,0:T(8,128)(2,1)S(1)}, u32[]{:S(2)}, u32[]{:S(2)}) collective-permute-start(bf16[128,320]{1,0:T(8,128)(2,1)S(1)} %slice.162), channel_id=1, source_target_pairs={{0,3},{1,0},{2,1},{3,2},{4,7},{5,4},{6,5},{7,6},{8,11},{9,8},{10,9... | collective-permute-start | bytes 245768 | tf_op jit(solution)/shard_map/ppermute | solution.py:18
  110.2 4.9 %collective-permute-done.12 = bf16[256,320]{1,0:T(8,128)(2,1)} collective-permute-done((bf16[256,320]{1,0:T(8,128)(2,1)}, bf16[256,320]{1,0:T(8,128)(2,1)}, u32[]{:S(2)}, u32[]{:S(2)}) %collective-permute-start.12) | collective-permute-done | bytes 163872 | tf_op jit(solution)/shard_map/ppermute | solution.py:18
  115.1 7.0 %collective-permute-start.17 = (bf16[128,320]{1,0:T(8,128)(2,1)S(1)}, bf16[128,320]{1,0:T(8,128)(2,1)S(1)}, u32[]{:S(2)}, u32[]{:S(2)}) collective-permute-start(bf16[128,320]{1,0:T(8,128)(2,1)S(1)} %slice.161), channel_id=1, source_target_pairs={{0,1},{1,2},{2,3},{3,0},{4,5},{5,6},{6,7},{7,4},{8,9},{9,10},{10,1... | collective-permute-start | bytes 245768 | tf_op jit(solution)/shard_map/ppermute | solution.py:18
  124.9 2.2 collective-permute-start.14
  127.8 8.0 %collective-permute-done.8 = bf16[256,384]{1,0:T(8,128)(2,1)S(1)} collective-permute-done((bf16[256,384]{1,0:T(8,128)(2,1)S(1)}, bf16[256,384]{1,0:T(8,128)(2,1)S(1)}, u32[]{:S(2)}, u32[]{:S(2)}) %collective-permute-start.8) | collective-permute-done | bytes 196640 | tf_op jit(solution)/shard_map/ppermute | solution.py:18
  135.8 6.0 %collective-permute-start.13 = (bf16[128,320]{1,0:T(8,128)(2,1)}, bf16[128,320]{1,0:T(8,128)(2,1)}, u32[]{:S(2)}, u32[]{:S(2)}) collective-permute-start(bf16[128,320]{1,0:T(8,128)(2,1)} %slice.158), channel_id=1, source_target_pairs={{0,1},{1,2},{2,3},{3,0},{4,5},{5,6},{6,7},{7,4},{8,9},{9,10},{10,1... | collective-permute-start | bytes 245768 | tf_op jit(solution)/shard_map/ppermute | solution.py:18
  142.5 3.2 collective-permute-start.10
  145.7 6.0 %collective-permute-start.9 = (bf16[128,384]{1,0:T(8,128)(2,1)}, bf16[128,384]{1,0:T(8,128)(2,1)}, u32[]{:S(2)}, u32[]{:S(2)}) collective-permute-start(bf16[128,384]{1,0:T(8,128)(2,1)} %slice.156), channel_id=1, source_target_pairs={{0,1},{1,2},{2,3},{3,0},{4,5},{5,6},{6,7},{7,4},{8,9},{9,10},{10,1... | collective-permute-start | bytes 294920 | tf_op jit(solution)/shard_map/ppermute | solution.py:18
  152.5 2.3 concatenate.54
  166.4 17.9 %all-to-all-start = ((bf16[32,8,704]{2,1,0:T(8,128)(2,1)}), bf16[32,8,704]{2,1,0:T(8,128)(2,1)}, u32[]{:S(2)}, u32[]{:S(2)}) async-start(bf16[32,8,704]{2,1,0:T(8,128)(2,1)} %bitcast.27), calls=%async_computation | async-start | bytes 786432 | tf_op jit(solution)/shard_map/all_to_all | solution.py:128
  185.8 1.8 convolution_add_fusion
  187.5 7.0 %all-to-all-done = bf16[32,8,704]{2,1,0:T(8,128)(2,1)} async-done(((bf16[32,8,704]{2,1,0:T(8,128)(2,1)}), bf16[32,8,704]{2,1,0:T(8,128)(2,1)}, u32[]{:S(2)}, u32[]{:S(2)}) %all-to-all-start) | async-done | bytes 360480 | tf_op jit(solution)/shard_map/all_to_all | solution.py:128
  196.9 10.8 %psum.7 = f32[6,256]{1,0:T(8,128)S(1)} all-reduce(f32[6,256]{1,0:T(8,128)S(1)} %stack.39), channel_id=1, replica_groups=mesh['g'=4,'y'=4,'x'=4,'c'=2,'m'=4] {'m'}, use_global_device_ids=true, to_apply=%region_15.16 | all-reduce | flops 1536 | bytes 12288 | tf_op jit(solution)/shard_map/psum | solution.py:165
  210.2 2.1 multiply_reduce_fusion
  212.4 5.5 %collective-permute-start.27 = (f32[832]{0:T(1024)S(1)}, f32[832]{0:T(1024)S(1)}, u32[]{:S(2)}, u32[]{:S(2)}) collective-permute-start(f32[832]{0:T(1024)S(1)} %get-tuple-element.80), channel_id=1, source_target_pairs={{0,3},{1,0},{2,1},{3,2},{4,7},{5,4},{6,5},{7,6},{8,11},{9,8},{10,9... | collective-permute-start | bytes 9992 | tf_op jit(solution)/shard_map/ppermute | solution.py:18
  217.8 7.0 %collective-permute-start.26 = (f32[832]{0:T(1024)S(1)}, f32[832]{0:T(1024)S(1)}, u32[]{:S(2)}, u32[]{:S(2)}) collective-permute-start(f32[832]{0:T(1024)S(1)} %get-tuple-element.79), channel_id=1, source_target_pairs={{0,2},{1,3},{2,0},{3,1},{4,6},{5,7},{6,4},{7,5},{8,10},{9,11},{10,... | collective-permute-start | bytes 9992 | tf_op jit(solution)/shard_map/ppermute | solution.py:18
  224.8 3.7 %collective-permute-start.25 = (f32[832]{0:T(1024)S(1)}, f32[832]{0:T(1024)S(1)}, u32[]{:S(2)}, u32[]{:S(2)}) collective-permute-start(f32[832]{0:T(1024)S(1)} %get-tuple-element.78), channel_id=1, source_target_pairs={{0,1},{1,2},{2,3},{3,0},{4,5},{5,6},{6,7},{7,4},{8,9},{9,10},{10,1... | collective-permute-start | bytes 9992 | tf_op jit(solution)/shard_map/ppermute | solution.py:18
  228.6 4.8 %fusion.4 = f32[1280,704]{0,1:T(8,128)} fusion(s32[1280]{0:T(1024)S(1)} %fusion.78, f32[256,1280]{1,0:T(8,128)S(1)} %subtract_multiply_fusion, f32[1280]{0:T(1024)S(1)} %concatenate.55, f32[256,320]{0,1:T(8,128)} %copy-done.5, f32[256,384]{0,1:T(8,128)} %copy-done.3), kind=kOutput, calls=%fused_computation.12 | convolution fusion | flops 1303576576 | bytes 5646336 | tf_op jit(solution)/shard_map/dot_general | solution.py:30
  233.4 2.6 dynamic-slice_convert_fusion
  236.2 5.1 %collective-permute-start.38 = (bf16[640,704]{0,1:T(8,128)(2,1)}, bf16[640,704]{0,1:T(8,128)(2,1)S(1)}, u32[]{:S(2)}, u32[]{:S(2)}) collective-permute-start(bf16[640,704]{0,1:T(8,128)(2,1)} %dynamic-slice_convert_fusion), channel_id=1, source_target_pairs={{0,4},{4,0},{1,5},{5,1},{2,6},{6,2},{3,7},{7,3},{8,12},{12,8},{9,1... | collective-permute-start | bytes 2703368 | tf_op jit(solution)/shard_map/ppermute | solution.py:18
  242.2 1.9 collective-permute-start.28
  245.2 2.4 collective-permute-start.31
  247.7 3.5 %collective-permute-start.30 = (f32[1025]{0:T(1024)S(1)}, f32[1025]{0:T(1024)S(1)}, u32[]{:S(2)}, u32[]{:S(2)}) collective-permute-start(f32[1025]{0:T(1024)S(1)} %add.624), channel_id=1, source_target_pairs={{0,16},{8,24},{16,0},{24,8},{1,17},{9,25},{17,1},{25,9},{2,18},{10... | collective-permute-start | bytes 12308 | tf_op jit(solution)/shard_map/ppermute | solution.py:18
  251.2 1.9 collective-permute-start.29
  253.6 3.3 collective-permute-done.29
  256.8 2.3 collective-permute-start.34
  259.2 2.6 collective-permute-start.33
  261.8 2.2 collective-permute-start.32
  264.9 5.4 %collective-permute-start.24 = (bf16[256,320]{1,0:T(8,128)(2,1)}, bf16[256,320]{1,0:T(8,128)(2,1)}, u32[]{:S(2)}, u32[]{:S(2)}) collective-permute-start(bf16[256,320]{1,0:T(8,128)(2,1)} %get-tuple-element.59), channel_id=1, source_target_pairs={{0,3},{1,0},{2,1},{3,2},{4,7},{5,4},{6,5},{7,6},{8,11},{9,8},{10,9... | collective-permute-start | bytes 491528 | tf_op jit(solution)/shard_map/ppermute | solution.py:18
  270.3 7.0 %collective-permute-start.23 = (bf16[256,320]{1,0:T(8,128)(2,1)S(1)}, bf16[256,320]{1,0:T(8,128)(2,1)}, u32[]{:S(2)}, u32[]{:S(2)}) collective-permute-start(bf16[256,320]{1,0:T(8,128)(2,1)S(1)} %get-tuple-element.60), channel_id=1, source_target_pairs={{0,2},{1,3},{2,0},{3,1},{4,6},{5,7},{6,4},{7,5},{8,10},{9,11},{10,... | collective-permute-start | bytes 491528 | tf_op jit(solution)/shard_map/ppermute | solution.py:18
  277.3 9.2 %collective-permute-start.37 = (f32[1025]{0:T(1024)S(1)}, f32[1025]{0:T(1024)S(1)}, u32[]{:S(2)}, u32[]{:S(2)}) collective-permute-start(f32[1025]{0:T(1024)S(1)} %add_add_fusion.1), channel_id=1, source_target_pairs={{0,384},{128,0},{256,128},{384,256},{1,385},{129,1},{257,129},{385... | collective-permute-start | bytes 12308 | tf_op jit(solution)/shard_map/ppermute | solution.py:18
  286.5 1.9 collective-permute-start.36
  288.4 2.2 collective-permute-start.35
  290.6 1.7 add_convert_fusion
  292.3 1.7 copy.45
  294.0 5.2 %all-to-all-start.1 = ((bf16[16,40,704]{2,1,0:T(8,128)(2,1)}), bf16[16,40,704]{2,1,0:T(8,128)(2,1)S(1)}, u32[]{:S(2)}, u32[]{:S(2)}) async-start(bf16[16,40,704]{2,1,0:T(8,128)(2,1)} %bitcast.49), calls=%async_computation.1 | async-start | bytes 1966080 | tf_op jit(solution)/shard_map/all_to_all | solution.py:188
  299.3 2.6 collective-permute-start.22
  304.4 8.0 %all-to-all-done.1 = bf16[16,40,704]{2,1,0:T(8,128)(2,1)S(1)} async-done(((bf16[16,40,704]{2,1,0:T(8,128)(2,1)}), bf16[16,40,704]{2,1,0:T(8,128)(2,1)S(1)}, u32[]{:S(2)}, u32[]{:S(2)}) %all-to-all-start.1) | async-done | bytes 901152 | tf_op jit(solution)/shard_map/all_to_all | solution.py:188
  312.6 4.9 %collective-permute-start.41 = (bf16[10,704]{1,0:T(8,128)(2,1)S(1)}, bf16[10,704]{1,0:T(8,128)(2,1)S(1)}, u32[]{:S(2)}, u32[]{:S(2)}) collective-permute-start(bf16[10,704]{1,0:T(8,128)(2,1)S(1)} %get-tuple-element.62), channel_id=1, source_target_pairs={{0,384},{128,0},{256,128},{384,256},{1,385},{129,1},{257,129},{385... | collective-permute-start | bytes 42248 | tf_op jit(solution)/shard_map/ppermute | solution.py:18
  317.5 2.2 collective-permute-start.40
  319.6 2.2 collective-permute-start.39
  (180 shorter events, 44.0 us)
Async XLA Ops:
  0.6 41.4 %copy-start.23 = (bf16[40,320]{1,0:T(8,128)(2,1)S(1)}, bf16[40,320]{1,0:T(8,128)(2,1)}, u32[]{:S(2)}) copy-start(bf16[40,320]{1,0:T(8,128)(2,1)} %param.19) | copy-start | bytes 76804
  0.6 41.4 %copy-start.22 = (bf16[48,384]{1,0:T(8,128)(2,1)S(1)}, bf16[48,384]{1,0:T(8,128)(2,1)}, u32[]{:S(2)}) copy-start(bf16[48,384]{1,0:T(8,128)(2,1)} %param.16) | copy-start | bytes 110596
  0.7 38.5 %copy-start.28 = (s32[1,64]{1,0:T(1,128)S(1)}, s32[1,64]{1,0:T(1,128)}, u32[]{:S(2)}) copy-start(s32[1,64]{1,0:T(1,128)} %param.20) | copy-start | bytes 772
  0.7 40.6 %copy-start.27 = (s32[2]{0:T(128)S(1)}, s32[2]{0:T(128)}, u32[]{:S(2)}) copy-start(s32[2]{0:T(128)} %param.21) | copy-start | bytes 28
  0.7 41.4 %copy-start.25 = (f32[320]{0:T(512)S(1)}, f32[320]{0:T(512)}, u32[]{:S(2)}) copy-start(f32[320]{0:T(512)} %param.27) | copy-start | bytes 3844
  0.7 41.4 %copy-start.26 = (f32[384]{0:T(512)S(1)}, f32[384]{0:T(512)}, u32[]{:S(2)}) copy-start(f32[384]{0:T(512)} %param.25) | copy-start | bytes 4612
  0.7 49.8 %copy-start.11 = (bf16[1280,320]{0,1:T(8,128)(2,1)S(1)}, bf16[1280,320]{0,1:T(8,128)(2,1)}, u32[]{:S(2)}) copy-start(bf16[1280,320]{0,1:T(8,128)(2,1)} %param.26) | copy-start | bytes 2457604
  0.7 74.9 %collective-permute-start.19 = (f32[320]{0:T(512)}, f32[320]{0:T(512)S(1)}, u32[]{:S(2)}, u32[]{:S(2)}) collective-permute-start(f32[320]{0:T(512)} %param.23), channel_id=1, source_target_pairs={{0,3},{1,0},{2,1},{3,2},{4,7},{5,4},{6,5},{7,6},{8,11},{9,8},{10,9... | collective-permute-start | bytes 3848 | tf_op jit(solution)/shard_map/ppermute | solution.py:18
  14.1 66.2 %collective-permute-start.20 = (f32[320]{0:T(512)}, f32[320]{0:T(512)S(1)}, u32[]{:S(2)}, u32[]{:S(2)}) collective-permute-start(f32[320]{0:T(512)} %param.23), channel_id=1, source_target_pairs={{0,2},{1,3},{2,0},{3,1},{4,6},{5,7},{6,4},{7,5},{8,10},{9,11},{10,... | collective-permute-start | bytes 3848 | tf_op jit(solution)/shard_map/ppermute | solution.py:18
  19.0 65.7 %collective-permute-start.21 = (f32[320]{0:T(512)}, f32[320]{0:T(512)S(1)}, u32[]{:S(2)}, u32[]{:S(2)}) collective-permute-start(f32[320]{0:T(512)} %param.23), channel_id=1, source_target_pairs={{0,1},{1,2},{2,3},{3,0},{4,5},{5,6},{6,7},{7,4},{8,9},{9,10},{10,1... | collective-permute-start | bytes 3848 | tf_op jit(solution)/shard_map/ppermute | solution.py:18
  27.1 15.0 %collective-permute-start = (bf16[88,384]{1,0:T(8,128)(2,1)S(1)}, bf16[88,384]{1,0:T(8,128)(2,1)S(1)}, u32[]{:S(2)}, u32[]{:S(2)}) collective-permute-start(bf16[88,384]{1,0:T(8,128)(2,1)S(1)} %fusion.56), channel_id=1, source_target_pairs={{0,8},{8,16},{16,24},{24,0},{1,9},{9,17},{17,25},{25,1},{2,10},{10... | collective-permute-start | bytes 202760 | tf_op jit(solution)/shard_map/ppermute | solution.py:18
  30.3 14.9 %collective-permute-start.1 = (bf16[88,384]{1,0:T(8,128)(2,1)S(1)}, bf16[88,384]{1,0:T(8,128)(2,1)S(1)}, u32[]{:S(2)}, u32[]{:S(2)}) collective-permute-start(bf16[88,384]{1,0:T(8,128)(2,1)S(1)} %fusion.56), channel_id=1, source_target_pairs={{0,16},{8,24},{16,0},{24,8},{1,17},{9,25},{17,1},{25,9},{2,18},{10... | collective-permute-start | bytes 202760 | tf_op jit(solution)/shard_map/ppermute | solution.py:18
  42.1 5.0 %collective-permute-start.2 = (bf16[88,384]{1,0:T(8,128)(2,1)S(1)}, bf16[88,384]{1,0:T(8,128)(2,1)S(1)}, u32[]{:S(2)}, u32[]{:S(2)}) collective-permute-start(bf16[88,384]{1,0:T(8,128)(2,1)S(1)} %fusion.56), channel_id=1, source_target_pairs={{0,24},{8,0},{16,8},{24,16},{1,25},{9,1},{17,9},{25,17},{2,26},{10... | collective-permute-start | bytes 202760 | tf_op jit(solution)/shard_map/ppermute | solution.py:18
  47.2 8.7 %collective-permute-start.3 = (bf16[4,88,384]{2,1,0:T(8,128)(2,1)S(1)}, bf16[4,88,384]{2,1,0:T(8,128)(2,1)S(1)}, u32[]{:S(2)}, u32[]{:S(2)}) collective-permute-start(bf16[4,88,384]{2,1,0:T(8,128)(2,1)S(1)} %bitcast_dynamic-update-slice_fusion.4), channel_id=1, source_target_pairs={{0,32},{32,64},{64,96},{96,0},{1,33},{33,65},{65,97},{97,1},{2,34}... | collective-permute-start | bytes 811016 | tf_op jit(solution)/shard_map/ppermute | solution.py:18
  51.2 11.0 %collective-permute-start.4 = (bf16[4,88,384]{2,1,0:T(8,128)(2,1)S(1)}, bf16[4,88,384]{2,1,0:T(8,128)(2,1)S(1)}, u32[]{:S(2)}, u32[]{:S(2)}) collective-permute-start(bf16[4,88,384]{2,1,0:T(8,128)(2,1)S(1)} %bitcast_dynamic-update-slice_fusion.4), channel_id=1, source_target_pairs={{0,64},{32,96},{64,0},{96,32},{1,65},{33,97},{65,1},{97,33},{2,66}... | collective-permute-start | bytes 811016 | tf_op jit(solution)/shard_map/ppermute | solution.py:18
  55.8 17.4 %copy-start.10 = (bf16[1280,384]{1,0:T(8,128)(2,1)S(1)}, bf16[1280,384]{1,0:T(8,128)(2,1)}, u32[]{:S(2)}) copy-start(bf16[1280,384]{1,0:T(8,128)(2,1)} %param.24) | copy-start | bytes 2949124
  55.9 10.1 %collective-permute-start.5 = (bf16[4,88,384]{2,1,0:T(8,128)(2,1)S(1)}, bf16[4,88,384]{2,1,0:T(8,128)(2,1)S(1)}, u32[]{:S(2)}, u32[]{:S(2)}) collective-permute-start(bf16[4,88,384]{2,1,0:T(8,128)(2,1)S(1)} %bitcast_dynamic-update-slice_fusion.4), channel_id=1, source_target_pairs={{0,96},{32,0},{64,32},{96,64},{1,97},{33,1},{65,33},{97,65},{2,98}... | collective-permute-start | bytes 811016 | tf_op jit(solution)/shard_map/ppermute | solution.py:18
  62.2 31.9 %collective-permute-start.15 = (bf16[256,320]{1,0:T(8,128)(2,1)}, bf16[256,320]{1,0:T(8,128)(2,1)S(1)}, u32[]{:S(2)}, u32[]{:S(2)}) collective-permute-start(bf16[256,320]{1,0:T(8,128)(2,1)} %bitcast.29), channel_id=1, source_target_pairs={{0,3},{1,0},{2,1},{3,2},{4,7},{5,4},{6,5},{7,6},{8,11},{9,8},{10,9... | collective-permute-start | bytes 491528 | tf_op jit(solution)/shard_map/ppermute | solution.py:18
  66.0 8.8 %copy-start.18 = (bf16[64,4,320]{2,1,0:T(4,128)(2,1)S(1)}, bf16[64,4,320]{2,1,0:T(4,128)(2,1)}, u32[]{:S(2)}) copy-start(bf16[64,4,320]{2,1,0:T(4,128)(2,1)} %param.17) | copy-start | bytes 491524
  66.0 23.6 %copy-start.20 = (bf16[64,4,320]{2,1,0:T(4,128)(2,1)S(1)}, bf16[64,4,320]{2,1,0:T(4,128)(2,1)}, u32[]{:S(2)}) copy-start(bf16[64,4,320]{2,1,0:T(4,128)(2,1)} %param.18) | copy-start | bytes 491524
  66.0 89.9 %collective-permute-start.6 = (bf16[4,4,88,384]{3,2,1,0:T(8,128)(2,1)S(1)}, bf16[4,4,88,384]{3,2,1,0:T(8,128)(2,1)}, u32[]{:S(2)}, u32[]{:S(2)}) collective-permute-start(bf16[4,4,88,384]{3,2,1,0:T(8,128)(2,1)S(1)} %bitcast_dynamic-update-slice_fusion), channel_id=1, source_target_pairs={{0,4},{4,0},{1,5},{5,1},{2,6},{6,2},{3,7},{7,3},{8,12},{12,8},{9,1... | collective-permute-start | bytes 3244040 | tf_op jit(solution)/shard_map/ppermute | solution.py:18
  74.8 15.8 %copy-start.21 = (bf16[64,4,384]{2,1,0:T(4,128)(2,1)S(1)}, bf16[64,4,384]{2,1,0:T(4,128)(2,1)}, u32[]{:S(2)}) copy-start(bf16[64,4,384]{2,1,0:T(4,128)(2,1)} %param.15) | copy-start | bytes 589828
  75.6 22.5 %collective-permute-start.16 = (bf16[256,320]{1,0:T(8,128)(2,1)}, bf16[256,320]{1,0:T(8,128)(2,1)}, u32[]{:S(2)}, u32[]{:S(2)}) collective-permute-start(bf16[256,320]{1,0:T(8,128)(2,1)} %bitcast.29), channel_id=1, source_target_pairs={{0,1},{1,2},{2,3},{3,0},{4,5},{5,6},{6,7},{7,4},{8,9},{9,10},{10,1... | collective-permute-start | bytes 491528 | tf_op jit(solution)/shard_map/ppermute | solution.py:18
  80.3 23.9 %collective-permute-start.11 = (bf16[256,320]{1,0:T(8,128)(2,1)}, bf16[256,320]{1,0:T(8,128)(2,1)}, u32[]{:S(2)}, u32[]{:S(2)}) collective-permute-start(bf16[256,320]{1,0:T(8,128)(2,1)} %reshape.438), channel_id=1, source_target_pairs={{0,3},{1,0},{2,1},{3,2},{4,7},{5,4},{6,5},{7,6},{8,11},{9,8},{10,9... | collective-permute-start | bytes 491528 | tf_op jit(solution)/shard_map/ppermute | solution.py:18
  84.8 30.4 %collective-permute-start.12 = (bf16[256,320]{1,0:T(8,128)(2,1)}, bf16[256,320]{1,0:T(8,128)(2,1)}, u32[]{:S(2)}, u32[]{:S(2)}) collective-permute-start(bf16[256,320]{1,0:T(8,128)(2,1)} %reshape.438), channel_id=1, source_target_pairs={{0,1},{1,2},{2,3},{3,0},{4,5},{5,6},{6,7},{7,4},{8,9},{9,10},{10,1... | collective-permute-start | bytes 491528 | tf_op jit(solution)/shard_map/ppermute | solution.py:18
  94.1 41.7 %collective-permute-start.8 = (bf16[256,384]{1,0:T(8,128)(2,1)S(1)}, bf16[256,384]{1,0:T(8,128)(2,1)S(1)}, u32[]{:S(2)}, u32[]{:S(2)}) collective-permute-start(bf16[256,384]{1,0:T(8,128)(2,1)S(1)} %reshape.436), channel_id=1, source_target_pairs={{0,1},{1,2},{2,3},{3,0},{4,5},{5,6},{6,7},{7,4},{8,9},{9,10},{10,1... | collective-permute-start | bytes 589832 | tf_op jit(solution)/shard_map/ppermute | solution.py:18
  98.1 26.8 %collective-permute-start.7 = (bf16[256,384]{1,0:T(8,128)(2,1)S(1)}, bf16[256,384]{1,0:T(8,128)(2,1)S(1)}, u32[]{:S(2)}, u32[]{:S(2)}) collective-permute-start(bf16[256,384]{1,0:T(8,128)(2,1)S(1)} %reshape.436), channel_id=1, source_target_pairs={{0,3},{1,0},{2,1},{3,2},{4,7},{5,4},{6,5},{7,6},{8,11},{9,8},{10,9... | collective-permute-start | bytes 589832 | tf_op jit(solution)/shard_map/ppermute | solution.py:18
  104.3 38.2 %collective-permute-start.18 = (bf16[128,320]{1,0:T(8,128)(2,1)S(1)}, bf16[128,320]{1,0:T(8,128)(2,1)S(1)}, u32[]{:S(2)}, u32[]{:S(2)}) collective-permute-start(bf16[128,320]{1,0:T(8,128)(2,1)S(1)} %slice.162), channel_id=1, source_target_pairs={{0,3},{1,0},{2,1},{3,2},{4,7},{5,4},{6,5},{7,6},{8,11},{9,8},{10,9... | collective-permute-start | bytes 245768 | tf_op jit(solution)/shard_map/ppermute | solution.py:18
  115.1 30.5 %collective-permute-start.17 = (bf16[128,320]{1,0:T(8,128)(2,1)S(1)}, bf16[128,320]{1,0:T(8,128)(2,1)S(1)}, u32[]{:S(2)}, u32[]{:S(2)}) collective-permute-start(bf16[128,320]{1,0:T(8,128)(2,1)S(1)} %slice.161), channel_id=1, source_target_pairs={{0,1},{1,2},{2,3},{3,0},{4,5},{5,6},{6,7},{7,4},{8,9},{9,10},{10,1... | collective-permute-start | bytes 245768 | tf_op jit(solution)/shard_map/ppermute | solution.py:18
  124.9 10.9 %copy-start.12 = (bf16[256,384]{1,0:T(8,128)(2,1)}, bf16[256,384]{1,0:T(8,128)(2,1)S(1)}, u32[]{:S(2)}) copy-start(bf16[256,384]{1,0:T(8,128)(2,1)S(1)} %collective-permute-done.7) | copy-start | bytes 589828
  124.9 37.2 %collective-permute-start.14 = (bf16[128,320]{1,0:T(8,128)(2,1)}, bf16[128,320]{1,0:T(8,128)(2,1)}, u32[]{:S(2)}, u32[]{:S(2)}) collective-permute-start(bf16[128,320]{1,0:T(8,128)(2,1)} %slice.159), channel_id=1, source_target_pairs={{0,3},{1,0},{2,1},{3,2},{4,7},{5,4},{6,5},{7,6},{8,11},{9,8},{10,9... | collective-permute-start | bytes 245768 | tf_op jit(solution)/shard_map/ppermute | solution.py:18
  135.8 6.0 %copy-start.14 = (bf16[256,384]{1,0:T(8,128)(2,1)}, bf16[256,384]{1,0:T(8,128)(2,1)S(1)}, u32[]{:S(2)}) copy-start(bf16[256,384]{1,0:T(8,128)(2,1)S(1)} %collective-permute-done.8) | copy-start | bytes 589828
  135.8 26.3 %collective-permute-start.13 = (bf16[128,320]{1,0:T(8,128)(2,1)}, bf16[128,320]{1,0:T(8,128)(2,1)}, u32[]{:S(2)}, u32[]{:S(2)}) collective-permute-start(bf16[128,320]{1,0:T(8,128)(2,1)} %slice.158), channel_id=1, source_target_pairs={{0,1},{1,2},{2,3},{3,0},{4,5},{5,6},{6,7},{7,4},{8,9},{9,10},{10,1... | collective-permute-start | bytes 245768 | tf_op jit(solution)/shard_map/ppermute | solution.py:18
  142.4 9.2 %copy-start.16 = (bf16[128,320]{1,0:T(8,128)(2,1)}, bf16[128,320]{1,0:T(8,128)(2,1)S(1)}, u32[]{:S(2)}) copy-start(bf16[128,320]{1,0:T(8,128)(2,1)S(1)} %collective-permute-done.18) | copy-start | bytes 245764
  142.5 21.3 %collective-permute-start.10 = (bf16[128,384]{1,0:T(8,128)(2,1)}, bf16[128,384]{1,0:T(8,128)(2,1)}, u32[]{:S(2)}, u32[]{:S(2)}) collective-permute-start(bf16[128,384]{1,0:T(8,128)(2,1)} %slice.157), channel_id=1, source_target_pairs={{0,3},{1,0},{2,1},{3,2},{4,7},{5,4},{6,5},{7,6},{8,11},{9,8},{10,9... | collective-permute-start | bytes 294920 | tf_op jit(solution)/shard_map/ppermute | solution.py:18
  145.7 6.0 %copy-start.17 = (bf16[128,320]{1,0:T(8,128)(2,1)}, bf16[128,320]{1,0:T(8,128)(2,1)S(1)}, u32[]{:S(2)}) copy-start(bf16[128,320]{1,0:T(8,128)(2,1)S(1)} %collective-permute-done.17) | copy-start | bytes 245764
  145.7 18.1 %collective-permute-start.9 = (bf16[128,384]{1,0:T(8,128)(2,1)}, bf16[128,384]{1,0:T(8,128)(2,1)}, u32[]{:S(2)}, u32[]{:S(2)}) collective-permute-start(bf16[128,384]{1,0:T(8,128)(2,1)} %slice.156), channel_id=1, source_target_pairs={{0,1},{1,2},{2,3},{3,0},{4,5},{5,6},{6,7},{7,4},{8,9},{9,10},{10,1... | collective-permute-start | bytes 294920 | tf_op jit(solution)/shard_map/ppermute | solution.py:18
  157.6 2.9 copy-start.13
  159.2 2.9 copy-start.9
  166.4 28.1 %all-to-all-start = ((bf16[32,8,704]{2,1,0:T(8,128)(2,1)}), bf16[32,8,704]{2,1,0:T(8,128)(2,1)}, u32[]{:S(2)}, u32[]{:S(2)}) async-start(bf16[32,8,704]{2,1,0:T(8,128)(2,1)} %bitcast.27), calls=%async_computation | async-start | bytes 786432 | tf_op jit(solution)/shard_map/all_to_all | solution.py:128
  209.0 3.3 %copy-start.5 = (f32[256,320]{0,1:T(8,128)}, f32[256,320]{0,1:T(8,128)S(1)}, u32[]{:S(2)}) copy-start(f32[256,320]{0,1:T(8,128)S(1)} %subtract_multiply_fusion.2) | copy-start | bytes 983044
  212.4 29.0 %collective-permute-start.27 = (f32[832]{0:T(1024)S(1)}, f32[832]{0:T(1024)S(1)}, u32[]{:S(2)}, u32[]{:S(2)}) collective-permute-start(f32[832]{0:T(1024)S(1)} %get-tuple-element.80), channel_id=1, source_target_pairs={{0,3},{1,0},{2,1},{3,2},{4,7},{5,4},{6,5},{7,6},{8,11},{9,8},{10,9... | collective-permute-start | bytes 9992 | tf_op jit(solution)/shard_map/ppermute | solution.py:18
  217.8 23.5 %collective-permute-start.26 = (f32[832]{0:T(1024)S(1)}, f32[832]{0:T(1024)S(1)}, u32[]{:S(2)}, u32[]{:S(2)}) collective-permute-start(f32[832]{0:T(1024)S(1)} %get-tuple-element.79), channel_id=1, source_target_pairs={{0,2},{1,3},{2,0},{3,1},{4,6},{5,7},{6,4},{7,5},{8,10},{9,11},{10,... | collective-permute-start | bytes 9992 | tf_op jit(solution)/shard_map/ppermute | solution.py:18
  224.8 16.6 %collective-permute-start.25 = (f32[832]{0:T(1024)S(1)}, f32[832]{0:T(1024)S(1)}, u32[]{:S(2)}, u32[]{:S(2)}) collective-permute-start(f32[832]{0:T(1024)S(1)} %get-tuple-element.78), channel_id=1, source_target_pairs={{0,1},{1,2},{2,3},{3,0},{4,5},{5,6},{6,7},{7,4},{8,9},{9,10},{10,1... | collective-permute-start | bytes 9992 | tf_op jit(solution)/shard_map/ppermute | solution.py:18
  233.4 2.6 copy-start.6
  233.4 30.6 %copy-start.7 = (bf16[256,1280]{1,0:T(8,128)(2,1)S(1)}, bf16[256,1280]{1,0:T(8,128)(2,1)}, u32[]{:S(2)}) copy-start(bf16[256,1280]{1,0:T(8,128)(2,1)} %get-tuple-element.57) | copy-start | bytes 1966084
  236.2 52.2 %collective-permute-start.38 = (bf16[640,704]{0,1:T(8,128)(2,1)}, bf16[640,704]{0,1:T(8,128)(2,1)S(1)}, u32[]{:S(2)}, u32[]{:S(2)}) collective-permute-start(bf16[640,704]{0,1:T(8,128)(2,1)} %dynamic-slice_convert_fusion), channel_id=1, source_target_pairs={{0,4},{4,0},{1,5},{5,1},{2,6},{6,2},{3,7},{7,3},{8,12},{12,8},{9,1... | collective-permute-start | bytes 2703368 | tf_op jit(solution)/shard_map/ppermute | solution.py:18
  242.2 3.1 collective-permute-start.28
  245.2 8.0 %collective-permute-start.31 = (f32[1025]{0:T(1024)S(1)}, f32[1025]{0:T(1024)S(1)}, u32[]{:S(2)}, u32[]{:S(2)}) collective-permute-start(f32[1025]{0:T(1024)S(1)} %add.624), channel_id=1, source_target_pairs={{0,24},{8,0},{16,8},{24,16},{1,25},{9,1},{17,9},{25,17},{2,26},{10... | collective-permute-start | bytes 12308 | tf_op jit(solution)/shard_map/ppermute | solution.py:18
  247.7 5.9 %collective-permute-start.30 = (f32[1025]{0:T(1024)S(1)}, f32[1025]{0:T(1024)S(1)}, u32[]{:S(2)}, u32[]{:S(2)}) collective-permute-start(f32[1025]{0:T(1024)S(1)} %add.624), channel_id=1, source_target_pairs={{0,16},{8,24},{16,0},{24,8},{1,17},{9,25},{17,1},{25,9},{2,18},{10... | collective-permute-start | bytes 12308 | tf_op jit(solution)/shard_map/ppermute | solution.py:18
  251.2 5.6 %collective-permute-start.29 = (f32[1025]{0:T(1024)S(1)}, f32[1025]{0:T(1024)S(1)}, u32[]{:S(2)}, u32[]{:S(2)}) collective-permute-start(f32[1025]{0:T(1024)S(1)} %add.624), channel_id=1, source_target_pairs={{0,8},{8,16},{16,24},{24,0},{1,9},{9,17},{17,25},{25,1},{2,10},{10... | collective-permute-start | bytes 12308 | tf_op jit(solution)/shard_map/ppermute | solution.py:18
  256.8 13.4 %collective-permute-start.34 = (f32[1025]{0:T(1024)S(1)}, f32[1025]{0:T(1024)S(1)}, u32[]{:S(2)}, u32[]{:S(2)}) collective-permute-start(f32[1025]{0:T(1024)S(1)} %add_add_fusion.2), channel_id=1, source_target_pairs={{0,96},{32,0},{64,32},{96,64},{1,97},{33,1},{65,33},{97,65},{2,98}... | collective-permute-start | bytes 12308 | tf_op jit(solution)/shard_map/ppermute | solution.py:18
  259.2 18.1 %collective-permute-start.33 = (f32[1025]{0:T(1024)S(1)}, f32[1025]{0:T(1024)S(1)}, u32[]{:S(2)}, u32[]{:S(2)}) collective-permute-start(f32[1025]{0:T(1024)S(1)} %add_add_fusion.2), channel_id=1, source_target_pairs={{0,64},{32,96},{64,0},{96,32},{1,65},{33,97},{65,1},{97,33},{2,66}... | collective-permute-start | bytes 12308 | tf_op jit(solution)/shard_map/ppermute | solution.py:18
  261.8 15.5 %collective-permute-start.32 = (f32[1025]{0:T(1024)S(1)}, f32[1025]{0:T(1024)S(1)}, u32[]{:S(2)}, u32[]{:S(2)}) collective-permute-start(f32[1025]{0:T(1024)S(1)} %add_add_fusion.2), channel_id=1, source_target_pairs={{0,32},{32,64},{64,96},{96,0},{1,33},{33,65},{65,97},{97,1},{2,34}... | collective-permute-start | bytes 12308 | tf_op jit(solution)/shard_map/ppermute | solution.py:18
  264.9 54.7 %collective-permute-start.24 = (bf16[256,320]{1,0:T(8,128)(2,1)}, bf16[256,320]{1,0:T(8,128)(2,1)}, u32[]{:S(2)}, u32[]{:S(2)}) collective-permute-start(bf16[256,320]{1,0:T(8,128)(2,1)} %get-tuple-element.59), channel_id=1, source_target_pairs={{0,3},{1,0},{2,1},{3,2},{4,7},{5,4},{6,5},{7,6},{8,11},{9,8},{10,9... | collective-permute-start | bytes 491528 | tf_op jit(solution)/shard_map/ppermute | solution.py:18
  270.3 51.6 %collective-permute-start.23 = (bf16[256,320]{1,0:T(8,128)(2,1)S(1)}, bf16[256,320]{1,0:T(8,128)(2,1)}, u32[]{:S(2)}, u32[]{:S(2)}) collective-permute-start(bf16[256,320]{1,0:T(8,128)(2,1)S(1)} %get-tuple-element.60), channel_id=1, source_target_pairs={{0,2},{1,3},{2,0},{3,1},{4,6},{5,7},{6,4},{7,5},{8,10},{9,11},{10,... | collective-permute-start | bytes 491528 | tf_op jit(solution)/shard_map/ppermute | solution.py:18
  277.3 22.0 %collective-permute-start.37 = (f32[1025]{0:T(1024)S(1)}, f32[1025]{0:T(1024)S(1)}, u32[]{:S(2)}, u32[]{:S(2)}) collective-permute-start(f32[1025]{0:T(1024)S(1)} %add_add_fusion.1), channel_id=1, source_target_pairs={{0,384},{128,0},{256,128},{384,256},{1,385},{129,1},{257,129},{385... | collective-permute-start | bytes 12308 | tf_op jit(solution)/shard_map/ppermute | solution.py:18
  286.5 15.4 %collective-permute-start.36 = (f32[1025]{0:T(1024)S(1)}, f32[1025]{0:T(1024)S(1)}, u32[]{:S(2)}, u32[]{:S(2)}) collective-permute-start(f32[1025]{0:T(1024)S(1)} %add_add_fusion.1), channel_id=1, source_target_pairs={{0,256},{128,384},{256,0},{384,128},{1,257},{129,385},{257,1},{385... | collective-permute-start | bytes 12308 | tf_op jit(solution)/shard_map/ppermute | solution.py:18
  288.4 13.5 %collective-permute-start.35 = (f32[1025]{0:T(1024)S(1)}, f32[1025]{0:T(1024)S(1)}, u32[]{:S(2)}, u32[]{:S(2)}) collective-permute-start(f32[1025]{0:T(1024)S(1)} %add_add_fusion.1), channel_id=1, source_target_pairs={{0,128},{128,256},{256,384},{384,0},{1,129},{129,257},{257,385},{3... | collective-permute-start | bytes 12308 | tf_op jit(solution)/shard_map/ppermute | solution.py:18
  294.0 18.3 %all-to-all-start.1 = ((bf16[16,40,704]{2,1,0:T(8,128)(2,1)}), bf16[16,40,704]{2,1,0:T(8,128)(2,1)S(1)}, u32[]{:S(2)}, u32[]{:S(2)}) async-start(bf16[16,40,704]{2,1,0:T(8,128)(2,1)} %bitcast.49), calls=%async_computation.1 | async-start | bytes 1966080 | tf_op jit(solution)/shard_map/all_to_all | solution.py:188
  299.3 22.6 %collective-permute-start.22 = (bf16[256,320]{1,0:T(8,128)(2,1)S(1)}, bf16[256,320]{1,0:T(8,128)(2,1)S(1)}, u32[]{:S(2)}, u32[]{:S(2)}) collective-permute-start(bf16[256,320]{1,0:T(8,128)(2,1)S(1)} %get-tuple-element.58), channel_id=1, source_target_pairs={{0,1},{1,2},{2,3},{3,0},{4,5},{5,6},{6,7},{7,4},{8,9},{9,10},{10,1... | collective-permute-start | bytes 491528 | tf_op jit(solution)/shard_map/ppermute | solution.py:18
  312.6 11.5 %collective-permute-start.41 = (bf16[10,704]{1,0:T(8,128)(2,1)S(1)}, bf16[10,704]{1,0:T(8,128)(2,1)S(1)}, u32[]{:S(2)}, u32[]{:S(2)}) collective-permute-start(bf16[10,704]{1,0:T(8,128)(2,1)S(1)} %get-tuple-element.62), channel_id=1, source_target_pairs={{0,384},{128,0},{256,128},{384,256},{1,385},{129,1},{257,129},{385... | collective-permute-start | bytes 42248 | tf_op jit(solution)/shard_map/ppermute | solution.py:18
  317.5 7.0 %collective-permute-start.40 = (bf16[10,704]{1,0:T(8,128)(2,1)S(1)}, bf16[10,704]{1,0:T(8,128)(2,1)S(1)}, u32[]{:S(2)}, u32[]{:S(2)}) collective-permute-start(bf16[10,704]{1,0:T(8,128)(2,1)S(1)} %get-tuple-element.63), channel_id=1, source_target_pairs={{0,256},{128,384},{256,0},{384,128},{1,257},{129,385},{257,1},{385... | collective-permute-start | bytes 42248 | tf_op jit(solution)/shard_map/ppermute | solution.py:18
  319.6 6.4 %collective-permute-start.39 = (bf16[10,704]{1,0:T(8,128)(2,1)S(1)}, bf16[10,704]{1,0:T(8,128)(2,1)S(1)}, u32[]{:S(2)}, u32[]{:S(2)}) collective-permute-start(bf16[10,704]{1,0:T(8,128)(2,1)S(1)} %get-tuple-element.61), channel_id=1, source_target_pairs={{0,128},{128,256},{256,384},{384,0},{1,129},{129,257},{257,385},{3... | collective-permute-start | bytes 42248 | tf_op jit(solution)/shard_map/ppermute | solution.py:18
  (9 other events, 17.0 us)

commit v2 on v1

v2 whole, which is shorter than its diff:
```python
import jax
import jax.numpy as jnp
from jax import lax
from jax.sharding import Mesh
from jax.sharding import PartitionSpec as P

eps = 1e-06
loss_weight = 1024.0
f32 = jnp.float32
bf16 = jnp.bfloat16

EXTENT = {"g": 4, "y": 4, "x": 4, "c": 2, "m": 4}
DP = ("y", "x", "c")


def swap(array):
    return lax.ppermute(array, "c", [(0, 1), (1, 0)])


def exchange(array, axis):
    return lax.all_to_all(array, axis, split_axis=0, concat_axis=0, tiled=True)


def dot(a, b):
    return jnp.dot(a, b, preferred_element_type=f32)


def dot_last(a, b):
    return lax.dot_general(a, b, (((1,), (1,)), ((), ())), preferred_element_type=f32)


def dot_rows(a, b):
    return lax.dot_general(a, b, (((0,), (0,)), ((), ())), preferred_element_type=f32)


def one_hot(picked, width):
    return (lax.broadcasted_iota(jnp.int32, (picked.shape[0], width), 1) == picked[:, None]).astype(
        bf16
    )


def split(array, count):
    terms = []
    for _ in range(count):
        term = lax.reduce_precision(array, 8, 7)
        terms.append(term.astype(bf16))
        array = array - term
    return terms


def to_rows(vector, width):
    terms = jnp.concatenate(split(vector, 2))
    rows = -(-terms.shape[0] // (8 * width)) * 8
    return jnp.pad(terms, (0, rows * width - terms.shape[0])).reshape(rows, width)


def from_rows(rows, length):
    terms = rows.astype(f32).reshape(*rows.shape[:-2], -1)
    return terms[..., :length] + terms[..., length : 2 * length]


def head_grad(out, target, inner, square, tsquare, live):
    inverse = lax.rsqrt(square + eps) * lax.rsqrt(tsquare + eps)
    cosine = inner * inverse
    return -loss_weight * live * (target * inverse - cosine * out / (square + eps))


def local(
    dino_context,
    dino_stream,
    dino_out_proj,
    sam_context,
    sam_stream,
    sam_out_proj,
    owners,
    valid_rows,
    student_stream,
    norm_gain,
    adapt_dino,
    adapt_dino_bias,
    adapt_sam,
    adapt_sam_bias,
):
    m, c = lax.axis_index("m"), lax.axis_index("c")
    slots, per_peer, wd = dino_context.shape
    ws = sam_context.shape[2]
    rows = slots * per_peer
    own_slots, window, wf = student_stream.shape
    wt = wd + ws
    feats = wf * EXTENT["m"]
    peers = slots // own_slots
    kd, ks = dino_out_proj.shape[0], sam_out_proj.shape[0]

    gain_terms = jnp.pad(jnp.stack(split(norm_gain, 3)), ((0, 5), (0, ws)))
    sam_student = jnp.concatenate(
        [sam_context.reshape(rows, ws), student_stream.reshape(rows, wf)], axis=1
    )
    sam_student = lax.all_gather(
        jnp.concatenate([sam_student, gain_terms], axis=0), "m", axis=0, tiled=False
    )
    dino_full = lax.all_gather(dino_context.reshape(rows, wd), "m", axis=1, tiled=True)
    packed = jnp.concatenate(
        [dino_out_proj, jnp.pad(sam_out_proj, ((0, 0), (0, wd - ws)))], axis=0
    )
    proj = exchange(jnp.tile(packed, (peers, 1)), DP).reshape(peers, kd + ks, wd)
    dino_proj = proj[:, :kd].reshape(peers * kd, wd)
    sam_proj = proj[:, kd:, :ws].reshape(peers * ks, ws)

    dino_mixed = dot(dino_full, dino_proj)
    sam_full = jnp.concatenate([sam_student[j, :rows, :ws] for j in range(4)], axis=1)
    sam_mixed = dot(sam_full, sam_proj)
    dino_feat = (dino_stream.reshape(rows, wd).astype(f32) + dino_mixed).astype(bf16)
    sam_feat = (sam_stream.reshape(rows, ws).astype(f32) + sam_mixed).astype(bf16)
    feat = jnp.concatenate([dino_feat, sam_feat], axis=1)
    image_row = jnp.arange(per_peer, dtype=jnp.int32)[None, :]
    goes_to = (owners[0][:, None] * per_peer + image_row).reshape(-1)
    sent = dot_rows(one_hot(goes_to, rows), feat).astype(bf16)
    arrived = exchange(sent, DP)
    place = jnp.arange(rows, dtype=jnp.int32)
    slot, row = place // window, place % window
    source = (row // per_peer) * (own_slots * per_peer) + slot * per_peer + row % per_peer
    target = dot(one_hot(source, rows), arrived)
    dino_target, sam_target = target[:, :wd], target[:, wd:]

    live = (
        (jnp.arange(window, dtype=jnp.int32)[None, :] < valid_rows[:, None])
        .astype(f32)
        .reshape(rows, 1)
    )
    values = jnp.concatenate([sam_student[j, :rows, ws:] for j in range(4)], axis=1).astype(f32)
    terms = sam_student[:, rows : rows + 3, :wf].astype(f32)
    gain = (terms[:, 0] + (terms[:, 1] + terms[:, 2])).reshape(1, feats)
    center = jnp.sum(values, axis=1, keepdims=True) / feats
    spread = jnp.sum(values * values, axis=1, keepdims=True) / feats - center * center
    scale = lax.rsqrt(spread + eps)
    standard = (values - center) * scale
    normed = (standard * gain).astype(bf16)
    adapt = jnp.concatenate([adapt_dino, adapt_sam], axis=1)
    out = dot(normed, adapt) + jnp.concatenate([adapt_dino_bias, adapt_sam_bias])[None, :]
    dino_out, sam_out = out[:, :wd], out[:, wd:]
    each = feats // (EXTENT["g"] * peers)
    spot = jnp.arange(feats, dtype=jnp.int32)
    i, rest = spot % each, spot // each
    g_of, rest = rest % 4, rest // 4
    x_of, rest = rest % 4, rest // 4
    y_of, c_of = rest % 4, (rest // 4 + c) % 2
    feature = (((g_of * 4 + y_of) * 4 + x_of) * 2 + c_of) * each + i
    dealt = dot_last(normed, one_hot(feature, feats)).astype(bf16)

    stats = lax.psum(
        jnp.stack(
            [
                jnp.sum(dino_out * dino_target, axis=1),
                jnp.sum(dino_out * dino_out, axis=1),
                jnp.sum(dino_target * dino_target, axis=1),
                jnp.sum(sam_out * sam_target, axis=1),
                jnp.sum(sam_out * sam_out, axis=1),
                jnp.sum(sam_target * sam_target, axis=1),
            ]
        ),
        "m",
    )[:, :, None]
    dino_grad = head_grad(dino_out, dino_target, stats[0], stats[1], stats[2], live)
    sam_grad = head_grad(sam_out, sam_target, stats[3], stats[4], stats[5], live)
    grad = jnp.concatenate([dino_grad, sam_grad], axis=1)
    back = grad.astype(bf16)

    partial = dot_last(adapt, back)
    low = lax.psum_scatter(partial.astype(bf16), "m", scatter_dimension=0, tiled=True)
    scaled_part = partial * gain.T
    row_sums = jnp.stack(
        [jnp.sum(scaled_part, axis=0), jnp.sum(scaled_part * standard.T, axis=0)]
    )
    gain_part = jnp.sum(partial * standard.T, axis=1)

    half = feats // 2
    length = wt + feats + 1
    vector = jnp.concatenate([jnp.sum(grad, axis=0), gain_part, jnp.sum(live).reshape(1)])
    mine = dot_rows(dealt[:, :half], back)
    theirs = dot_rows(dealt[:, half:], back).astype(bf16)
    received = swap(jnp.concatenate([theirs, to_rows(vector, wt)], axis=0))
    chip = (mine + received[:half].astype(f32)).astype(bf16)
    vector = vector + from_rows(received[half:], length)
    beside = to_rows(vector, wt)
    chip = jnp.concatenate(
        [chip.reshape(16, -1, wt), jnp.broadcast_to(beside[None], (16,) + beside.shape)], axis=1
    )
    chip, row_sums = lax.optimization_barrier((chip, row_sums))
    slab = exchange(chip.reshape(-1, wt), ("y", "x")).reshape(chip.shape)
    row_sums = lax.psum(row_sums, "m")
    strip = 4 * each
    weight = jnp.sum(slab[:, :strip].astype(f32), axis=0).astype(bf16)
    vector = jnp.sum(from_rows(slab[:, strip:], length), axis=0)
    beside = to_rows(vector, wt)
    deal = jnp.concatenate(
        [weight.reshape(4, each, wt), jnp.broadcast_to(beside[None], (4,) + beside.shape)], axis=1
    )
    share = exchange(deal.reshape(-1, wt), "g").reshape(deal.shape)
    weight = jnp.sum(share[:, :each].astype(f32), axis=0)
    vector = jnp.sum(from_rows(share[:, each:], length), axis=0)
    factor = lax.rsqrt(vector[-1])
    weight = (factor * weight).astype(bf16)
    gain_grad = factor * lax.psum_scatter(vector[wt:-1], "m", scatter_dimension=0, tiled=True)

    own = student_stream.reshape(rows, wf).astype(f32)
    own_standard = (own - center) * scale
    scaled = low.astype(f32).T * norm_gain[None, :]
    first_sum, second_sum = row_sums[0][:, None] / feats, row_sums[1][:, None] / feats
    stream_grad = ((scaled - first_sum - own_standard * second_sum) * scale).astype(bf16)
    return (
        stream_grad.reshape(own_slots, window, wf),
        weight[:, :wd],
        factor * vector[:wd],
        weight[:, wd:],
        factor * vector[wd:wt],
        gain_grad,
    )


def solution(mesh):
    parts = Mesh(
        mesh.devices.reshape(tuple(EXTENT[axis] for axis in ("g", "y", "x", "c", "m"))),
        ("g", "y", "x", "c", "m"),
    )
    every = ("g",) + DP
    placed = (
        P("g", DP, "m"),
        P("g", DP, "m"),
        P(DP, "m"),
        P("g", DP, "m"),
        P("g", DP, "m"),
        P(DP, "m"),
        P("g", None),
        P(every),
        P(every, None, "m"),
        P("m"),
        P(None, "m"),
        P("m"),
        P(None, "m"),
        P("m"),
    )
    return jax.shard_map(
        local,
        mesh=parts,
        in_specs=placed,
        out_specs=(
            P(every, None, "m"),
            P(every, "m"),
            P("m"),
            P(every, "m"),
            P("m"),
            P("m"),
        ),
        check_vma=False,
    )
```

time: 334 us -> 272 us (0.81); the launches traced: 327 us -> 271 us
  starting transfers between devices: 207 us -> 26.7 us
  blocking collectives: 10.8 us -> 142 us
  between operations: 2.89 us -> 16 us
  waiting for transfers between devices: 41.1 us -> 30.1 us
  other arithmetic: 22.5 us -> 11.8 us
  local copies, waits for them, and re-layouts: 25 us -> 34.1 us
  matrix products: 17.7 us -> 9.75 us
    ppermute x42 -> x1, starting transfers between devices: 184 us -> 4.46 us  [swap(): return lax.ppermute(array, 'c', [(0, 1), (1, 0)])]
    all_gather x0 -> x1, blocking collectives: none -> 89.7 us  [local(): lax.all_gather(dino_context.reshape(rows, wd), 'm', axis=1, tiled=True)]
    ppermute x42 -> x1, waiting for transfers between devices: 26.2 us -> 1.75 us  [swap(): return lax.ppermute(array, 'c', [(0, 1), (1, 0)])]
    all_to_all x0 -> x1, blocking collectives: none -> 20.9 us  [exchange(): return lax.all_to_all(array, axis, split_axis=0, concat_axis=0, tiled=True)]
    psum x0 -> x1, blocking collectives: none -> 19.1 us  [local(): row_sums = lax.psum(row_sums, 'm')]
    reduce_scatter x0 -> x1, waiting for transfers between devices: none -> 18.6 us  [local(): lax.psum_scatter(partial.astype(bf16), 'm', scatter_dimension=0, tiled=True)]
    unnamed x61 -> x53, local copies, waits for them, and re-layouts: 4.14 us -> 14.7 us
    dot_general x11 -> x4, matrix products: 10.9 us -> 2.52 us  [dot(): return jnp.dot(a, b, preferred_element_type=f32)]
  transfers between devices with their start and end apart: 44 -> 6, of which waited for: 12 -> 5; matrix products, arithmetic and copies ran while one was open for 17% -> 11% of each run, Pallas kernels for 0% -> 0%
where the time goes in v2:
time: 272 us; the launch traced here: 271 us
  blocking collectives  142 us (52%)
  local copies, waits for them, and re-layouts  34.1 us (13%)
  waiting for transfers between devices  30.1 us (11%)
  starting transfers between devices  26.7 us (10%)
  between operations  16 us (6%)
  other arithmetic  11.8 us (4%)
  matrix products  9.75 us (4%)
    all_gather x1, blocking collectives, local(): lax.all_gather(dino_context.reshape(rows, wd), 'm', axis=1, tiled=True)  89.7 us
    all_to_all x3, starting transfers between devices, exchange(): return lax.all_to_all(array, axis, split_axis=0, concat_axis=0, tiled=True)  22.1 us
    all_to_all x1, blocking collectives, exchange(): return lax.all_to_all(array, axis, split_axis=0, concat_axis=0, tiled=True)  20.9 us
    psum x1, blocking collectives, local(): row_sums = lax.psum(row_sums, 'm')  19.1 us
    reduce_scatter x1, waiting for transfers between devices, local(): lax.psum_scatter(partial.astype(bf16), 'm', scatter_dimension=0, tiled=True)  18.6 us
    unnamed x53, local copies, waits for them, and re-layouts  14.7 us
    psum x1, blocking collectives, local(): lax.psum(jnp.stack([jnp.sum(dino_out * dino_target, axis=1), jnp.sum(dino...  12.7 us
    all_to_all x3, waiting for transfers between devices, exchange(): return lax.all_to_all(array, axis, split_axis=0, concat_axis=0, tiled=True)  9.26 us
  transfers between devices with their start and end apart: 6, of which 5 were waited for; matrix products, arithmetic and copies ran while one was open for 11% of the time, Pallas kernels for 0%

profile of v2, /device:TPU:1, one launch (start us, length us, event | category | flops | bytes accessed | tf_op | source)
XLA Modules:
  0.0 270.8 jit_solution(8615764212593386064)
XLA Ops:
  7.2 0.7 reduce-precision_convert_fusion.4
  8.0 0.2 copy.78
  8.2 1.0 reshape.475
  9.2 0.1 copy.77
  9.4 0.9 copy.79
  10.4 1.5 tile.2
  11.9 10.7 %all-to-all-start = ((bf16[32,88,384]{2,1,0:T(8,128)(2,1)}), bf16[32,88,384]{2,1,0:T(8,128)(2,1)S(1)}, u32[]{:S(2)}, u32[]{:S(2)}) async-start(bf16[32,88,384]{2,1,0:T(8,128)(2,1)} %tile.2), calls=%async_computation | async-start | bytes 4325376 | tf_op jit(solution)/shard_map/all_to_all | solution.py:21
  22.8 0.9 copy.80
  23.7 0.2 copy.75
  23.9 0.7 reshape.474
  24.8 2.2 copy.74
  27.2 0.7 convert_reduce_fusion.2
  27.8 89.7 %all_gather.9 = bf16[256,1536]{1,0:T(8,128)(2,1)S(1)} all-gather(bf16[256,384]{1,0:T(8,128)(2,1)} %reshape.474), channel_id=1, replica_groups=mesh['g'=4,'y'=4,'x'=4,'c'=2,'m'=4] {'m'}, dimensions={1}, use_global_device_ids=true | all-gather | bytes 983040 | tf_op jit(solution)/shard_map/all_gather | solution.py:101
  117.5 0.5 all-gather.3.cloned.1.call-done
  118.0 0.7 slice_convert_fusion.3
  118.9 2.9 %fusion.96 = (bf16[1,256,320]{2,1,0:T(8,128)(2,1)}, bf16[1,256,320]{2,1,0:T(8,128)(2,1)}, bf16[1,256,320]{2,1,0:T(8,128)(2,1)}, bf16[1,256,320]{2,1,0:T(8,128)(2...) fusion(bf16[4,264,640]{2,1,0:T(8,128)(2,1)} %bitcast.92), kind=kLoop, calls=%fused_computation.205 | loop fusion | bytes 2621440 | tf_op jit(solution)/shard_map/slice | solution.py:130
  121.8 1.7 copy.94
  123.5 1.7 copy.93
  125.2 1.7 copy.92
  126.9 1.7 copy.91
  128.6 2.1 concatenate.52
  130.7 1.4 convert_reduce_fusion
  132.2 1.0 copy-done.2
  133.3 0.5 fusion.15
  133.9 0.5 fusion.14
  134.5 0.3 convolution_convert_fusion.1
  134.8 0.9 copy.81
  135.8 8.1 %all-to-all-start.1 = ((bf16[32,8,704]{2,1,0:T(8,128)(2,1)}), bf16[32,8,704]{2,1,0:T(8,128)(2,1)S(1)}, u32[]{:S(2)}, u32[]{:S(2)}) async-start(bf16[32,8,704]{2,1,0:T(8,128)(2,1)} %bitcast.10), calls=%async_computation.1 | async-start | bytes 786432 | tf_op jit(solution)/shard_map/all_to_all | solution.py:21
  143.9 2.5 fusion.2
  146.4 1.1 convolution_add_fusion
  147.5 6.5 %all-to-all-done.1 = bf16[32,8,704]{2,1,0:T(8,128)(2,1)S(1)} async-done(((bf16[32,8,704]{2,1,0:T(8,128)(2,1)}), bf16[32,8,704]{2,1,0:T(8,128)(2,1)S(1)}, u32[]{:S(2)}, u32[]{:S(2)}) %all-to-all-start.1) | async-done | bytes 360480 | tf_op jit(solution)/shard_map/all_to_all | solution.py:21
  154.0 0.4 fusion.20
  154.6 12.7 %psum.14 = f32[6,256]{1,0:T(8,128)S(1)} all-reduce(f32[6,256]{1,0:T(8,128)S(1)} %stack.52), channel_id=1, replica_groups=mesh['g'=4,'y'=4,'x'=4,'c'=2,'m'=4] {'m'}, use_global_device_ids=true, to_apply=%region_8.9 | all-reduce | flops 1536 | bytes 12288 | tf_op jit(solution)/shard_map/psum | solution.py:150
  167.5 1.0 copy-done.21
  168.5 3.5 %fusion.9 = (f32[256]{0:T(256)S(1)}, f32[1280]{0:T(1024)S(1)}, f32[256]{0:T(256)S(1)}, bf16[1280,256]{1,0:T(8,128)(2,1)}) fusion(f32[1280]{0:T(1024)S(1)} %add.316, f32[256]{0:T(256)S(1)} %get-tuple-element.84, f32[256]{0:T(256)S(1)} %get-tuple-element.83, bf16[256,320]{0,1:T(8,128)(2,1)S(1)} %bitcast.96, bf16[256,320]{0,1:T(8,128)(2,1)} %bitcast.98, ...), kind=kOutput, calls=%fused_computation.16 | convolution fusion | flops 471267584 | bytes 3848192 | tf_op jit(solution)/shard_map/dot_general | solution.py:29
  172.0 0.2 fusion.17
  172.2 0.7 concatenate.57
  173.1 0.2 copy.86
  173.3 0.4 convolution_convert_fusion
  173.9 1.5 copy.87
  175.3 4.5 %collective-permute-start = (bf16[648,704]{1,0:T(8,128)(2,1)}, bf16[648,704]{1,0:T(8,128)(2,1)S(1)}, u32[]{:S(2)}, u32[]{:S(2)}) collective-permute-start(bf16[648,704]{1,0:T(8,128)(2,1)} %copy.87), channel_id=1, source_target_pairs={{0,4},{4,0},{1,5},{5,1},{2,6},{6,2},{3,7},{7,3},{8,12},{12,8},{9,1... | collective-permute-start | bytes 2737160 | tf_op jit(solution)/shard_map/ppermute | solution.py:17
  179.8 0.4 fusion.26
  180.3 1.7 collective-permute-done
  182.0 1.0 copy-done.1
  183.3 0.9 slice-done
  184.2 1.3 copy.95
  185.5 2.3 add_convert_fusion
  187.8 1.6 copy.89
  189.5 20.9 %all_to_all.30 = bf16[16,48,704]{2,1,0:T(8,128)(2,1)S(1)} all-to-all(bf16[16,48,704]{2,1,0:T(8,128)(2,1)S(1)} %pad_maximum_fusion.3), channel_id=1, replica_groups=mesh['g'=4,'y'=4,'x'=4,'c'=2,'m'=4] {'y','x'}, dimensions={0} | all-to-all | bytes 2162688 | tf_op jit(solution)/shard_map/all_to_all | solution.py:21
  210.4 0.1 reshape.494
  210.9 0.1 slice_reduce_fusion
  211.1 0.7 pad_maximum_fusion.7
  211.8 3.3 %all-to-all-start.3 = ((bf16[4,18,704]{2,1,0:T(8,128)(2,1)}), bf16[4,18,704]{2,1,0:T(8,128)(2,1)S(1)}, u32[]{:S(2)}, u32[]{:S(2)}) async-start(bf16[4,18,704]{2,1,0:T(8,128)(2,1)} %pad_maximum_fusion.7), calls=%async_computation.4 | async-start | bytes 294912 | tf_op jit(solution)/shard_map/all_to_all | solution.py:21
  215.2 1.3 dynamic-slice
  217.1 2.8 %all-to-all-done.3 = bf16[4,18,704]{2,1,0:T(8,128)(2,1)S(1)} async-done(((bf16[4,18,704]{2,1,0:T(8,128)(2,1)}), bf16[4,18,704]{2,1,0:T(8,128)(2,1)S(1)}, u32[]{:S(2)}, u32[]{:S(2)}) %all-to-all-start.3) | async-done | bytes 101408 | tf_op jit(solution)/shard_map/all_to_all | solution.py:21
  220.3 0.6 slice.229
  221.6 0.6 slice.231
  222.2 0.6 slice.233
  222.8 19.1 %all-reduce.6 = (f32[2,256]{1,0:T(2,128)S(1)}, f32[1280]{0:T(1024)S(1)}) all-reduce(f32[2,256]{1,0:T(2,128)S(1)} %pad_maximum_fusion.10, f32[1280]{0:T(1024)S(1)} %slice.235), channel_id=1, replica_groups=mesh['g'=4,'y'=4,'x'=4,'c'=2,'m'=4] {'m'}, use_global_device_ids=true, to_apply=%region_15.16 | all-reduce | flops 1792 | bytes 14336 | tf_op jit(solution)/shard_map/psum | solution.py:190
  241.8 0.7 dynamic-slice_multiply_fusion
  242.5 0.6 slice_multiply_fusion.1
  243.1 0.6 slice_multiply_fusion
  243.6 18.6 %reduce-scatter.2.cloned.1.call-done = bf16[320,256]{1,0:T(8,128)(2,1)} async-done(((bf16[1280,256]{1,0:T(8,128)(2,1)}), bf16[320,256]{1,0:T(8,128)(2,1)}) %reduce-scatter.2.cloned.1.call-update) | async-done | bytes 163856 | tf_op jit(solution)/shard_map/reduce_scatter | solution.py:169
  262.2 1.7 copy_bitcast_fusion.1
  (103 shorter events, 2.9 us)
Async XLA Ops:
  7.2 1.0 copy-start
  7.2 110.8 %all-gather.3.cloned.1.call-start = ((), (), s32[]{:S(2)}) async-start(), calls=%async_computation.6 | async-start | bytes 1689600 | tf_op jit(solution)/shard_map/all_gather | solution.py:98
  9.2 1.2 copy-start.14
  9.2 1.2 copy-start.15
  11.9 10.7 %copy-start.12 = (bf16[64,4,320]{2,1,0:T(4,128)(2,1)S(1)}, bf16[64,4,320]{2,1,0:T(4,128)(2,1)}, u32[]{:S(2)}) copy-start(bf16[64,4,320]{2,1,0:T(4,128)(2,1)} %param.18) | copy-start | bytes 491524
  11.9 120.2 %all-to-all-start = ((bf16[32,88,384]{2,1,0:T(8,128)(2,1)}), bf16[32,88,384]{2,1,0:T(8,128)(2,1)S(1)}, u32[]{:S(2)}, u32[]{:S(2)}) async-start(bf16[32,88,384]{2,1,0:T(8,128)(2,1)} %tile.2), calls=%async_computation | async-start | bytes 4325376 | tf_op jit(solution)/shard_map/all_to_all | solution.py:21
  22.6 1.0 copy-start.13
  22.7 1.2 copy-start.11
  22.8 1.9 copy-start.22
  23.9 3.2 %copy-start.17 = (f32[320]{0:T(512)S(1)}, f32[320]{0:T(512)}, u32[]{:S(2)}) copy-start(f32[320]{0:T(512)} %param.27) | copy-start | bytes 3844
  23.9 3.2 %copy-start.18 = (f32[384]{0:T(512)S(1)}, f32[384]{0:T(512)}, u32[]{:S(2)}) copy-start(f32[384]{0:T(512)} %param.25) | copy-start | bytes 4612
  23.9 3.3 %copy-start.19 = (s32[2]{0:T(128)S(1)}, s32[2]{0:T(128)}, u32[]{:S(2)}) copy-start(s32[2]{0:T(128)} %param.21) | copy-start | bytes 28
  132.1 1.1 copy-start.2
  132.1 1.2 copy-start.3
  134.4 9.4 %copy-start.5 = (bf16[1,256,320]{1,2,0:T(8,128)(2,1)S(1)}, bf16[1,256,320]{1,2,0:T(8,128)(2,1)}, u32[]{:S(2)}) copy-start(bf16[1,256,320]{1,2,0:T(8,128)(2,1)} %copy.94) | copy-start | bytes 491524
  134.5 9.4 %copy-start.6 = (bf16[1,256,320]{1,2,0:T(8,128)(2,1)S(1)}, bf16[1,256,320]{1,2,0:T(8,128)(2,1)}, u32[]{:S(2)}) copy-start(bf16[1,256,320]{1,2,0:T(8,128)(2,1)} %copy.93) | copy-start | bytes 491524
  134.5 9.4 %copy-start.7 = (bf16[1,256,320]{1,2,0:T(8,128)(2,1)S(1)}, bf16[1,256,320]{1,2,0:T(8,128)(2,1)}, u32[]{:S(2)}) copy-start(bf16[1,256,320]{1,2,0:T(8,128)(2,1)} %copy.92) | copy-start | bytes 491524
  134.5 9.4 %copy-start.8 = (bf16[1,256,320]{1,2,0:T(8,128)(2,1)S(1)}, bf16[1,256,320]{1,2,0:T(8,128)(2,1)}, u32[]{:S(2)}) copy-start(bf16[1,256,320]{1,2,0:T(8,128)(2,1)} %copy.91) | copy-start | bytes 491524
  135.8 18.3 %all-to-all-start.1 = ((bf16[32,8,704]{2,1,0:T(8,128)(2,1)}), bf16[32,8,704]{2,1,0:T(8,128)(2,1)S(1)}, u32[]{:S(2)}, u32[]{:S(2)}) async-start(bf16[32,8,704]{2,1,0:T(8,128)(2,1)} %bitcast.10), calls=%async_computation.1 | async-start | bytes 786432 | tf_op jit(solution)/shard_map/all_to_all | solution.py:21
  143.9 2.5 copy-start.4
  143.9 2.5 copy-start.20
  167.3 1.2 copy-start.21
  168.5 4.8 %copy-start.9 = (bf16[256,1280]{1,0:T(8,128)(2,1)S(1)}, bf16[256,1280]{1,0:T(8,128)(2,1)}, u32[]{:S(2)}) copy-start(bf16[256,1280]{1,0:T(8,128)(2,1)} %fusion.2) | copy-start | bytes 1966084
  173.8 6.0 %copy-start.10 = (bf16[256,1280]{1,0:T(8,128)(2,1)S(1)}, bf16[256,1280]{1,0:T(8,128)(2,1)}, u32[]{:S(2)}) copy-start(bf16[256,1280]{1,0:T(8,128)(2,1)} %fusion.2) | copy-start | bytes 1966084
  175.3 6.7 %collective-permute-start = (bf16[648,704]{1,0:T(8,128)(2,1)}, bf16[648,704]{1,0:T(8,128)(2,1)S(1)}, u32[]{:S(2)}, u32[]{:S(2)}) collective-permute-start(bf16[648,704]{1,0:T(8,128)(2,1)} %copy.87), channel_id=1, source_target_pairs={{0,4},{4,0},{1,5},{5,1},{2,6},{6,2},{3,7},{7,3},{8,12},{12,8},{9,1... | collective-permute-start | bytes 2737160 | tf_op jit(solution)/shard_map/ppermute | solution.py:17
  182.0 1.0 copy-start.1
  183.0 1.2 slice-start
  211.0 51.2 %copy-start.16 = (f32[320]{0:T(512)S(1)}, f32[320]{0:T(512)}, u32[]{:S(2)}) copy-start(f32[320]{0:T(512)} %param.23) | copy-start | bytes 3844
  211.8 8.1 %all-to-all-start.3 = ((bf16[4,18,704]{2,1,0:T(8,128)(2,1)}), bf16[4,18,704]{2,1,0:T(8,128)(2,1)S(1)}, u32[]{:S(2)}, u32[]{:S(2)}) async-start(bf16[4,18,704]{2,1,0:T(8,128)(2,1)} %pad_maximum_fusion.7), calls=%async_computation.4 | async-start | bytes 294912 | tf_op jit(solution)/shard_map/all_to_all | solution.py:21
  215.1 47.1 %reduce-scatter.2.cloned.1.call-start = ((), (), s32[]{:S(2)}) async-start(), calls=%async_computation.5 | async-start | bytes 819200 | tf_op jit(solution)/shard_map/reduce_scatter | solution.py:169
Sparse Core Ops, SparseCore 0:
  10.5 107.4 all-gather.2
  218.8 43.3 reduce-scatter.1

commit v3 on v2

--- a/solution.py
+++ b/solution.py
@@ -91,24 +91,25 @@
     peers = slots // own_slots
     kd, ks = dino_out_proj.shape[0], sam_out_proj.shape[0]
 
-    gain_terms = jnp.pad(jnp.stack(split(norm_gain, 3)), ((0, 5), (0, ws)))
-    sam_student = jnp.concatenate(
-        [sam_context.reshape(rows, ws), student_stream.reshape(rows, wf)], axis=1
-    )
-    sam_student = lax.all_gather(
-        jnp.concatenate([sam_student, gain_terms], axis=0), "m", axis=0, tiled=False
-    )
-    dino_full = lax.all_gather(dino_context.reshape(rows, wd), "m", axis=1, tiled=True)
+    context = jnp.concatenate(
+        [dino_context.reshape(rows, wd), sam_context.reshape(rows, ws)], axis=1
+    )
+    context, student_stream, dino_out_proj, sam_out_proj, norm_gain = lax.optimization_barrier(
+        (context, student_stream, dino_out_proj, sam_out_proj, norm_gain)
+    )
+    context = lax.all_gather(context, "m", axis=0, tiled=False)
+    gain_terms = jnp.pad(jnp.stack(split(norm_gain, 3)), ((0, 5), (0, 0)))
+    student = jnp.concatenate([student_stream.reshape(rows, wf), gain_terms], axis=0)
+    student = lax.all_gather(student, "m", axis=1, tiled=True)
     packed = jnp.concatenate(
         [dino_out_proj, jnp.pad(sam_out_proj, ((0, 0), (0, wd - ws)))], axis=0
     )
     proj = exchange(jnp.tile(packed, (peers, 1)), DP).reshape(peers, kd + ks, wd)
-    dino_proj = proj[:, :kd].reshape(peers * kd, wd)
-    sam_proj = proj[:, kd:, :ws].reshape(peers * ks, ws)
-
-    dino_mixed = dot(dino_full, dino_proj)
-    sam_full = jnp.concatenate([sam_student[j, :rows, :ws] for j in range(4)], axis=1)
-    sam_mixed = dot(sam_full, sam_proj)
+    dino_proj = proj[:, :kd].reshape(4, wd, wd)
+    sam_proj = proj[:, kd:, :ws].reshape(4, ws, ws)
+
+    dino_mixed = sum(dot(context[j, :, :wd], dino_proj[j]) for j in range(4))
+    sam_mixed = sum(dot(context[j, :, wd:], sam_proj[j]) for j in range(4))
     dino_feat = (dino_stream.reshape(rows, wd).astype(f32) + dino_mixed).astype(bf16)
     sam_feat = (sam_stream.reshape(rows, ws).astype(f32) + sam_mixed).astype(bf16)
     feat = jnp.concatenate([dino_feat, sam_feat], axis=1)
@@ -127,9 +128,8 @@
         .astype(f32)
         .reshape(rows, 1)
     )
-    values = jnp.concatenate([sam_student[j, :rows, ws:] for j in range(4)], axis=1).astype(f32)
-    terms = sam_student[:, rows : rows + 3, :wf].astype(f32)
-    gain = (terms[:, 0] + (terms[:, 1] + terms[:, 2])).reshape(1, feats)
+    values = student[:rows].astype(f32)
+    gain = jnp.sum(student[rows:].astype(f32), axis=0, keepdims=True)
     center = jnp.sum(values, axis=1, keepdims=True) / feats
     spread = jnp.sum(values * values, axis=1, keepdims=True) / feats - center * center
     scale = lax.rsqrt(spread + eps)
@@ -185,9 +185,9 @@
     chip = jnp.concatenate(
         [chip.reshape(16, -1, wt), jnp.broadcast_to(beside[None], (16,) + beside.shape)], axis=1
     )
-    chip, row_sums = lax.optimization_barrier((chip, row_sums))
     slab = exchange(chip.reshape(-1, wt), ("y", "x")).reshape(chip.shape)
-    row_sums = lax.psum(row_sums, "m")
+    scaled = low.astype(f32).T * norm_gain[None, :]
+    slab, scaled = lax.optimization_barrier((slab, scaled))
     strip = 4 * each
     weight = jnp.sum(slab[:, :strip].astype(f32), axis=0).astype(bf16)
     vector = jnp.sum(from_rows(slab[:, strip:], length), axis=0)
@@ -200,11 +200,12 @@
     vector = jnp.sum(from_rows(share[:, each:], length), axis=0)
     factor = lax.rsqrt(vector[-1])
     weight = (factor * weight).astype(bf16)
-    gain_grad = factor * lax.psum_scatter(vector[wt:-1], "m", scatter_dimension=0, tiled=True)
+    sums = lax.psum(jnp.concatenate([row_sums.reshape(-1), vector[wt:-1]]), "m")
+    row_sums = sums[: 2 * rows].reshape(2, rows)
+    gain_grad = factor * lax.dynamic_slice_in_dim(sums, 2 * rows + m * wf, wf)
 
     own = student_stream.reshape(rows, wf).astype(f32)
     own_standard = (own - center) * scale
-    scaled = low.astype(f32).T * norm_gain[None, :]
     first_sum, second_sum = row_sums[0][:, None] / feats, row_sums[1][:, None] / feats
     stream_grad = ((scaled - first_sum - own_standard * second_sum) * scale).astype(bf16)
     return (

time: 272 us -> 252 us (0.926)
  blocking collectives: 142 us -> 83.1 us
  waiting for transfers between devices: 30.1 us -> 65.3 us
  local copies, waits for them, and re-layouts: 34.1 us -> 24.2 us
  matrix products: 9.75 us -> 15.4 us
  starting transfers between devices: 26.7 us -> 30 us
  other arithmetic: 11.8 us -> 14.8 us
    all_gather x1, blocking collectives: 89.7 us -> 59.8 us  [local(): student = lax.all_gather(student, 'm', axis=1, tiled=True)]
    all_gather x1, waiting for transfers between devices: 0.51 us -> 22.5 us  [local(): context = lax.all_gather(context, 'm', axis=0, tiled=False)]
    all_to_all x1 -> x0, blocking collectives: 20.9 us -> none  [exchange(): return lax.all_to_all(array, axis, split_axis=0, concat_axis=0, tiled=True)]
    unnamed x53 -> x64, local copies, waits for them, and re-layouts: 14.7 us -> 3.56 us
    reduce_scatter x1, waiting for transfers between devices: 18.6 us -> 27.9 us  [local(): lax.psum_scatter(partial.astype(bf16), 'm', scatter_dimension=0, tiled=True)]
    psum x1, blocking collectives: 19.1 us -> 11.4 us  [local(): sums = lax.psum(jnp.concatenate([row_sums.reshape(-1), vector[wt:-1]]), 'm')]
    dot_general x4 -> x10, matrix products: 2.52 us -> 8.48 us  [dot(): return jnp.dot(a, b, preferred_element_type=f32)]
    all_to_all x3 -> x4, starting transfers between devices: 22.1 us -> 25.4 us  [exchange(): return lax.all_to_all(array, axis, split_axis=0, concat_axis=0, tiled=True)]
  transfers between devices with their start and end apart: 6 -> 7, of which waited for: 5 -> 5; matrix products, arithmetic and copies ran while one was open for 11% -> 11% of each run, Pallas kernels for 0% -> 0%
where the time goes in v3:
time: 252 us; the launch traced here: 248 us
  blocking collectives  83.1 us (33%)
  waiting for transfers between devices  65.3 us (26%)
  starting transfers between devices  30 us (12%)
  local copies, waits for them, and re-layouts  24.2 us (10%)
  between operations  15.5 us (6%)
  matrix products  15.4 us (6%)
  other arithmetic  14.8 us (6%)
    all_gather x1, blocking collectives, local(): student = lax.all_gather(student, 'm', axis=1, tiled=True)  59.8 us
    reduce_scatter x1, waiting for transfers between devices, local(): lax.psum_scatter(partial.astype(bf16), 'm', scatter_dimension=0, tiled=True)  27.9 us
    all_to_all x4, starting transfers between devices, exchange(): return lax.all_to_all(array, axis, split_axis=0, concat_axis=0, tiled=True)  25.4 us
    all_gather x1, waiting for transfers between devices, local(): context = lax.all_gather(context, 'm', axis=0, tiled=False)  22.5 us
    all_to_all x4, waiting for transfers between devices, exchange(): return lax.all_to_all(array, axis, split_axis=0, concat_axis=0, tiled=True)  12.3 us
    psum x1, blocking collectives, local(): lax.psum(jnp.stack([jnp.sum(dino_out * dino_target, axis=1), jnp.sum(dino...  11.9 us
    psum x1, blocking collectives, local(): sums = lax.psum(jnp.concatenate([row_sums.reshape(-1), vector[wt:-1]]), 'm')  11.4 us
    dot_general x10, matrix products, dot(): return jnp.dot(a, b, preferred_element_type=f32)  8.48 us
  transfers between devices with their start and end apart: 7, of which 5 were waited for; matrix products, arithmetic and copies ran while one was open for 11% of the time, Pallas kernels for 0%

profile of v3, /device:TPU:1, one launch (start us, length us, event | category | flops | bytes accessed | tf_op | source)
XLA Modules:
  0.0 248.3 jit_solution(9452776544365273308)
XLA Ops:
  7.2 1.0 reshape.451
  8.3 1.0 reshape.450
  9.2 0.8 pad_maximum_fusion.6
  10.1 1.5 tile.2
  11.6 10.7 %all-to-all-start = ((bf16[32,88,384]{2,1,0:T(8,128)(2,1)}), bf16[32,88,384]{2,1,0:T(8,128)(2,1)S(1)}, u32[]{:S(2)}, u32[]{:S(2)}) async-start(bf16[32,88,384]{2,1,0:T(8,128)(2,1)} %tile.2), calls=%async_computation | async-start | bytes 4325376 | tf_op jit(solution)/shard_map/all_to_all | solution.py:21
  22.4 0.7 all-gather.4.cloned.1.call-update
  23.1 0.7 iota_add_fusion
  23.8 1.0 reshape.466
  24.8 0.9 copy.67
  25.7 1.7 reshape.465
  27.4 1.4 add.317
  28.8 1.3 copy.70
  30.6 59.8 %all-gather.1 = bf16[4,320,264]{1,2,0:T(8,128)(2,1)} all-gather(bf16[1,320,264]{1,2,0:T(8,128)(2,1)S(1)} %copy.65), channel_id=1, replica_groups=mesh['g'=4,'y'=4,'x'=4,'c'=2,'m'=4] {'m'}, dimensions={0}, use_global_device_ids=true | all-gather | bytes 844800 | tf_op jit(solution)/shard_map/all_gather | solution.py:103
  90.4 1.6 copy.66
  92.0 0.7 pad_maximum_fusion.9
  92.7 1.3 convert_reduce_fusion.3
  94.5 0.3 copy-done.18
  95.0 2.5 %fusion.2 = bf16[256,1280]{1,0:T(8,128)(2,1)} fusion(s32[1280]{0:T(1024)S(1)} %fusion.69, f32[1280]{0:T(1024)S(1)} %convert_reduce_fusion.1, f32[256]{0:T(256)S(1)} %get-tuple-element.92, f32[256]{0:T(256)S(1)} %get-tuple-element.91, bf16[264,1280]{0,1:T(8,128)(2,1)S(1)} %bitcast.106), kind=kOutput, calls=%fused_computation.3 | convolution fusion | flops 842465280 | bytes 1329152 | tf_op jit(solution)/shard_map/dot_general | solution.py:29
  97.5 0.9 fusion.97
  98.4 1.1 fusion.96
  99.5 22.5 %all-gather.4.cloned.1.call-done = bf16[1024,704]{1,0:T(8,128)(2,1)} async-done(((bf16[256,704]{1,0:T(8,128)(2,1)}), bf16[1024,704]{1,0:T(8,128)(2,1)}) %all-gather.4.cloned.1.call-update) | async-done | bytes 1441808 | tf_op jit(solution)/shard_map/all_gather | solution.py:100
  122.0 1.5 fusion.30
  123.5 1.3 convolution_add_fusion.6
  124.9 0.3 convolution_add_fusion.5
  125.2 0.3 fusion.16
  125.7 1.3 fusion.31
  127.3 0.3 convolution_add_fusion.2
  127.6 0.3 fusion.15
  128.0 0.4 convolution_convert_fusion.1
  128.4 0.9 copy.69
  129.3 7.5 %all-to-all-start.1 = ((bf16[32,8,704]{2,1,0:T(8,128)(2,1)}), bf16[32,8,704]{2,1,0:T(8,128)(2,1)S(1)}, u32[]{:S(2)}, u32[]{:S(2)}) async-start(bf16[32,8,704]{2,1,0:T(8,128)(2,1)} %bitcast.24), calls=%async_computation.1 | async-start | bytes 786432 | tf_op jit(solution)/shard_map/all_to_all | solution.py:21
  136.9 2.6 %convolution_add_fusion = f32[256,704]{0,1:T(8,128)S(1)} fusion(bf16[1280,320]{1,0:T(8,128)(2,1)} %copy.70, bf16[1280,384]{1,0:T(8,128)(2,1)} %param.24, f32[704]{0:T(1024)S(1)} %copy-done.24, f32[1280]{0:T(1024)S(1)} %copy-done.19, f32[256]{0:T(256)S(1)} %copy-done.23, f32[256]{0:T(256)S(1)} %copy-done.21, bf16[264,1280]{0,1:T(8,128)(2,1)S(1)} %bitcast.107), kind=kOutput, calls=%fused_computation.19 | convolution fusion | flops 466796544 | bytes 3192832 | tf_op jit(solution)/shard_map/dot_general | solution.py:25
  139.5 7.4 %all-to-all-done.1 = bf16[32,8,704]{2,1,0:T(8,128)(2,1)S(1)} async-done(((bf16[32,8,704]{2,1,0:T(8,128)(2,1)}), bf16[32,8,704]{2,1,0:T(8,128)(2,1)S(1)}, u32[]{:S(2)}, u32[]{:S(2)}) %all-to-all-start.1) | async-done | bytes 360480 | tf_op jit(solution)/shard_map/all_to_all | solution.py:21
  147.0 0.4 fusion.23
  147.6 11.9 %psum.14 = f32[6,256]{1,0:T(8,128)S(1)} all-reduce(f32[6,256]{1,0:T(8,128)S(1)} %stack.52), channel_id=1, replica_groups=mesh['g'=4,'y'=4,'x'=4,'c'=2,'m'=4] {'m'}, use_global_device_ids=true, to_apply=%region_9.10 | all-reduce | flops 1536 | bytes 12288 | tf_op jit(solution)/shard_map/psum | solution.py:150
  159.6 1.0 subtract_multiply_fusion.1
  160.6 1.1 subtract_multiply_fusion
  161.9 3.2 %fusion.9 = (f32[256]{0:T(256)S(1)}, f32[1280]{0:T(1024)S(1)}, f32[256]{0:T(256)S(1)}, bf16[1280,256]{1,0:T(8,128)(2,1)}) fusion(f32[1280]{0:T(1024)S(1)} %copy-done.19, f32[256]{0:T(256)S(1)} %copy-done.23, f32[256]{0:T(256)S(1)} %copy-done.21, bf16[264,1280]{0,1:T(8,128)(2,1)S(1)} %bitcast.108, f32[256,320]{0,1:T(8,128)S(1)} %subtract_multiply_fusion.1, ...), kind=kOutput, calls=%fused_computation.16 | convolution fusion | flops 468973824 | bytes 3848192 | tf_op jit(solution)/shard_map/dot_general | solution.py:29
  165.1 0.8 concatenate.52
  166.2 0.4 convolution_convert_fusion
  166.8 1.5 copy.72
  168.3 4.5 %collective-permute-start = (bf16[648,704]{1,0:T(8,128)(2,1)}, bf16[648,704]{1,0:T(8,128)(2,1)}, u32[]{:S(2)}, u32[]{:S(2)}) collective-permute-start(bf16[648,704]{1,0:T(8,128)(2,1)} %copy.72), channel_id=1, source_target_pairs={{0,4},{4,0},{1,5},{5,1},{2,6},{6,2},{3,7},{7,3},{8,12},{12,8},{9,1... | collective-permute-start | bytes 2737160 | tf_op jit(solution)/shard_map/ppermute | solution.py:17
  172.8 0.4 fusion.26
  173.2 1.9 collective-permute-done
  175.1 0.7 slice_convert_fusion.2
  176.2 1.3 slice.259
  177.4 1.3 copy.76
  178.8 1.3 add_convert_fusion
  180.1 1.0 copy.74
  181.1 1.1 pad_maximum_fusion.3
  182.3 3.8 %all-to-all-start.2 = ((bf16[16,48,704]{2,1,0:T(8,128)(2,1)}), bf16[16,48,704]{2,1,0:T(8,128)(2,1)S(1)}, u32[]{:S(2)}, u32[]{:S(2)}) async-start(bf16[16,48,704]{2,1,0:T(8,128)(2,1)} %pad_maximum_fusion.3), calls=%async_computation.2 | async-start | bytes 2359296 | tf_op jit(solution)/shard_map/all_to_all | solution.py:21
  186.1 27.9 %reduce-scatter.2.cloned.1.call-done = bf16[320,256]{1,0:T(8,128)(2,1)} async-done(((bf16[1280,256]{1,0:T(8,128)(2,1)}), bf16[320,256]{1,0:T(8,128)(2,1)}) %reduce-scatter.2.cloned.1.call-update) | async-done | bytes 163856 | tf_op jit(solution)/shard_map/reduce_scatter | solution.py:169
  214.0 1.0 multiply_bitcast_fusion
  215.7 0.7 pad_maximum_fusion.7
  216.4 3.3 %all-to-all-start.3 = ((bf16[4,18,704]{2,1,0:T(8,128)(2,1)}), bf16[4,18,704]{2,1,0:T(8,128)(2,1)S(1)}, u32[]{:S(2)}, u32[]{:S(2)}) async-start(bf16[4,18,704]{2,1,0:T(8,128)(2,1)} %pad_maximum_fusion.7), calls=%async_computation.4 | async-start | bytes 294912 | tf_op jit(solution)/shard_map/all_to_all | solution.py:21
  219.8 4.9 %all-to-all-done.3 = bf16[4,18,704]{2,1,0:T(8,128)(2,1)S(1)} async-done(((bf16[4,18,704]{2,1,0:T(8,128)(2,1)}), bf16[4,18,704]{2,1,0:T(8,128)(2,1)S(1)}, u32[]{:S(2)}, u32[]{:S(2)}) %all-to-all-start.3) | async-done | bytes 101408 | tf_op jit(solution)/shard_map/all_to_all | solution.py:21
  225.0 0.6 slice.271
  226.2 0.6 slice_multiply_fusion.1
  226.9 0.6 slice.273
  227.5 0.6 slice.275
  228.1 0.6 slice_multiply_fusion
  228.7 11.4 %psum.15 = f32[1792]{0:T(1024)S(1)} all-reduce(f32[1792]{0:T(1024)S(1)} %pad_maximum_fusion.8), channel_id=1, replica_groups=mesh['g'=4,'y'=4,'x'=4,'c'=2,'m'=4] {'m'}, use_global_device_ids=true, to_apply=%region_19.20 | all-reduce | flops 1792 | bytes 14336 | tf_op jit(solution)/shard_map/psum | solution.py:203
  240.1 0.7 dynamic-slice_multiply_fusion
  240.7 0.8 copy_bitcast_fusion.1
  (118 shorter events, 4.0 us)
Async XLA Ops:
  7.2 23.2 %copy-start = (bf16[2,128,320]{1,2,0:T(8,128)(2,1)S(1)}, bf16[2,128,320]{1,2,0:T(8,128)(2,1)}, u32[]{:S(2)}) copy-start(bf16[2,128,320]{1,2,0:T(8,128)(2,1)} %param.22) | copy-start | bytes 491524
  7.2 2.9 %copy-start.13 = (bf16[48,384]{1,0:T(8,128)(2,1)S(1)}, bf16[48,384]{1,0:T(8,128)(2,1)}, u32[]{:S(2)}) copy-start(bf16[48,384]{1,0:T(8,128)(2,1)} %param.16) | copy-start | bytes 110596
  7.2 2.8 %copy-start.14 = (bf16[40,320]{1,0:T(8,128)(2,1)S(1)}, bf16[40,320]{1,0:T(8,128)(2,1)}, u32[]{:S(2)}) copy-start(bf16[40,320]{1,0:T(8,128)(2,1)} %param.19) | copy-start | bytes 76804
  11.6 11.5 %copy-start.29 = (s32[1,64]{1,0:T(1,128)S(1)}, s32[1,64]{1,0:T(1,128)}, u32[]{:S(2)}) copy-start(s32[1,64]{1,0:T(1,128)} %param.20) | copy-start | bytes 772
  11.6 85.9 %all-to-all-start = ((bf16[32,88,384]{2,1,0:T(8,128)(2,1)}), bf16[32,88,384]{2,1,0:T(8,128)(2,1)S(1)}, u32[]{:S(2)}, u32[]{:S(2)}) async-start(bf16[32,88,384]{2,1,0:T(8,128)(2,1)} %tile.2), calls=%async_computation | async-start | bytes 4325376 | tf_op jit(solution)/shard_map/all_to_all | solution.py:21
  22.3 6.5 %copy-start.11 = (bf16[1280,320]{0,1:T(8,128)(2,1)S(1)}, bf16[1280,320]{0,1:T(8,128)(2,1)}, u32[]{:S(2)}) copy-start(bf16[1280,320]{0,1:T(8,128)(2,1)} %param.26) | copy-start | bytes 2457604
  22.3 99.7 %all-gather.4.cloned.1.call-start = ((), (), s32[]{:S(2)}) async-start(), calls=%async_computation.6 | async-start | bytes 1966080 | tf_op jit(solution)/shard_map/all_gather | solution.py:100
  24.8 5.3 %copy-start.16 = (f32[320]{0:T(512)S(1)}, f32[320]{0:T(512)}, u32[]{:S(2)}) copy-start(f32[320]{0:T(512)} %param.23) | copy-start | bytes 3844
  30.4 61.6 %copy-start.25 = (f32[320]{0:T(512)S(1)}, f32[320]{0:T(512)}, u32[]{:S(2)}) copy-start(f32[320]{0:T(512)} %param.27) | copy-start | bytes 3844
  30.4 61.6 %copy-start.26 = (f32[384]{0:T(512)S(1)}, f32[384]{0:T(512)}, u32[]{:S(2)}) copy-start(f32[384]{0:T(512)} %param.25) | copy-start | bytes 4612
  30.4 62.3 %copy-start.28 = (s32[2]{0:T(128)S(1)}, s32[2]{0:T(128)}, u32[]{:S(2)}) copy-start(s32[2]{0:T(128)} %param.21) | copy-start | bytes 28
  92.0 44.9 %copy-start.1 = (bf16[4,320,264]{2,1,0:T(8,128)(2,1)}, bf16[4,320,264]{2,1,0:T(8,128)(2,1)S(1)}, u32[]{:S(2)}) copy-start(bf16[4,320,264]{2,1,0:T(8,128)(2,1)S(1)} %copy.66) | copy-start | bytes 2027524
  94.2 0.6 copy-start.18
  94.4 0.6 copy-start.20
  94.4 0.6 copy-start.22
  99.5 25.4 %copy-start.10 = (bf16[8,40,320]{2,1,0:T(8,128)(2,1)S(1)}, bf16[8,40,320]{2,1,0:T(8,128)(2,1)}, u32[]{:S(2)}) copy-start(bf16[8,40,320]{2,1,0:T(8,128)(2,1)} %get-tuple-element.70) | copy-start | bytes 614404
  122.0 2.8 %copy-start.5 = (bf16[1024,704]{1,0:T(8,128)(2,1)S(1)}, bf16[1024,704]{1,0:T(8,128)(2,1)}, u32[]{:S(2)}) copy-start(bf16[1024,704]{1,0:T(8,128)(2,1)} %all-gather.4.cloned.1.call-done) | copy-start | bytes 4325380
  122.0 3.2 %copy-start.6 = (f32[256,320]{0,1:T(8,128)S(1)}, f32[256,320]{0,1:T(8,128)}, u32[]{:S(2)}) copy-start(f32[256,320]{0,1:T(8,128)} %copy.67) | copy-start | bytes 983044
  125.2 1.8 copy-start.8
  125.7 1.6 copy-start.7
  125.7 1.9 copy-start.4
  125.7 1.9 copy-start.9
  127.3 0.7 copy-start.27
  128.0 8.9 %copy-start.19 = (f32[1280]{0:T(1024)S(1)}, f32[1280]{0:T(1024)}, u32[]{:S(2)}) copy-start(f32[1280]{0:T(1024)} %copy-done.18) | copy-start | bytes 15364
  128.0 8.9 %copy-start.21 = (f32[256]{0:T(256)S(1)}, f32[256]{0:T(256)}, u32[]{:S(2)}) copy-start(f32[256]{0:T(256)} %copy-done.20) | copy-start | bytes 3076
  128.0 8.9 %copy-start.23 = (f32[256]{0:T(256)S(1)}, f32[256]{0:T(256)}, u32[]{:S(2)}) copy-start(f32[256]{0:T(256)} %copy-done.22) | copy-start | bytes 3076
  128.0 8.9 %copy-start.24 = (f32[704]{0:T(1024)S(1)}, f32[704]{0:T(1024)}, u32[]{:S(2)}) copy-start(f32[704]{0:T(1024)} %pad_maximum_fusion.9) | copy-start | bytes 8452
  129.3 17.7 %all-to-all-start.1 = ((bf16[32,8,704]{2,1,0:T(8,128)(2,1)}), bf16[32,8,704]{2,1,0:T(8,128)(2,1)S(1)}, u32[]{:S(2)}, u32[]{:S(2)}) async-start(bf16[32,8,704]{2,1,0:T(8,128)(2,1)} %bitcast.24), calls=%async_computation.1 | async-start | bytes 786432 | tf_op jit(solution)/shard_map/all_to_all | solution.py:21
  136.8 77.2 %reduce-scatter.2.cloned.1.call-start = ((), (), s32[]{:S(2)}) async-start(), calls=%async_computation.5 | async-start | bytes 819200 | tf_op jit(solution)/shard_map/reduce_scatter | solution.py:169
  139.5 7.9 %copy-start.3 = (f32[256,704]{0,1:T(8,128)}, f32[256,704]{0,1:T(8,128)S(1)}, u32[]{:S(2)}) copy-start(f32[256,704]{0,1:T(8,128)S(1)} %convolution_add_fusion) | copy-start | bytes 2162692
  139.5 20.0 %copy-start.15 = (f32[256]{0:T(256)S(1)}, f32[256]{0:T(256)}, u32[]{:S(2)}) copy-start(f32[256]{0:T(256)} %get-tuple-element.94) | copy-start | bytes 3076
  147.5 14.3 %copy-start.2 = (bf16[4,320,264]{2,1,0:T(8,128)(2,1)S(1)}, bf16[4,320,264]{2,1,0:T(8,128)(2,1)}, u32[]{:S(2)}) copy-start(bf16[4,320,264]{2,1,0:T(8,128)(2,1)} %copy-done.1) | copy-start | bytes 2027524
  161.9 4.3 %copy-start.12 = (bf16[256,1280]{1,0:T(8,128)(2,1)S(1)}, bf16[256,1280]{1,0:T(8,128)(2,1)}, u32[]{:S(2)}) copy-start(bf16[256,1280]{1,0:T(8,128)(2,1)} %fusion.2) | copy-start | bytes 1966084
  168.3 6.8 %collective-permute-start = (bf16[648,704]{1,0:T(8,128)(2,1)}, bf16[648,704]{1,0:T(8,128)(2,1)}, u32[]{:S(2)}, u32[]{:S(2)}) collective-permute-start(bf16[648,704]{1,0:T(8,128)(2,1)} %copy.72), channel_id=1, source_target_pairs={{0,4},{4,0},{1,5},{5,1},{2,6},{6,2},{3,7},{7,3},{8,12},{12,8},{9,1... | collective-permute-start | bytes 2737160 | tf_op jit(solution)/shard_map/ppermute | solution.py:17
  182.3 31.7 %copy-start.17 = (f32[320]{0:T(512)S(1)}, f32[320]{0:T(512)}, u32[]{:S(2)}) copy-start(f32[320]{0:T(512)} %param.23) | copy-start | bytes 3844
  182.3 32.8 %all-to-all-start.2 = ((bf16[16,48,704]{2,1,0:T(8,128)(2,1)}), bf16[16,48,704]{2,1,0:T(8,128)(2,1)S(1)}, u32[]{:S(2)}, u32[]{:S(2)}) async-start(bf16[16,48,704]{2,1,0:T(8,128)(2,1)} %pad_maximum_fusion.3), calls=%async_computation.2 | async-start | bytes 2359296 | tf_op jit(solution)/shard_map/all_to_all | solution.py:21
  216.4 8.2 %all-to-all-start.3 = ((bf16[4,18,704]{2,1,0:T(8,128)(2,1)}), bf16[4,18,704]{2,1,0:T(8,128)(2,1)S(1)}, u32[]{:S(2)}, u32[]{:S(2)}) async-start(bf16[4,18,704]{2,1,0:T(8,128)(2,1)} %pad_maximum_fusion.7), calls=%async_computation.4 | async-start | bytes 294912 | tf_op jit(solution)/shard_map/all_to_all | solution.py:21
Sparse Core Ops, SparseCore 0:
  25.3 96.7 all-gather.3
  172.9 41.0 reduce-scatter.1

commit v4 on v2

--- a/solution.py
+++ b/solution.py
@@ -13,8 +13,8 @@
 DP = ("y", "x", "c")
 
 
-def swap(array):
-    return lax.ppermute(array, "c", [(0, 1), (1, 0)])
+def shift_m(array, by):
+    return lax.ppermute(array, "m", [(i, (i + by) % 4) for i in range(4)])
 
 
 def exchange(array, axis):
@@ -81,7 +81,7 @@
     adapt_sam,
     adapt_sam_bias,
 ):
-    m, c = lax.axis_index("m"), lax.axis_index("c")
+    m = lax.axis_index("m")
     slots, per_peer, wd = dino_context.shape
     ws = sam_context.shape[2]
     rows = slots * per_peer
@@ -91,14 +91,8 @@
     peers = slots // own_slots
     kd, ks = dino_out_proj.shape[0], sam_out_proj.shape[0]
 
-    gain_terms = jnp.pad(jnp.stack(split(norm_gain, 3)), ((0, 5), (0, ws)))
-    sam_student = jnp.concatenate(
-        [sam_context.reshape(rows, ws), student_stream.reshape(rows, wf)], axis=1
-    )
-    sam_student = lax.all_gather(
-        jnp.concatenate([sam_student, gain_terms], axis=0), "m", axis=0, tiled=False
-    )
     dino_full = lax.all_gather(dino_context.reshape(rows, wd), "m", axis=1, tiled=True)
+    sam_full = lax.all_gather(sam_context.reshape(rows, ws), "m", axis=1, tiled=True)
     packed = jnp.concatenate(
         [dino_out_proj, jnp.pad(sam_out_proj, ((0, 0), (0, wd - ws)))], axis=0
     )
@@ -107,7 +101,6 @@
     sam_proj = proj[:, kd:, :ws].reshape(peers * ks, ws)
 
     dino_mixed = dot(dino_full, dino_proj)
-    sam_full = jnp.concatenate([sam_student[j, :rows, :ws] for j in range(4)], axis=1)
     sam_mixed = dot(sam_full, sam_proj)
     dino_feat = (dino_stream.reshape(rows, wd).astype(f32) + dino_mixed).astype(bf16)
     sam_feat = (sam_stream.reshape(rows, ws).astype(f32) + sam_mixed).astype(bf16)
@@ -115,7 +108,12 @@
     image_row = jnp.arange(per_peer, dtype=jnp.int32)[None, :]
     goes_to = (owners[0][:, None] * per_peer + image_row).reshape(-1)
     sent = dot_rows(one_hot(goes_to, rows), feat).astype(bf16)
+    gain_terms = jnp.pad(jnp.stack(split(norm_gain, 3)), ((0, 5), (0, 0)))
+    student = jnp.concatenate([student_stream.reshape(rows, wf), gain_terms], axis=0)
+    sent, student = lax.optimization_barrier((sent, student))
     arrived = exchange(sent, DP)
+    student = lax.all_gather(student, "m", axis=1, tiled=True)
+    arrived, student = lax.optimization_barrier((arrived, student))
     place = jnp.arange(rows, dtype=jnp.int32)
     slot, row = place // window, place % window
     source = (row // per_peer) * (own_slots * per_peer) + slot * per_peer + row % per_peer
@@ -127,9 +125,8 @@
         .astype(f32)
         .reshape(rows, 1)
     )
-    values = jnp.concatenate([sam_student[j, :rows, ws:] for j in range(4)], axis=1).astype(f32)
-    terms = sam_student[:, rows : rows + 3, :wf].astype(f32)
-    gain = (terms[:, 0] + (terms[:, 1] + terms[:, 2])).reshape(1, feats)
+    values = student[:rows].astype(f32)
+    gain = jnp.sum(student[rows:].astype(f32), axis=0, keepdims=True)
     center = jnp.sum(values, axis=1, keepdims=True) / feats
     spread = jnp.sum(values * values, axis=1, keepdims=True) / feats - center * center
     scale = lax.rsqrt(spread + eps)
@@ -139,13 +136,13 @@
     out = dot(normed, adapt) + jnp.concatenate([adapt_dino_bias, adapt_sam_bias])[None, :]
     dino_out, sam_out = out[:, :wd], out[:, wd:]
     each = feats // (EXTENT["g"] * peers)
-    spot = jnp.arange(feats, dtype=jnp.int32)
-    i, rest = spot % each, spot // each
-    g_of, rest = rest % 4, rest // 4
-    x_of, rest = rest % 4, rest // 4
-    y_of, c_of = rest % 4, (rest // 4 + c) % 2
-    feature = (((g_of * 4 + y_of) * 4 + x_of) * 2 + c_of) * each + i
-    dealt = dot_last(normed, one_hot(feature, feats)).astype(bf16)
+    strip = EXTENT["g"] * each
+    block = strip + 8
+    spot = jnp.arange(peers * block, dtype=jnp.int32)
+    inside = spot % block
+    feature = (inside // each * peers + spot // block) * each + inside % each
+    dealt = dot_last(one_hot(jnp.where(inside < strip, feature, -1), feats), normed).astype(bf16)
+    dealt = jnp.concatenate([dealt, one_hot(jnp.where(inside < strip, -1, inside - strip), 16)], axis=1)
 
     stats = lax.psum(
         jnp.stack(
@@ -166,45 +163,46 @@
     back = grad.astype(bf16)
 
     partial = dot_last(adapt, back)
-    low = lax.psum_scatter(partial.astype(bf16), "m", scatter_dimension=0, tiled=True)
     scaled_part = partial * gain.T
     row_sums = jnp.stack(
         [jnp.sum(scaled_part, axis=0), jnp.sum(scaled_part * standard.T, axis=0)]
     )
     gain_part = jnp.sum(partial * standard.T, axis=1)
 
-    half = feats // 2
     length = wt + feats + 1
     vector = jnp.concatenate([jnp.sum(grad, axis=0), gain_part, jnp.sum(live).reshape(1)])
-    mine = dot_rows(dealt[:, :half], back)
-    theirs = dot_rows(dealt[:, half:], back).astype(bf16)
-    received = swap(jnp.concatenate([theirs, to_rows(vector, wt)], axis=0))
-    chip = (mine + received[:half].astype(f32)).astype(bf16)
-    vector = vector + from_rows(received[half:], length)
     beside = to_rows(vector, wt)
-    chip = jnp.concatenate(
-        [chip.reshape(16, -1, wt), jnp.broadcast_to(beside[None], (16,) + beside.shape)], axis=1
-    )
-    chip, row_sums = lax.optimization_barrier((chip, row_sums))
-    slab = exchange(chip.reshape(-1, wt), ("y", "x")).reshape(chip.shape)
-    row_sums = lax.psum(row_sums, "m")
-    strip = 4 * each
+    under = jnp.concatenate([back, jnp.pad(beside, ((0, 16 - beside.shape[0]), (0, 0)))], axis=0)
+    weight = dot(dealt, under).astype(bf16)
+    parts = partial.astype(bf16).reshape(4, wf, rows)
+    slab = exchange(weight, DP).reshape(peers, block, wt)
+    normed_grad = sum(
+        part.astype(f32)
+        for part in [lax.dynamic_index_in_dim(parts, m, 0, False)]
+        + [
+            shift_m(lax.dynamic_index_in_dim(parts, (m + by) % 4, 0, False), by)
+            for by in (2, 1, 3)
+        ]
+    )
     weight = jnp.sum(slab[:, :strip].astype(f32), axis=0).astype(bf16)
     vector = jnp.sum(from_rows(slab[:, strip:], length), axis=0)
     beside = to_rows(vector, wt)
     deal = jnp.concatenate(
         [weight.reshape(4, each, wt), jnp.broadcast_to(beside[None], (4,) + beside.shape)], axis=1
     )
+    deal, normed_grad = lax.optimization_barrier((deal, normed_grad))
     share = exchange(deal.reshape(-1, wt), "g").reshape(deal.shape)
     weight = jnp.sum(share[:, :each].astype(f32), axis=0)
     vector = jnp.sum(from_rows(share[:, each:], length), axis=0)
     factor = lax.rsqrt(vector[-1])
     weight = (factor * weight).astype(bf16)
-    gain_grad = factor * lax.psum_scatter(vector[wt:-1], "m", scatter_dimension=0, tiled=True)
+    sums = lax.psum(jnp.concatenate([row_sums.reshape(-1), vector[wt:-1]]), "m")
+    row_sums = sums[: 2 * rows].reshape(2, rows)
+    gain_grad = factor * lax.dynamic_slice_in_dim(sums, 2 * rows + m * wf, wf)
 
     own = student_stream.reshape(rows, wf).astype(f32)
     own_standard = (own - center) * scale
-    scaled = low.astype(f32).T * norm_gain[None, :]
+    scaled = normed_grad.T * norm_gain[None, :]
     first_sum, second_sum = row_sums[0][:, None] / feats, row_sums[1][:, None] / feats
     stream_grad = ((scaled - first_sum - own_standard * second_sum) * scale).astype(bf16)
     return (

time: 272 us -> 236 us (0.87)
  starting transfers between devices: 26.7 us -> 66.8 us
  blocking collectives: 142 us -> 105 us
  local copies, waits for them, and re-layouts: 34.1 us -> 19.5 us
  between operations: 16 us -> 2.02 us
  waiting for transfers between devices: 30.1 us -> 19.5 us
    all_gather x1, blocking collectives: 89.7 us -> 27.7 us  [local(): lax.all_gather(dino_context.reshape(rows, wd), 'm', axis=1, tiled=True)]
    all_gather x0 -> x2, blocking collectives: none -> 54.2 us  [the longest x1 33.1 us: local(): lax.all_gather(sam_context.reshape(rows, ws), 'm', axis=1, tiled=True)]
    all_to_all x3 -> x4, starting transfers between devices: 22.1 us -> 50.7 us  [exchange(): return lax.all_to_all(array, axis, split_axis=0, concat_axis=0, tiled=True)]
    all_to_all x1 -> x0, blocking collectives: 20.9 us -> none  [exchange(): return lax.all_to_all(array, axis, split_axis=0, concat_axis=0, tiled=True)]
    reduce_scatter x1 -> x0, waiting for transfers between devices: 18.6 us -> none  [local(): lax.psum_scatter(partial.astype(bf16), 'm', scatter_dimension=0, tiled=True)]
    ppermute x1 -> x3, waiting for transfers between devices: 1.75 us -> 14.6 us  [shift_m(): return lax.ppermute(array, 'm', [(i, (i + by) % 4) for i in range(4)])]
    ppermute x1 -> x3, starting transfers between devices: 4.46 us -> 16.2 us  [shift_m(): return lax.ppermute(array, 'm', [(i, (i + by) % 4) for i in range(4)])]
    unnamed x53 -> x63, local copies, waits for them, and re-layouts: 14.7 us -> 5.42 us
  transfers between devices with their start and end apart: 6 -> 7, of which waited for: 5 -> 4; matrix products, arithmetic and copies ran while one was open for 11% -> 5% of each run, Pallas kernels for 0% -> 0%
where the time goes in v4:
time: 236 us; the launch traced here: 233 us
  blocking collectives  105 us (44%)
  starting transfers between devices  66.8 us (28%)
  local copies, waits for them, and re-layouts  19.5 us (8%)
  waiting for transfers between devices  19.5 us (8%)
  other arithmetic  12 us (5%)
  matrix products  7.48 us (3%)
    all_to_all x4, starting transfers between devices, exchange(): return lax.all_to_all(array, axis, split_axis=0, concat_axis=0, tiled=True)  50.7 us
    all_gather x1, blocking collectives, local(): lax.all_gather(sam_context.reshape(rows, ws), 'm', axis=1, tiled=True)  33.1 us
    all_gather x1, blocking collectives, local(): lax.all_gather(dino_context.reshape(rows, wd), 'm', axis=1, tiled=True)  27.7 us
    all_gather x1, blocking collectives, local(): student = lax.all_gather(student, 'm', axis=1, tiled=True)  21.1 us
    ppermute x3, starting transfers between devices, shift_m(): return lax.ppermute(array, 'm', [(i, (i + by) % 4) for i in range(4)])  16.2 us
    ppermute x3, waiting for transfers between devices, shift_m(): return lax.ppermute(array, 'm', [(i, (i + by) % 4) for i in range(4)])  14.6 us
    psum x1, blocking collectives, local(): lax.psum(jnp.stack([jnp.sum(dino_out * dino_target, axis=1), jnp.sum(dino...  13.5 us
    psum x1, blocking collectives, local(): sums = lax.psum(jnp.concatenate([row_sums.reshape(-1), vector[wt:-1]]), 'm')  10.1 us
  transfers between devices with their start and end apart: 7, of which 4 were waited for; matrix products, arithmetic and copies ran while one was open for 5% of the time, Pallas kernels for 0%

profile of v4, /device:TPU:1, one launch (start us, length us, event | category | flops | bytes accessed | tf_op | source)
XLA Modules:
  0.0 232.8 jit_solution(12136777716719719286)
XLA Ops:
  0.6 0.8 fusion.45
  1.5 1.5 tile.2
  3.0 10.7 %all-to-all-start = ((bf16[32,88,384]{2,1,0:T(8,128)(2,1)}), bf16[32,88,384]{2,1,0:T(8,128)(2,1)S(1)}, u32[]{:S(2)}, u32[]{:S(2)}) async-start(bf16[32,88,384]{2,1,0:T(8,128)(2,1)} %tile.2), calls=%async_computation | async-start | bytes 4325376 | tf_op jit(solution)/shard_map/all_to_all | solution.py:21
  13.8 0.5 multiply_bitcast_fusion
  14.4 0.2 copy.58
  14.5 0.7 reshape.356
  15.3 0.2 copy.54
  15.7 1.0 reshape.371
  16.8 0.9 copy.56
  17.6 0.7 iota_add_fusion
  18.5 2.2 copy.62
  20.8 0.7 convert_reduce_fusion.3
  21.5 0.7 fusion.39
  22.2 33.1 %all_gather.10 = bf16[256,1280]{0,1:T(8,128)(2,1)} all-gather(bf16[256,320]{0,1:T(8,128)(2,1)S(1)} %copy.55), channel_id=1, replica_groups=mesh['g'=4,'y'=4,'x'=4,'c'=2,'m'=4] {'m'}, dimensions={1}, use_global_device_ids=true | all-gather | bytes 819200 | tf_op jit(solution)/shard_map/all_gather | solution.py:95
  55.3 27.7 %all_gather.9 = bf16[256,1536]{1,0:T(8,128)(2,1)S(1)} all-gather(bf16[256,384]{1,0:T(8,128)(2,1)S(1)} %copy-done.5), channel_id=1, replica_groups=mesh['g'=4,'y'=4,'x'=4,'c'=2,'m'=4] {'m'}, dimensions={1}, use_global_device_ids=true | all-gather | bytes 983040 | tf_op jit(solution)/shard_map/all_gather | solution.py:94
  82.9 0.6 fusion.44
  83.7 0.5 fusion.15
  84.4 1.0 copy-done.6
  85.4 0.4 fusion.16
  85.9 0.3 convolution_convert_fusion.1
  86.2 0.9 copy.59
  87.1 18.2 %all-to-all-start.1 = ((bf16[32,8,704]{2,1,0:T(8,128)(2,1)}), bf16[32,8,704]{2,1,0:T(8,128)(2,1)S(1)}, u32[]{:S(2)}, u32[]{:S(2)}) async-start(bf16[32,8,704]{2,1,0:T(8,128)(2,1)} %bitcast.5), calls=%async_computation.1 | async-start | bytes 786432 | tf_op jit(solution)/shard_map/all_to_all | solution.py:21
  105.3 0.2 copy.60
  105.5 21.1 %all-gather = bf16[4,320,264]{1,2,0:T(8,128)(2,1)S(1)} all-gather(bf16[1,320,264]{1,2,0:T(8,128)(2,1)S(1)} %copy.60), channel_id=1, replica_groups=mesh['g'=4,'y'=4,'x'=4,'c'=2,'m'=4] {'m'}, dimensions={0}, use_global_device_ids=true | all-gather | bytes 844800 | tf_op jit(solution)/shard_map/all_gather | solution.py:115
  126.6 0.7 copy.61
  127.3 0.2 convert_reduce_fusion
  127.5 0.2 convert_reduce_fusion.1
  127.7 0.4 fusion.38
  128.3 0.2 copy-done.2
  128.5 0.3 copy-done.27
  128.8 1.1 convolution_add_fusion
  130.1 13.5 %psum.14 = f32[6,256]{1,0:T(8,128)S(1)} all-reduce(f32[6,256]{1,0:T(8,128)S(1)} %stack.52), channel_id=1, replica_groups=mesh['g'=4,'y'=4,'x'=4,'c'=2,'m'=4] {'m'}, use_global_device_ids=true, to_apply=%region_9.10 | all-reduce | flops 1536 | bytes 12288 | tf_op jit(solution)/shard_map/psum | solution.py:147
  144.0 0.2 fusion.21
  144.1 0.9 copy-done.3
  145.0 0.3 copy-done.28
  145.3 1.4 fusion.9
  146.8 0.7 concatenate.46
  147.7 0.2 copy.63
  147.9 2.0 fusion.2
  149.8 1.3 convolution_convert_fusion
  151.1 2.4 %copy.64 = bf16[1536,704]{1,0:T(8,128)(2,1)} copy(bf16[1536,704]{0,1:T(8,128)(2,1)S(1)} %convolution_convert_fusion) | data formatting | bytes 4325376 | tf_op jit(solution)/shard_map/convert_element_type | solution.py:176
  153.6 10.7 %all-to-all-start.2 = ((bf16[32,48,704]{2,1,0:T(8,128)(2,1)}), bf16[32,48,704]{2,1,0:T(8,128)(2,1)S(1)}, u32[]{:S(2)}, u32[]{:S(2)}) async-start(bf16[32,48,704]{2,1,0:T(8,128)(2,1)} %bitcast.97), calls=%async_computation.2 | async-start | bytes 4718592 | tf_op jit(solution)/shard_map/all_to_all | solution.py:21
  164.4 0.8 dynamic-slice_bitcast_fusion.2
  165.1 7.0 %collective-permute-start = (bf16[320,256]{1,0:T(8,128)(2,1)}, bf16[320,256]{1,0:T(8,128)(2,1)S(1)}, u32[]{:S(2)}, u32[]{:S(2)}) collective-permute-start(bf16[320,256]{1,0:T(8,128)(2,1)} %get-tuple-element.58), channel_id=1, source_target_pairs={{0,2},{1,3},{2,0},{3,1},{4,6},{5,7},{6,4},{7,5},{8,10},{9,11},{10,... | collective-permute-start | bytes 491528 | tf_op jit(solution)/shard_map/ppermute | solution.py:17
  172.1 6.1 %collective-permute-start.1 = (bf16[320,256]{1,0:T(8,128)(2,1)}, bf16[320,256]{1,0:T(8,128)(2,1)S(1)}, u32[]{:S(2)}, u32[]{:S(2)}) collective-permute-start(bf16[320,256]{1,0:T(8,128)(2,1)} %get-tuple-element.60), channel_id=1, source_target_pairs={{0,1},{1,2},{2,3},{3,0},{4,5},{5,6},{6,7},{7,4},{8,9},{9,10},{10,1... | collective-permute-start | bytes 491528 | tf_op jit(solution)/shard_map/ppermute | solution.py:17
  178.3 3.1 %collective-permute-start.2 = (bf16[320,256]{1,0:T(8,128)(2,1)}, bf16[320,256]{1,0:T(8,128)(2,1)}, u32[]{:S(2)}, u32[]{:S(2)}) collective-permute-start(bf16[320,256]{1,0:T(8,128)(2,1)} %get-tuple-element.59), channel_id=1, source_target_pairs={{0,3},{1,0},{2,1},{3,2},{4,7},{5,4},{6,5},{7,6},{8,11},{9,8},{10,9... | collective-permute-start | bytes 491528 | tf_op jit(solution)/shard_map/ppermute | solution.py:17
  181.3 0.2 collective-permute-done
  181.5 9.8 %collective-permute-done.1 = bf16[320,256]{1,0:T(8,128)(2,1)S(1)} collective-permute-done((bf16[320,256]{1,0:T(8,128)(2,1)}, bf16[320,256]{1,0:T(8,128)(2,1)S(1)}, u32[]{:S(2)}, u32[]{:S(2)}) %collective-permute-start.1) | collective-permute-done | bytes 163872 | tf_op jit(solution)/shard_map/ppermute | solution.py:17
  191.3 4.7 %collective-permute-done.2 = bf16[320,256]{1,0:T(8,128)(2,1)} collective-permute-done((bf16[320,256]{1,0:T(8,128)(2,1)}, bf16[320,256]{1,0:T(8,128)(2,1)}, u32[]{:S(2)}, u32[]{:S(2)}) %collective-permute-start.2) | collective-permute-done | bytes 163872 | tf_op jit(solution)/shard_map/ppermute | solution.py:17
  196.0 1.7 fusion.33
  197.8 1.1 reshape.373
  198.9 1.2 fusion.37
  200.3 0.3 slice_reduce_fusion
  200.6 0.7 pad_maximum_fusion.4
  201.3 11.0 %all-to-all-start.3 = ((bf16[4,18,704]{2,1,0:T(8,128)(2,1)}), bf16[4,18,704]{2,1,0:T(8,128)(2,1)S(1)}, u32[]{:S(2)}, u32[]{:S(2)}) async-start(bf16[4,18,704]{2,1,0:T(8,128)(2,1)} %pad_maximum_fusion.4), calls=%async_computation.3 | async-start | bytes 294912 | tf_op jit(solution)/shard_map/all_to_all | solution.py:21
  212.4 4.8 %all-to-all-done.3 = bf16[4,18,704]{2,1,0:T(8,128)(2,1)S(1)} async-done(((bf16[4,18,704]{2,1,0:T(8,128)(2,1)}), bf16[4,18,704]{2,1,0:T(8,128)(2,1)S(1)}, u32[]{:S(2)}, u32[]{:S(2)}) %all-to-all-start.3) | async-done | bytes 101408 | tf_op jit(solution)/shard_map/all_to_all | solution.py:21
  217.5 0.6 slice.153
  218.8 0.6 slice_multiply_fusion
  219.4 0.6 slice_multiply_fusion.1
  220.0 0.6 slice.155
  220.6 0.6 slice.157
  221.2 10.1 %psum.15 = f32[1792]{0:T(1024)S(1)} all-reduce(f32[1792]{0:T(1024)S(1)} %pad_maximum_fusion.5), channel_id=1, replica_groups=mesh['g'=4,'y'=4,'x'=4,'c'=2,'m'=4] {'m'}, use_global_device_ids=true, to_apply=%region_18.19 | all-reduce | flops 1792 | bytes 14336 | tf_op jit(solution)/shard_map/psum | solution.py:199
  231.4 0.7 dynamic-slice_multiply_fusion
  232.0 0.8 copy_bitcast_fusion.1
  (103 shorter events, 2.3 us)
Async XLA Ops:
  0.6 20.8 %copy-start = (bf16[2,128,320]{1,2,0:T(8,128)(2,1)S(1)}, bf16[2,128,320]{1,2,0:T(8,128)(2,1)}, u32[]{:S(2)}) copy-start(bf16[2,128,320]{1,2,0:T(8,128)(2,1)} %param.22) | copy-start | bytes 491524
  3.0 10.7 %copy-start.12 = (f32[320]{0:T(512)S(1)}, f32[320]{0:T(512)}, u32[]{:S(2)}) copy-start(f32[320]{0:T(512)} %param.23) | copy-start | bytes 3844
  3.0 10.8 %copy-start.29 = (s32[1,64]{1,0:T(1,128)S(1)}, s32[1,64]{1,0:T(1,128)}, u32[]{:S(2)}) copy-start(s32[1,64]{1,0:T(1,128)} %param.20) | copy-start | bytes 772
  3.0 11.5 %copy-start.8 = (bf16[64,4,384]{2,1,0:T(4,128)(2,1)S(1)}, bf16[64,4,384]{2,1,0:T(4,128)(2,1)}, u32[]{:S(2)}) copy-start(bf16[64,4,384]{2,1,0:T(4,128)(2,1)} %param.14) | copy-start | bytes 589828
  3.0 12.3 %copy-start.10 = (bf16[64,4,384]{2,1,0:T(4,128)(2,1)S(1)}, bf16[64,4,384]{2,1,0:T(4,128)(2,1)}, u32[]{:S(2)}) copy-start(bf16[64,4,384]{2,1,0:T(4,128)(2,1)} %param.15) | copy-start | bytes 589828
  3.0 80.5 %all-to-all-start = ((bf16[32,88,384]{2,1,0:T(8,128)(2,1)}), bf16[32,88,384]{2,1,0:T(8,128)(2,1)S(1)}, u32[]{:S(2)}, u32[]{:S(2)}) async-start(bf16[32,88,384]{2,1,0:T(8,128)(2,1)} %tile.2), calls=%async_computation | async-start | bytes 4325376 | tf_op jit(solution)/shard_map/all_to_all | solution.py:21
  13.8 1.7 copy-start.9
  16.7 4.0 %copy-start.22 = (f32[320]{0:T(512)S(1)}, f32[320]{0:T(512)}, u32[]{:S(2)}) copy-start(f32[320]{0:T(512)} %param.27) | copy-start | bytes 3844
  16.7 4.0 %copy-start.23 = (f32[384]{0:T(512)S(1)}, f32[384]{0:T(512)}, u32[]{:S(2)}) copy-start(f32[384]{0:T(512)} %param.25) | copy-start | bytes 4612
  16.7 4.0 %copy-start.26 = (s32[2]{0:T(128)S(1)}, s32[2]{0:T(128)}, u32[]{:S(2)}) copy-start(s32[2]{0:T(128)} %param.21) | copy-start | bytes 28
  20.7 34.6 %copy-start.5 = (bf16[256,384]{1,0:T(8,128)(2,1)S(1)}, bf16[256,384]{1,0:T(8,128)(2,1)}, u32[]{:S(2)}) copy-start(bf16[256,384]{1,0:T(8,128)(2,1)} %reshape.356) | copy-start | bytes 589828
  84.2 1.1 copy-start.6
  84.2 1.2 copy-start.7
  85.8 19.5 %copy-start.4 = (bf16[264,320]{0,1:T(8,128)(2,1)S(1)}, bf16[264,320]{0,1:T(8,128)(2,1)}, u32[]{:S(2)}) copy-start(bf16[264,320]{0,1:T(8,128)(2,1)} %fusion.39) | copy-start | bytes 506884
  87.1 40.1 %all-to-all-start.1 = ((bf16[32,8,704]{2,1,0:T(8,128)(2,1)}), bf16[32,8,704]{2,1,0:T(8,128)(2,1)S(1)}, u32[]{:S(2)}, u32[]{:S(2)}) async-start(bf16[32,8,704]{2,1,0:T(8,128)(2,1)} %bitcast.5), calls=%async_computation.1 | async-start | bytes 786432 | tf_op jit(solution)/shard_map/all_to_all | solution.py:21
  127.3 1.2 copy-start.2
  127.3 1.5 copy-start.27
  127.7 0.5 copy-start.14
  127.7 0.6 copy-start.18
  143.8 1.2 copy-start.3
  143.8 1.2 copy-start.15
  143.8 1.2 copy-start.19
  143.8 1.5 copy-start.28
  145.3 2.5 %copy-start.16 = (f32[256]{0:T(256)S(1)}, f32[256]{0:T(256)}, u32[]{:S(2)}) copy-start(f32[256]{0:T(256)} %copy-done.14) | copy-start | bytes 3076
  145.3 2.5 %copy-start.20 = (f32[256]{0:T(256)S(1)}, f32[256]{0:T(256)}, u32[]{:S(2)}) copy-start(f32[256]{0:T(256)} %copy-done.18) | copy-start | bytes 3076
  147.9 2.0 copy-start.11
  153.6 44.1 %all-to-all-start.2 = ((bf16[32,48,704]{2,1,0:T(8,128)(2,1)}), bf16[32,48,704]{2,1,0:T(8,128)(2,1)S(1)}, u32[]{:S(2)}, u32[]{:S(2)}) async-start(bf16[32,48,704]{2,1,0:T(8,128)(2,1)} %bitcast.97), calls=%async_computation.2 | async-start | bytes 4718592 | tf_op jit(solution)/shard_map/all_to_all | solution.py:21
  165.1 16.4 %collective-permute-start = (bf16[320,256]{1,0:T(8,128)(2,1)}, bf16[320,256]{1,0:T(8,128)(2,1)S(1)}, u32[]{:S(2)}, u32[]{:S(2)}) collective-permute-start(bf16[320,256]{1,0:T(8,128)(2,1)} %get-tuple-element.58), channel_id=1, source_target_pairs={{0,2},{1,3},{2,0},{3,1},{4,6},{5,7},{6,4},{7,5},{8,10},{9,11},{10,... | collective-permute-start | bytes 491528 | tf_op jit(solution)/shard_map/ppermute | solution.py:17
  172.1 19.2 %collective-permute-start.1 = (bf16[320,256]{1,0:T(8,128)(2,1)}, bf16[320,256]{1,0:T(8,128)(2,1)S(1)}, u32[]{:S(2)}, u32[]{:S(2)}) collective-permute-start(bf16[320,256]{1,0:T(8,128)(2,1)} %get-tuple-element.60), channel_id=1, source_target_pairs={{0,1},{1,2},{2,3},{3,0},{4,5},{5,6},{6,7},{7,4},{8,9},{9,10},{10,1... | collective-permute-start | bytes 491528 | tf_op jit(solution)/shard_map/ppermute | solution.py:17
  178.3 17.7 %collective-permute-start.2 = (bf16[320,256]{1,0:T(8,128)(2,1)}, bf16[320,256]{1,0:T(8,128)(2,1)}, u32[]{:S(2)}, u32[]{:S(2)}) collective-permute-start(bf16[320,256]{1,0:T(8,128)(2,1)} %get-tuple-element.59), channel_id=1, source_target_pairs={{0,3},{1,0},{2,1},{3,2},{4,7},{5,4},{6,5},{7,6},{8,11},{9,8},{10,9... | collective-permute-start | bytes 491528 | tf_op jit(solution)/shard_map/ppermute | solution.py:17
  200.2 12.1 %copy-start.24 = (f32[256]{0:T(256)S(1)}, f32[256]{0:T(256)}, u32[]{:S(2)}) copy-start(f32[256]{0:T(256)} %get-tuple-element.42) | copy-start | bytes 3076
  200.2 12.1 %copy-start.25 = (f32[256]{0:T(256)S(1)}, f32[256]{0:T(256)}, u32[]{:S(2)}) copy-start(f32[256]{0:T(256)} %get-tuple-element.44) | copy-start | bytes 3076
  200.2 31.8 %copy-start.1 = (f32[320,256]{1,0:T(8,128)S(1)}, f32[320,256]{1,0:T(8,128)}, u32[]{:S(2)}) copy-start(f32[320,256]{1,0:T(8,128)} %fusion.33) | copy-start | bytes 983044
  200.3 31.8 %copy-start.13 = (f32[320]{0:T(512)S(1)}, f32[320]{0:T(512)}, u32[]{:S(2)}) copy-start(f32[320]{0:T(512)} %param.23) | copy-start | bytes 3844
  200.3 31.8 %copy-start.17 = (f32[256]{0:T(256)S(1)}, f32[256]{0:T(256)}, u32[]{:S(2)}) copy-start(f32[256]{0:T(256)} %copy-done.14) | copy-start | bytes 3076
  200.3 31.8 %copy-start.21 = (f32[256]{0:T(256)S(1)}, f32[256]{0:T(256)}, u32[]{:S(2)}) copy-start(f32[256]{0:T(256)} %copy-done.18) | copy-start | bytes 3076
  201.3 15.9 %all-to-all-start.3 = ((bf16[4,18,704]{2,1,0:T(8,128)(2,1)}), bf16[4,18,704]{2,1,0:T(8,128)(2,1)S(1)}, u32[]{:S(2)}, u32[]{:S(2)}) async-start(bf16[4,18,704]{2,1,0:T(8,128)(2,1)} %pad_maximum_fusion.4), calls=%async_computation.3 | async-start | bytes 294912 | tf_op jit(solution)/shard_map/all_to_all | solution.py:21

commit v5 on v4

--- a/solution.py
+++ b/solution.py
@@ -1,6 +1,8 @@
 import jax
 import jax.numpy as jnp
 from jax import lax
+from jax.experimental import pallas as pl
+from jax.experimental.pallas import tpu as pltpu
 from jax.sharding import Mesh
 from jax.sharding import PartitionSpec as P
 
@@ -48,15 +50,39 @@
     return terms
 
 
-def to_rows(vector, width):
-    terms = jnp.concatenate(split(vector, 2))
-    rows = -(-terms.shape[0] // (8 * width)) * 8
-    return jnp.pad(terms, (0, rows * width - terms.shape[0])).reshape(rows, width)
-
-
-def from_rows(rows, length):
-    terms = rows.astype(f32).reshape(*rows.shape[:-2], -1)
-    return terms[..., :length] + terms[..., length : 2 * length]
+def split_rows(rows):
+    term = lax.reduce_precision(rows, 8, 7)
+    return jnp.concatenate([term, lax.reduce_precision(rows - term, 8, 7)], axis=0)
+
+
+def summed_rows(pieces):
+    rows = jnp.sum(pieces.astype(f32), axis=0)
+    return rows[:4] + rows[4:]
+
+
+def payload_kernel(dealt_ref, back_ref, beside_ref, out_ref):
+    block = beside_ref.shape[0]
+    step = 8 * block
+    for start in range(0, dealt_ref.shape[0], step):
+        rows = pl.ds(start, step)
+        weight = dot(dealt_ref[rows, :], back_ref[...])
+        whole = weight.reshape(8, block, weight.shape[1]) + beside_ref[...][None]
+        out_ref[rows, :] = whole.reshape(weight.shape).astype(bf16)
+
+
+def payload(dealt, back, beside):
+    n, k = dealt.shape
+    wt = back.shape[1]
+    return pl.pallas_call(
+        payload_kernel,
+        out_shape=jax.ShapeDtypeStruct((n, wt), bf16),
+        in_specs=[pl.BlockSpec(memory_space=pltpu.VMEM)] * 3,
+        out_specs=pl.BlockSpec(memory_space=pltpu.VMEM),
+        compiler_params=pltpu.CompilerParams(vmem_limit_bytes=24 * 2**20),
+        cost_estimate=pl.CostEstimate(
+            flops=2 * n * k * wt, bytes_accessed=2 * (n * k + k * wt + n * wt), transcendentals=0
+        ),
+    )(dealt, back, beside)
 
 
 def head_grad(out, target, inner, square, tsquare, live):
@@ -142,7 +168,6 @@
     inside = spot % block
     feature = (inside // each * peers + spot // block) * each + inside % each
     dealt = dot_last(one_hot(jnp.where(inside < strip, feature, -1), feats), normed).astype(bf16)
-    dealt = jnp.concatenate([dealt, one_hot(jnp.where(inside < strip, -1, inside - strip), 16)], axis=1)
 
     stats = lax.psum(
         jnp.stack(
@@ -169,11 +194,16 @@
     )
     gain_part = jnp.sum(partial * standard.T, axis=1)
 
-    length = wt + feats + 1
-    vector = jnp.concatenate([jnp.sum(grad, axis=0), gain_part, jnp.sum(live).reshape(1)])
-    beside = to_rows(vector, wt)
-    under = jnp.concatenate([back, jnp.pad(beside, ((0, 16 - beside.shape[0]), (0, 0)))], axis=0)
-    weight = dot(dealt, under).astype(bf16)
+    rest = feats - wt
+    vector = jnp.stack(
+        [
+            jnp.sum(grad, axis=0),
+            gain_part[:wt],
+            jnp.pad(gain_part[wt:], (0, wt - rest)),
+            jnp.full((wt,), jnp.sum(live)),
+        ]
+    )
+    weight = payload(dealt, back, jnp.pad(split_rows(vector), ((strip, 0), (0, 0))))
     parts = partial.astype(bf16).reshape(4, wf, rows)
     slab = exchange(weight, DP).reshape(peers, block, wt)
     normed_grad = sum(
@@ -185,20 +215,20 @@
         ]
     )
     weight = jnp.sum(slab[:, :strip].astype(f32), axis=0).astype(bf16)
-    vector = jnp.sum(from_rows(slab[:, strip:], length), axis=0)
-    beside = to_rows(vector, wt)
+    beside = split_rows(summed_rows(slab[:, strip:])).astype(bf16)
     deal = jnp.concatenate(
         [weight.reshape(4, each, wt), jnp.broadcast_to(beside[None], (4,) + beside.shape)], axis=1
     )
     deal, normed_grad = lax.optimization_barrier((deal, normed_grad))
     share = exchange(deal.reshape(-1, wt), "g").reshape(deal.shape)
     weight = jnp.sum(share[:, :each].astype(f32), axis=0)
-    vector = jnp.sum(from_rows(share[:, each:], length), axis=0)
-    factor = lax.rsqrt(vector[-1])
+    vector = summed_rows(share[:, each:])
+    row_sums, gain_rows = lax.psum((row_sums, vector[1:3]), "m")
+    factor = lax.rsqrt(vector[3, 0])
     weight = (factor * weight).astype(bf16)
-    sums = lax.psum(jnp.concatenate([row_sums.reshape(-1), vector[wt:-1]]), "m")
-    row_sums = sums[: 2 * rows].reshape(2, rows)
-    gain_grad = factor * lax.dynamic_slice_in_dim(sums, 2 * rows + m * wf, wf)
+    bias_grad = factor * vector[0]
+    gain_grad = jnp.concatenate([gain_rows[0], gain_rows[1, :rest]])
+    gain_grad = factor * lax.dynamic_slice_in_dim(gain_grad, m * wf, wf)
 
     own = student_stream.reshape(rows, wf).astype(f32)
     own_standard = (own - center) * scale
@@ -208,9 +238,9 @@
     return (
         stream_grad.reshape(own_slots, window, wf),
         weight[:, :wd],
-        factor * vector[:wd],
+        bias_grad[:wd],
         weight[:, wd:],
-        factor * vector[wd:wt],
+        bias_grad[wd:],
         gain_grad,
     )
 

time: 236 us -> 230 us (0.975)
  other arithmetic: 12 us -> 7.55 us
  waiting for transfers between devices: 19.5 us -> 17 us
    ppermute x3, waiting for transfers between devices: 14.6 us -> 12.1 us  [shift_m(): return lax.ppermute(array, 'm', [(i, (i + by) % 4) for i in range(4)])]
    convert_element_type x1 -> x0, local copies, waits for them, and re-layouts: 2.44 us -> none  [local(): weight = dot(dealt, under).astype(bf16)]
    unnamed x63 -> x40, local copies, waits for them, and re-layouts: 5.42 us -> 6.73 us
  transfers between devices with their start and end apart: 7 -> 7, of which waited for: 4 -> 3; matrix products, arithmetic and copies ran while one was open for 5% -> 5% of each run, Pallas kernels for 0% -> 0%
where the time goes in v5:
time: 230 us; the launch traced here: 226 us
  blocking collectives  106 us (46%)
  starting transfers between devices  67.7 us (29%)
  local copies, waits for them, and re-layouts  18 us (8%)
  waiting for transfers between devices  17 us (7%)
  other arithmetic  7.55 us (3%)
  matrix products  5.2 us (2%)
    all_to_all x4, starting transfers between devices, exchange(): return lax.all_to_all(array, axis, split_axis=0, concat_axis=0, tiled=True)  51.5 us
    all_gather x1, blocking collectives, local(): lax.all_gather(sam_context.reshape(rows, ws), 'm', axis=1, tiled=True)  33.1 us
    all_gather x1, blocking collectives, local(): lax.all_gather(dino_context.reshape(rows, wd), 'm', axis=1, tiled=True)  27.7 us
    all_gather x1, blocking collectives, local(): student = lax.all_gather(student, 'm', axis=1, tiled=True)  19.5 us
    ppermute x3, starting transfers between devices, shift_m(): return lax.ppermute(array, 'm', [(i, (i + by) % 4) for i in range(4)])  16.2 us
    psum x1, blocking collectives, local(): lax.psum(jnp.stack([jnp.sum(dino_out * dino_target, axis=1), jnp.sum(dino...  15.4 us
    ppermute x3, waiting for transfers between devices, shift_m(): return lax.ppermute(array, 'm', [(i, (i + by) % 4) for i in range(4)])  12.1 us
    psum x1, blocking collectives, local(): row_sums, gain_rows = lax.psum((row_sums, vector[1:3]), 'm')  10.7 us
  transfers between devices with their start and end apart: 7, of which 3 were waited for; matrix products, arithmetic and copies ran while one was open for 5% of the time, Pallas kernels for 0%

profile of v5, /device:TPU:1, one launch (start us, length us, event | category | flops | bytes accessed | tf_op | source)
XLA Modules:
  0.0 225.9 jit_solution(3294130409913360500)
XLA Ops:
  0.6 0.8 fusion.33
  1.5 1.5 tile.2
  3.0 10.7 %all-to-all-start = ((bf16[32,88,384]{2,1,0:T(8,128)(2,1)}), bf16[32,88,384]{2,1,0:T(8,128)(2,1)S(1)}, u32[]{:S(2)}, u32[]{:S(2)}) async-start(bf16[32,88,384]{2,1,0:T(8,128)(2,1)} %tile.2), calls=%async_computation | async-start | bytes 4325376 | tf_op jit(solution)/shard_map/all_to_all | solution.py:23
  13.8 0.2 copy.64
  14.0 0.7 reshape.358
  14.8 0.2 copy.60
  15.1 0.1 copy.61
  15.2 1.0 reshape.366
  16.2 0.9 copy.62
  17.2 0.1 add.257
  17.3 2.2 copy.69
  19.5 0.7 convert_reduce_fusion.5
  20.2 0.7 pad.33.clone
  21.0 0.7 fusion.28
  21.7 33.1 %all_gather.10 = bf16[256,1280]{0,1:T(8,128)(2,1)} all-gather(bf16[256,320]{0,1:T(8,128)(2,1)S(1)} %copy.61), channel_id=1, replica_groups=mesh['g'=4,'y'=4,'x'=4,'c'=2,'m'=4] {'m'}, dimensions={1}, use_global_device_ids=true | all-gather | bytes 819200 | tf_op jit(solution)/shard_map/all_gather | solution.py:121
  54.8 27.7 %all_gather.9 = bf16[256,1536]{1,0:T(8,128)(2,1)S(1)} all-gather(bf16[256,384]{1,0:T(8,128)(2,1)S(1)} %copy-done.4), channel_id=1, replica_groups=mesh['g'=4,'y'=4,'x'=4,'c'=2,'m'=4] {'m'}, dimensions={1}, use_global_device_ids=true | all-gather | bytes 983040 | tf_op jit(solution)/shard_map/all_gather | solution.py:120
  82.5 0.1 slice.154
  82.6 0.5 fusion.15
  83.3 1.0 copy-done.5
  84.3 0.4 fusion.16
  84.8 0.3 convolution_convert_fusion
  85.1 0.9 copy.65
  86.0 18.2 %all-to-all-start.1 = ((bf16[32,8,704]{2,1,0:T(8,128)(2,1)}), bf16[32,8,704]{2,1,0:T(8,128)(2,1)S(1)}, u32[]{:S(2)}, u32[]{:S(2)}) async-start(bf16[32,8,704]{2,1,0:T(8,128)(2,1)} %bitcast.5), calls=%async_computation.1 | async-start | bytes 786432 | tf_op jit(solution)/shard_map/all_to_all | solution.py:23
  104.2 0.2 copy.66
  104.4 19.5 %all-gather = bf16[4,320,264]{1,2,0:T(8,128)(2,1)S(1)} all-gather(bf16[1,320,264]{1,2,0:T(8,128)(2,1)S(1)} %copy.66), channel_id=1, replica_groups=mesh['g'=4,'y'=4,'x'=4,'c'=2,'m'=4] {'m'}, dimensions={0}, use_global_device_ids=true | all-gather | bytes 844800 | tf_op jit(solution)/shard_map/all_gather | solution.py:141
  123.9 0.7 copy.67
  124.6 0.2 convert_reduce_fusion
  124.8 0.2 convert_reduce_fusion.2
  125.0 0.3 fusion.27
  125.3 0.5 copy-done.1
  125.8 0.3 copy-done.16
  126.1 0.9 convolution_add_fusion
  127.0 0.2 multiply_reduce_fusion.1
  127.2 0.2 multiply_reduce_fusion.4
  127.4 15.4 %psum.21 = f32[6,256]{1,0:T(8,128)S(1)} all-reduce(f32[6,256]{1,0:T(8,128)S(1)} %stack.64), channel_id=1, replica_groups=mesh['g'=4,'y'=4,'x'=4,'c'=2,'m'=4] {'m'}, use_global_device_ids=true, to_apply=%region_9.10 | all-reduce | flops 1536 | bytes 12288 | tf_op jit(solution)/shard_map/psum | solution.py:172
  142.8 0.2 subtract_multiply_fusion.1
  143.1 0.2 subtract_multiply_fusion
  143.4 0.8 copy-done.2
  144.3 0.3 copy-done.17
  144.6 1.0 fusion.9
  145.6 1.7 fusion.2.dealt_ref
  147.5 2.2 shard_map.181
  149.7 11.7 %all-to-all-start.2 = ((bf16[32,48,704]{2,1,0:T(8,128)(2,1)}), bf16[32,48,704]{2,1,0:T(8,128)(2,1)S(1)}, u32[]{:S(2)}, u32[]{:S(2)}) async-start(bf16[32,48,704]{2,1,0:T(8,128)(2,1)} %bitcast.25), calls=%async_computation.2 | async-start | bytes 4718592 | tf_op jit(solution)/shard_map/all_to_all | solution.py:23
  161.4 0.8 dynamic-slice_bitcast_fusion.2
  162.2 7.0 %collective-permute-start = (bf16[320,256]{1,0:T(8,128)(2,1)}, bf16[320,256]{1,0:T(8,128)(2,1)S(1)}, u32[]{:S(2)}, u32[]{:S(2)}) collective-permute-start(bf16[320,256]{1,0:T(8,128)(2,1)} %get-tuple-element.60), channel_id=1, source_target_pairs={{0,2},{1,3},{2,0},{3,1},{4,6},{5,7},{6,4},{7,5},{8,10},{9,11},{10,... | collective-permute-start | bytes 491528 | tf_op jit(solution)/shard_map/ppermute | solution.py:19
  169.2 3.6 %collective-permute-start.1 = (bf16[320,256]{1,0:T(8,128)(2,1)}, bf16[320,256]{1,0:T(8,128)(2,1)S(1)}, u32[]{:S(2)}, u32[]{:S(2)}) collective-permute-start(bf16[320,256]{1,0:T(8,128)(2,1)} %get-tuple-element.62), channel_id=1, source_target_pairs={{0,1},{1,2},{2,3},{3,0},{4,5},{5,6},{6,7},{7,4},{8,9},{9,10},{10,1... | collective-permute-start | bytes 491528 | tf_op jit(solution)/shard_map/ppermute | solution.py:19
  172.9 5.6 %collective-permute-start.2 = (bf16[320,256]{1,0:T(8,128)(2,1)}, bf16[320,256]{1,0:T(8,128)(2,1)}, u32[]{:S(2)}, u32[]{:S(2)}) collective-permute-start(bf16[320,256]{1,0:T(8,128)(2,1)} %get-tuple-element.61), channel_id=1, source_target_pairs={{0,3},{1,0},{2,1},{3,2},{4,7},{5,4},{6,5},{7,6},{8,11},{9,8},{10,9... | collective-permute-start | bytes 491528 | tf_op jit(solution)/shard_map/ppermute | solution.py:19
  178.4 3.7 %collective-permute-done = bf16[320,256]{1,0:T(8,128)(2,1)S(1)} collective-permute-done((bf16[320,256]{1,0:T(8,128)(2,1)}, bf16[320,256]{1,0:T(8,128)(2,1)S(1)}, u32[]{:S(2)}, u32[]{:S(2)}) %collective-permute-start) | collective-permute-done | bytes 163872 | tf_op jit(solution)/shard_map/ppermute | solution.py:19
  182.2 0.7 copy-done.10
  182.8 0.7 copy-done.11
  183.5 8.4 %collective-permute-done.2 = bf16[320,256]{1,0:T(8,128)(2,1)} collective-permute-done((bf16[320,256]{1,0:T(8,128)(2,1)}, bf16[320,256]{1,0:T(8,128)(2,1)}, u32[]{:S(2)}, u32[]{:S(2)}) %collective-permute-start.2) | collective-permute-done | bytes 163872 | tf_op jit(solution)/shard_map/ppermute | solution.py:19
  191.8 1.1 fusion.24
  193.0 0.3 slice_reduce_fusion
  193.4 0.7 pad_maximum_fusion.4
  194.1 10.9 %all-to-all-start.3 = ((bf16[4,18,704]{2,1,0:T(8,128)(2,1)}), bf16[4,18,704]{2,1,0:T(8,128)(2,1)S(1)}, u32[]{:S(2)}, u32[]{:S(2)}) async-start(bf16[4,18,704]{2,1,0:T(8,128)(2,1)} %pad_maximum_fusion.4), calls=%async_computation.3 | async-start | bytes 294912 | tf_op jit(solution)/shard_map/all_to_all | solution.py:23
  205.1 4.8 %all-to-all-done.3 = bf16[4,18,704]{2,1,0:T(8,128)(2,1)S(1)} async-done(((bf16[4,18,704]{2,1,0:T(8,128)(2,1)}), bf16[4,18,704]{2,1,0:T(8,128)(2,1)S(1)}, u32[]{:S(2)}, u32[]{:S(2)}) %all-to-all-start.3) | async-done | bytes 101408 | tf_op jit(solution)/shard_map/all_to_all | solution.py:23
  210.0 10.7 %all-reduce.4 = (f32[2,256]{1,0:T(2,128)S(1)}, f32[2,704]{1,0:T(2,128)S(1)}) all-reduce(f32[2,256]{1,0:T(2,128)S(1)} %pad_maximum_fusion.8, f32[2,704]{1,0:T(2,128)S(1)} %slice.184), channel_id=1, replica_groups=mesh['g'=4,'y'=4,'x'=4,'c'=2,'m'=4] {'m'}, use_global_device_ids=true, to_apply=%region_17.18 | all-reduce | flops 1920 | bytes 15360 | tf_op jit(solution)/shard_map/psum | solution.py:226
  220.8 0.5 slice.177
  222.0 0.6 slice_reduce_fusion.3
  222.6 0.6 slice_reduce_fusion.4
  223.2 0.6 slice.179
  223.8 0.6 slice.182
  224.4 0.7 fusion.62
  225.1 0.8 copy_bitcast_fusion.1
  (79 shorter events, 1.2 us)
Async XLA Ops:
  0.6 20.3 %copy-start = (bf16[2,128,320]{1,2,0:T(8,128)(2,1)S(1)}, bf16[2,128,320]{1,2,0:T(8,128)(2,1)}, u32[]{:S(2)}) copy-start(bf16[2,128,320]{1,2,0:T(8,128)(2,1)} %param.22) | copy-start | bytes 491524
  3.0 10.7 %copy-start.12 = (f32[320]{0:T(512)S(1)}, f32[320]{0:T(512)}, u32[]{:S(2)}) copy-start(f32[320]{0:T(512)} %param.23) | copy-start | bytes 3844
  3.0 11.0 %copy-start.7 = (bf16[64,4,384]{2,1,0:T(4,128)(2,1)S(1)}, bf16[64,4,384]{2,1,0:T(4,128)(2,1)}, u32[]{:S(2)}) copy-start(bf16[64,4,384]{2,1,0:T(4,128)(2,1)} %param.14) | copy-start | bytes 589828
  3.0 11.7 %copy-start.9 = (bf16[64,4,384]{2,1,0:T(4,128)(2,1)S(1)}, bf16[64,4,384]{2,1,0:T(4,128)(2,1)}, u32[]{:S(2)}) copy-start(bf16[64,4,384]{2,1,0:T(4,128)(2,1)} %param.15) | copy-start | bytes 589828
  3.0 79.4 %all-to-all-start = ((bf16[32,88,384]{2,1,0:T(8,128)(2,1)}), bf16[32,88,384]{2,1,0:T(8,128)(2,1)S(1)}, u32[]{:S(2)}, u32[]{:S(2)}) async-start(bf16[32,88,384]{2,1,0:T(8,128)(2,1)} %tile.2), calls=%async_computation | async-start | bytes 4325376 | tf_op jit(solution)/shard_map/all_to_all | solution.py:23
  13.8 1.2 copy-start.8
  14.8 2.3 %copy-start.18 = (s32[1,64]{1,0:T(1,128)S(1)}, s32[1,64]{1,0:T(1,128)}, u32[]{:S(2)}) copy-start(s32[1,64]{1,0:T(1,128)} %param.20) | copy-start | bytes 772
  16.2 3.3 %copy-start.15 = (s32[2]{0:T(128)S(1)}, s32[2]{0:T(128)}, u32[]{:S(2)}) copy-start(s32[2]{0:T(128)} %param.21) | copy-start | bytes 28
  16.2 4.7 %copy-start.13 = (f32[320]{0:T(512)S(1)}, f32[320]{0:T(512)}, u32[]{:S(2)}) copy-start(f32[320]{0:T(512)} %param.27) | copy-start | bytes 3844
  16.2 4.7 %copy-start.14 = (f32[384]{0:T(512)S(1)}, f32[384]{0:T(512)}, u32[]{:S(2)}) copy-start(f32[384]{0:T(512)} %param.25) | copy-start | bytes 4612
  19.5 35.3 %copy-start.4 = (bf16[256,384]{1,0:T(8,128)(2,1)S(1)}, bf16[256,384]{1,0:T(8,128)(2,1)}, u32[]{:S(2)}) copy-start(bf16[256,384]{1,0:T(8,128)(2,1)} %reshape.358) | copy-start | bytes 589828
  83.1 1.1 copy-start.5
  83.1 1.2 copy-start.6
  84.8 19.4 %copy-start.3 = (bf16[264,320]{0,1:T(8,128)(2,1)S(1)}, bf16[264,320]{0,1:T(8,128)(2,1)}, u32[]{:S(2)}) copy-start(bf16[264,320]{0,1:T(8,128)(2,1)} %fusion.28) | copy-start | bytes 506884
  86.0 38.5 %all-to-all-start.1 = ((bf16[32,8,704]{2,1,0:T(8,128)(2,1)}), bf16[32,8,704]{2,1,0:T(8,128)(2,1)S(1)}, u32[]{:S(2)}, u32[]{:S(2)}) async-start(bf16[32,8,704]{2,1,0:T(8,128)(2,1)} %bitcast.5), calls=%async_computation.1 | async-start | bytes 786432 | tf_op jit(solution)/shard_map/all_to_all | solution.py:23
  124.6 1.2 copy-start.1
  124.6 1.5 copy-start.16
  143.1 1.2 copy-start.2
  143.1 1.5 copy-start.17
  149.7 43.3 %all-to-all-start.2 = ((bf16[32,48,704]{2,1,0:T(8,128)(2,1)}), bf16[32,48,704]{2,1,0:T(8,128)(2,1)S(1)}, u32[]{:S(2)}, u32[]{:S(2)}) async-start(bf16[32,48,704]{2,1,0:T(8,128)(2,1)} %bitcast.25), calls=%async_computation.2 | async-start | bytes 4718592 | tf_op jit(solution)/shard_map/all_to_all | solution.py:23
  162.2 19.9 %collective-permute-start = (bf16[320,256]{1,0:T(8,128)(2,1)}, bf16[320,256]{1,0:T(8,128)(2,1)S(1)}, u32[]{:S(2)}, u32[]{:S(2)}) collective-permute-start(bf16[320,256]{1,0:T(8,128)(2,1)} %get-tuple-element.60), channel_id=1, source_target_pairs={{0,2},{1,3},{2,0},{3,1},{4,6},{5,7},{6,4},{7,5},{8,10},{9,11},{10,... | collective-permute-start | bytes 491528 | tf_op jit(solution)/shard_map/ppermute | solution.py:19
  169.2 13.0 %collective-permute-start.1 = (bf16[320,256]{1,0:T(8,128)(2,1)}, bf16[320,256]{1,0:T(8,128)(2,1)S(1)}, u32[]{:S(2)}, u32[]{:S(2)}) collective-permute-start(bf16[320,256]{1,0:T(8,128)(2,1)} %get-tuple-element.62), channel_id=1, source_target_pairs={{0,1},{1,2},{2,3},{3,0},{4,5},{5,6},{6,7},{7,4},{8,9},{9,10},{10,1... | collective-permute-start | bytes 491528 | tf_op jit(solution)/shard_map/ppermute | solution.py:19
  172.9 19.0 %collective-permute-start.2 = (bf16[320,256]{1,0:T(8,128)(2,1)}, bf16[320,256]{1,0:T(8,128)(2,1)}, u32[]{:S(2)}, u32[]{:S(2)}) collective-permute-start(bf16[320,256]{1,0:T(8,128)(2,1)} %get-tuple-element.61), channel_id=1, source_target_pairs={{0,3},{1,0},{2,1},{3,2},{4,7},{5,4},{6,5},{7,6},{8,11},{9,8},{10,9... | collective-permute-start | bytes 491528 | tf_op jit(solution)/shard_map/ppermute | solution.py:19
  182.2 0.7 copy-start.10
  182.8 0.7 copy-start.11
  194.1 15.8 %all-to-all-start.3 = ((bf16[4,18,704]{2,1,0:T(8,128)(2,1)}), bf16[4,18,704]{2,1,0:T(8,128)(2,1)S(1)}, u32[]{:S(2)}, u32[]{:S(2)}) async-start(bf16[4,18,704]{2,1,0:T(8,128)(2,1)} %pad_maximum_fusion.4), calls=%async_computation.3 | async-start | bytes 294912 | tf_op jit(solution)/shard_map/all_to_all | solution.py:23

commit v6 on v5

--- a/solution.py
+++ b/solution.py
@@ -134,11 +134,13 @@
     image_row = jnp.arange(per_peer, dtype=jnp.int32)[None, :]
     goes_to = (owners[0][:, None] * per_peer + image_row).reshape(-1)
     sent = dot_rows(one_hot(goes_to, rows), feat).astype(bf16)
-    gain_terms = jnp.pad(jnp.stack(split(norm_gain, 3)), ((0, 5), (0, 0)))
-    student = jnp.concatenate([student_stream.reshape(rows, wf), gain_terms], axis=0)
+    spare = -3 * wf % rows
+    gain_terms = jnp.pad(jnp.concatenate(split(norm_gain, 3)), (0, spare)).reshape(-1, rows)
+    gain_terms = jnp.pad(gain_terms, ((0, -gain_terms.shape[0] % 8), (0, 0)))
+    student = jnp.concatenate([student_stream.reshape(rows, wf).T, gain_terms], axis=0)
     sent, student = lax.optimization_barrier((sent, student))
     arrived = exchange(sent, DP)
-    student = lax.all_gather(student, "m", axis=1, tiled=True)
+    student = lax.all_gather(student, "m", axis=0, tiled=False)
     arrived, student = lax.optimization_barrier((arrived, student))
     place = jnp.arange(rows, dtype=jnp.int32)
     slot, row = place // window, place % window
@@ -151,8 +153,9 @@
         .astype(f32)
         .reshape(rows, 1)
     )
-    values = student[:rows].astype(f32)
-    gain = jnp.sum(student[rows:].astype(f32), axis=0, keepdims=True)
+    values = student[:, :wf].reshape(feats, rows).T.astype(f32)
+    gain = student[:, wf:].reshape(4, -1)[:, : 3 * wf].reshape(4, 3, wf).astype(f32)
+    gain = jnp.sum(gain, axis=1).reshape(1, feats)
     center = jnp.sum(values, axis=1, keepdims=True) / feats
     spread = jnp.sum(values * values, axis=1, keepdims=True) / feats - center * center
     scale = lax.rsqrt(spread + eps)

time: 230 us -> 227 us (0.987)
  starting transfers between devices: 67.7 us -> 61 us
  waiting for transfers between devices: 17 us -> 23.3 us
  local copies, waits for them, and re-layouts: 18 us -> 13.8 us
    all_to_all x4, starting transfers between devices: 51.5 us -> 44.8 us  [exchange(): return lax.all_to_all(array, axis, split_axis=0, concat_axis=0, tiled=True)]
    ppermute x3, waiting for transfers between devices: 12.1 us -> 18.4 us  [shift_m(): return lax.ppermute(array, 'm', [(i, (i + by) % 4) for i in range(4)])]
    psum x1, blocking collectives: 15.4 us -> 12.4 us  [local(): lax.psum(jnp.stack([jnp.sum(dino_out * dino_target, axis=1), jnp.sum(dino...]
    unnamed x40 -> x39, local copies, waits for them, and re-layouts: 6.73 us -> 4.14 us
  transfers between devices with their start and end apart: 7 -> 7, of which waited for: 3 -> 3; matrix products, arithmetic and copies ran while one was open for 5% -> 4% of each run, Pallas kernels for 0% -> 0%
where the time goes in v6:
time: 227 us; the launch traced here: 223 us
  blocking collectives  107 us (47%)
  starting transfers between devices  61 us (27%)
  waiting for transfers between devices  23.3 us (10%)
  local copies, waits for them, and re-layouts  13.8 us (6%)
  other arithmetic  7.84 us (3%)
  matrix products  6.28 us (3%)
    all_to_all x4, starting transfers between devices, exchange(): return lax.all_to_all(array, axis, split_axis=0, concat_axis=0, tiled=True)  44.8 us
    all_gather x1, blocking collectives, local(): lax.all_gather(sam_context.reshape(rows, ws), 'm', axis=1, tiled=True)  33.1 us
    all_gather x1, blocking collectives, local(): lax.all_gather(dino_context.reshape(rows, wd), 'm', axis=1, tiled=True)  27.9 us
    all_gather x1, blocking collectives, local(): student = lax.all_gather(student, 'm', axis=0, tiled=False)  21.4 us
    ppermute x3, waiting for transfers between devices, shift_m(): return lax.ppermute(array, 'm', [(i, (i + by) % 4) for i in range(4)])  18.4 us
    ppermute x3, starting transfers between devices, shift_m(): return lax.ppermute(array, 'm', [(i, (i + by) % 4) for i in range(4)])  16.2 us
    psum x1, blocking collectives, local(): row_sums, gain_rows = lax.psum((row_sums, vector[1:3]), 'm')  12.4 us
    psum x1, blocking collectives, local(): lax.psum(jnp.stack([jnp.sum(dino_out * dino_target, axis=1), jnp.sum(dino...  12.4 us
  transfers between devices with their start and end apart: 7, of which 3 were waited for; matrix products, arithmetic and copies ran while one was open for 4% of the time, Pallas kernels for 0%

profile of v6, /device:TPU:1, one launch (start us, length us, event | category | flops | bytes accessed | tf_op | source)
XLA Modules:
  0.0 223.4 jit_solution(598941132782397089)
XLA Ops:
  0.6 0.8 fusion.32
  1.5 1.5 tile.2
  3.0 10.7 %all-to-all-start = ((bf16[32,88,384]{2,1,0:T(8,128)(2,1)}), bf16[32,88,384]{2,1,0:T(8,128)(2,1)S(1)}, u32[]{:S(2)}, u32[]{:S(2)}) async-start(bf16[32,88,384]{2,1,0:T(8,128)(2,1)} %tile.2), calls=%async_computation | async-start | bytes 4325376 | tf_op jit(solution)/shard_map/all_to_all | solution.py:23
  13.8 0.1 fusion.62
  13.9 0.7 reshape.372
  14.7 0.2 copy.51
  14.9 0.1 reshape.374
  15.0 0.1 copy.52
  15.2 0.9 copy.53
  16.2 0.1 add.259
  16.3 2.2 copy.57
  18.5 0.7 convert_reduce_fusion.4
  19.2 0.7 pad.38.clone
  20.0 0.7 fusion.27
  20.6 33.1 %all_gather.13 = bf16[256,1280]{0,1:T(8,128)(2,1)} all-gather(bf16[256,320]{0,1:T(8,128)(2,1)S(1)} %copy.52), channel_id=1, replica_groups=mesh['g'=4,'y'=4,'x'=4,'c'=2,'m'=4] {'m'}, dimensions={1}, use_global_device_ids=true | all-gather | bytes 819200 | tf_op jit(solution)/shard_map/all_gather | solution.py:121
  53.7 27.9 %all_gather.12 = bf16[256,1536]{1,0:T(8,128)(2,1)S(1)} all-gather(bf16[256,384]{1,0:T(8,128)(2,1)} %reshape.372), channel_id=1, replica_groups=mesh['g'=4,'y'=4,'x'=4,'c'=2,'m'=4] {'m'}, dimensions={1}, use_global_device_ids=true | all-gather | bytes 983040 | tf_op jit(solution)/shard_map/all_gather | solution.py:120
  81.6 0.1 slice.158
  81.7 0.5 fusion.14
  82.3 0.1 slice.159
  82.4 0.4 copy-done.5
  82.8 0.1 copy-done.6
  82.9 0.5 fusion.15
  83.3 0.3 convolution_convert_fusion
  83.7 0.9 copy.55
  84.6 18.2 %all-to-all-start.1 = ((bf16[32,8,704]{2,1,0:T(8,128)(2,1)}), bf16[32,8,704]{2,1,0:T(8,128)(2,1)S(1)}, u32[]{:S(2)}, u32[]{:S(2)}) async-start(bf16[32,8,704]{2,1,0:T(8,128)(2,1)} %bitcast.6), calls=%async_computation.1 | async-start | bytes 786432 | tf_op jit(solution)/shard_map/all_to_all | solution.py:23
  102.8 21.4 %all-gather = bf16[1312,256]{1,0:T(8,128)(2,1)S(1)} all-gather(bf16[328,256]{1,0:T(8,128)(2,1)S(1)} %copy-done.2), channel_id=2, replica_groups=mesh['g'=4,'y'=4,'x'=4,'c'=2,'m'=4] {'m'}, dimensions={0}, use_global_device_ids=true | all-gather | bytes 839680 | tf_op jit(solution)/shard_map/all_gather | solution.py:143
  124.2 0.2 convert_reduce_fusion
  124.4 0.2 fusion.10
  124.6 0.1 reshape.383
  124.8 0.1 mul.274
  124.9 0.3 fusion.26
  125.2 0.2 fusion.7
  125.4 2.2 convolution_add_fusion
  127.6 0.2 multiply_reduce_fusion.1
  127.8 0.2 multiply_reduce_fusion.4
  128.0 12.4 %psum.21 = f32[6,256]{1,0:T(8,128)S(1)} all-reduce(f32[6,256]{1,0:T(8,128)S(1)} %stack.48), channel_id=1, replica_groups=mesh['g'=4,'y'=4,'x'=4,'c'=2,'m'=4] {'m'}, use_global_device_ids=true, to_apply=%region_9.10 | all-reduce | flops 1536 | bytes 12288 | tf_op jit(solution)/shard_map/psum | solution.py:175
  140.5 0.2 subtract_multiply_fusion.1
  140.7 0.2 subtract_multiply_fusion
  141.1 0.6 copy-done.16
  141.7 1.0 fusion.9
  142.8 1.5 fusion.2.dealt_ref
  144.3 0.1 fusion.75
  144.4 2.2 shard_map.181
  146.6 10.0 %all-to-all-start.2 = ((bf16[32,48,704]{2,1,0:T(8,128)(2,1)}), bf16[32,48,704]{2,1,0:T(8,128)(2,1)S(1)}, u32[]{:S(2)}, u32[]{:S(2)}) async-start(bf16[32,48,704]{2,1,0:T(8,128)(2,1)} %bitcast.23), calls=%async_computation.2 | async-start | bytes 4718592 | tf_op jit(solution)/shard_map/all_to_all | solution.py:23
  156.6 0.8 dynamic-slice_bitcast_fusion.2
  157.4 7.0 %collective-permute-start = (bf16[320,256]{1,0:T(8,128)(2,1)}, bf16[320,256]{1,0:T(8,128)(2,1)}, u32[]{:S(2)}, u32[]{:S(2)}) collective-permute-start(bf16[320,256]{1,0:T(8,128)(2,1)} %get-tuple-element.58), channel_id=1, source_target_pairs={{0,2},{1,3},{2,0},{3,1},{4,6},{5,7},{6,4},{7,5},{8,10},{9,11},{10,... | collective-permute-start | bytes 491528 | tf_op jit(solution)/shard_map/ppermute | solution.py:19
  164.4 7.1 %collective-permute-start.1 = (bf16[320,256]{1,0:T(8,128)(2,1)}, bf16[320,256]{1,0:T(8,128)(2,1)S(1)}, u32[]{:S(2)}, u32[]{:S(2)}) collective-permute-start(bf16[320,256]{1,0:T(8,128)(2,1)} %get-tuple-element.60), channel_id=1, source_target_pairs={{0,1},{1,2},{2,3},{3,0},{4,5},{5,6},{6,7},{7,4},{8,9},{9,10},{10,1... | collective-permute-start | bytes 491528 | tf_op jit(solution)/shard_map/ppermute | solution.py:19
  171.5 2.1 collective-permute-start.2
  173.6 0.3 collective-permute-done
  173.9 18.2 %collective-permute-done.1 = bf16[320,256]{1,0:T(8,128)(2,1)S(1)} collective-permute-done((bf16[320,256]{1,0:T(8,128)(2,1)}, bf16[320,256]{1,0:T(8,128)(2,1)S(1)}, u32[]{:S(2)}, u32[]{:S(2)}) %collective-permute-start.1) | collective-permute-done | bytes 163872 | tf_op jit(solution)/shard_map/ppermute | solution.py:19
  192.0 0.7 copy-done.11
  192.7 1.2 fusion.23
  193.9 0.3 slice_reduce_fusion
  194.3 0.7 pad_maximum_fusion.4
  195.0 6.0 %all-to-all-start.3 = ((bf16[4,18,704]{2,1,0:T(8,128)(2,1)}), bf16[4,18,704]{2,1,0:T(8,128)(2,1)S(1)}, u32[]{:S(2)}, u32[]{:S(2)}) async-start(bf16[4,18,704]{2,1,0:T(8,128)(2,1)} %pad_maximum_fusion.4), calls=%async_computation.3 | async-start | bytes 294912 | tf_op jit(solution)/shard_map/all_to_all | solution.py:23
  201.0 4.8 %all-to-all-done.3 = bf16[4,18,704]{2,1,0:T(8,128)(2,1)S(1)} async-done(((bf16[4,18,704]{2,1,0:T(8,128)(2,1)}), bf16[4,18,704]{2,1,0:T(8,128)(2,1)S(1)}, u32[]{:S(2)}, u32[]{:S(2)}) %all-to-all-start.3) | async-done | bytes 101408 | tf_op jit(solution)/shard_map/all_to_all | solution.py:23
  205.9 12.4 %all-reduce.5 = (f32[2,256]{1,0:T(2,128)S(1)}, f32[2,704]{1,0:T(2,128)S(1)}) all-reduce(f32[2,256]{1,0:T(2,128)S(1)} %pad_maximum_fusion.7, f32[2,704]{1,0:T(2,128)S(1)} %slice.189), channel_id=1, replica_groups=mesh['g'=4,'y'=4,'x'=4,'c'=2,'m'=4] {'m'}, use_global_device_ids=true, to_apply=%region_17.18 | all-reduce | flops 1920 | bytes 15360 | tf_op jit(solution)/shard_map/psum | solution.py:229
  218.3 0.5 slice.182
  219.5 0.6 slice_reduce_fusion.3
  220.1 0.6 slice_reduce_fusion.4
  220.8 0.6 slice.184
  221.4 0.6 slice.187
  222.0 0.7 fusion.64
  222.6 0.8 copy_bitcast_fusion
  (79 shorter events, 0.9 us)
Async XLA Ops:
  0.6 19.3 %copy-start = (bf16[2,128,320]{1,2,0:T(8,128)(2,1)S(1)}, bf16[2,128,320]{1,2,0:T(8,128)(2,1)}, u32[]{:S(2)}) copy-start(bf16[2,128,320]{1,2,0:T(8,128)(2,1)} %param.22) | copy-start | bytes 491524
  3.0 10.7 %copy-start.12 = (f32[320]{0:T(512)S(1)}, f32[320]{0:T(512)}, u32[]{:S(2)}) copy-start(f32[320]{0:T(512)} %param.23) | copy-start | bytes 3844
  3.0 10.9 %copy-start.7 = (bf16[64,4,384]{2,1,0:T(4,128)(2,1)S(1)}, bf16[64,4,384]{2,1,0:T(4,128)(2,1)}, u32[]{:S(2)}) copy-start(bf16[64,4,384]{2,1,0:T(4,128)(2,1)} %param.14) | copy-start | bytes 589828
  3.0 11.6 %copy-start.9 = (bf16[64,4,384]{2,1,0:T(4,128)(2,1)S(1)}, bf16[64,4,384]{2,1,0:T(4,128)(2,1)}, u32[]{:S(2)}) copy-start(bf16[64,4,384]{2,1,0:T(4,128)(2,1)} %param.15) | copy-start | bytes 589828
  3.0 11.8 %copy-start.8 = (bf16[64,4,320]{2,1,0:T(4,128)(2,1)S(1)}, bf16[64,4,320]{2,1,0:T(4,128)(2,1)}, u32[]{:S(2)}) copy-start(bf16[64,4,320]{2,1,0:T(4,128)(2,1)} %param.17) | copy-start | bytes 491524
  3.0 78.5 %all-to-all-start = ((bf16[32,88,384]{2,1,0:T(8,128)(2,1)}), bf16[32,88,384]{2,1,0:T(8,128)(2,1)S(1)}, u32[]{:S(2)}, u32[]{:S(2)}) async-start(bf16[32,88,384]{2,1,0:T(8,128)(2,1)} %tile.2), calls=%async_computation | async-start | bytes 4325376 | tf_op jit(solution)/shard_map/all_to_all | solution.py:23
  13.8 1.3 copy-start.10
  13.8 2.3 %copy-start.17 = (s32[1,64]{1,0:T(1,128)S(1)}, s32[1,64]{1,0:T(1,128)}, u32[]{:S(2)}) copy-start(s32[1,64]{1,0:T(1,128)} %param.20) | copy-start | bytes 772
  14.8 3.7 %copy-start.15 = (s32[2]{0:T(128)S(1)}, s32[2]{0:T(128)}, u32[]{:S(2)}) copy-start(s32[2]{0:T(128)} %param.21) | copy-start | bytes 28
  14.9 5.0 %copy-start.13 = (f32[320]{0:T(512)S(1)}, f32[320]{0:T(512)}, u32[]{:S(2)}) copy-start(f32[320]{0:T(512)} %param.27) | copy-start | bytes 3844
  14.9 5.0 %copy-start.14 = (f32[384]{0:T(512)S(1)}, f32[384]{0:T(512)}, u32[]{:S(2)}) copy-start(f32[384]{0:T(512)} %param.25) | copy-start | bytes 4612
  81.7 1.1 copy-start.5
  81.7 1.2 copy-start.6
  82.9 19.9 %copy-start.2 = (bf16[328,256]{1,0:T(8,128)(2,1)S(1)}, bf16[328,256]{1,0:T(8,128)(2,1)}, u32[]{:S(2)}) copy-start(bf16[328,256]{1,0:T(8,128)(2,1)} %fusion.27) | copy-start | bytes 503812
  84.6 39.6 %all-to-all-start.1 = ((bf16[32,8,704]{2,1,0:T(8,128)(2,1)}), bf16[32,8,704]{2,1,0:T(8,128)(2,1)S(1)}, u32[]{:S(2)}, u32[]{:S(2)}) async-start(bf16[32,8,704]{2,1,0:T(8,128)(2,1)} %bitcast.6), calls=%async_computation.1 | async-start | bytes 786432 | tf_op jit(solution)/shard_map/all_to_all | solution.py:23
  124.2 1.2 copy-start.1
  125.4 2.2 copy-start.3
  140.5 1.2 copy-start.16
  141.7 1.1 copy-start.4
  146.6 47.2 %all-to-all-start.2 = ((bf16[32,48,704]{2,1,0:T(8,128)(2,1)}), bf16[32,48,704]{2,1,0:T(8,128)(2,1)S(1)}, u32[]{:S(2)}, u32[]{:S(2)}) async-start(bf16[32,48,704]{2,1,0:T(8,128)(2,1)} %bitcast.23), calls=%async_computation.2 | async-start | bytes 4718592 | tf_op jit(solution)/shard_map/all_to_all | solution.py:23
  157.4 16.5 %collective-permute-start = (bf16[320,256]{1,0:T(8,128)(2,1)}, bf16[320,256]{1,0:T(8,128)(2,1)}, u32[]{:S(2)}, u32[]{:S(2)}) collective-permute-start(bf16[320,256]{1,0:T(8,128)(2,1)} %get-tuple-element.58), channel_id=1, source_target_pairs={{0,2},{1,3},{2,0},{3,1},{4,6},{5,7},{6,4},{7,5},{8,10},{9,11},{10,... | collective-permute-start | bytes 491528 | tf_op jit(solution)/shard_map/ppermute | solution.py:19
  164.4 27.6 %collective-permute-start.1 = (bf16[320,256]{1,0:T(8,128)(2,1)}, bf16[320,256]{1,0:T(8,128)(2,1)S(1)}, u32[]{:S(2)}, u32[]{:S(2)}) collective-permute-start(bf16[320,256]{1,0:T(8,128)(2,1)} %get-tuple-element.60), channel_id=1, source_target_pairs={{0,1},{1,2},{2,3},{3,0},{4,5},{5,6},{6,7},{7,4},{8,9},{9,10},{10,1... | collective-permute-start | bytes 491528 | tf_op jit(solution)/shard_map/ppermute | solution.py:19
  171.5 21.2 %collective-permute-start.2 = (bf16[320,256]{1,0:T(8,128)(2,1)S(1)}, bf16[320,256]{1,0:T(8,128)(2,1)}, u32[]{:S(2)}, u32[]{:S(2)}) collective-permute-start(bf16[320,256]{1,0:T(8,128)(2,1)S(1)} %get-tuple-element.59), channel_id=1, source_target_pairs={{0,3},{1,0},{2,1},{3,2},{4,7},{5,4},{6,5},{7,6},{8,11},{9,8},{10,9... | collective-permute-start | bytes 491528 | tf_op jit(solution)/shard_map/ppermute | solution.py:19
  192.0 0.7 copy-start.11
  195.0 10.8 %all-to-all-start.3 = ((bf16[4,18,704]{2,1,0:T(8,128)(2,1)}), bf16[4,18,704]{2,1,0:T(8,128)(2,1)S(1)}, u32[]{:S(2)}, u32[]{:S(2)}) async-start(bf16[4,18,704]{2,1,0:T(8,128)(2,1)} %pad_maximum_fusion.4), calls=%async_computation.3 | async-start | bytes 294912 | tf_op jit(solution)/shard_map/all_to_all | solution.py:23
